TPU v7x, 512 devices: a whole 4x4x16 slice. The times are simulated.
512 devices in a mesh: point: 8 (over z_hi, core), space: 64 (over z_lo, x, y).
Axes of the slice: x: 4, y: 4, z: 16 (z_hi: 4, z_lo: 4; z = z_hi * 4 + z_lo), core: 2. Of those that a mesh axis runs over, the one named last changes fastest.
Arguments:
- adjoint: float32 [8, 4, 128, 256, 128], P('point', None, 'space'), may hold values from -6 to 6
- fwd_velocity: bfloat16 [8, 3, 128, 256, 128], P('point', None, 'space'), may hold values from -6 to 6
- reynolds: float32 [8], P('point'), may hold values from 100 to 2000
- weights: int32 [8], replicated, may hold values from 1 to 64
- porosity: float32 [128, 256, 128], P('space'), may hold values from 0.05 to 1
- flags: int32 [128, 256, 128], P('space'), may hold values from 0 to 2, as said below
Outputs:
- adjoint_out: float32 [8, 4, 128, 256, 128], P('point', None, 'space')
- porosity_new: float32 [128, 256, 128], P('space')
Inputs may be any that keep to these rules, and one draw needn't show every extreme that they name: `flags`: 1 marks a box of 128 x 64 cells (128 along the second dimension, 64 along the third, at a position that varies by draw) on the first plane, 2 such a box on the last plane, 0 elsewhere.
All inputs are finite; a program needn't handle non-finite values. Where the computation divides by a largest or mean magnitude, that divisor is 1e-20 or more.
Results may differ from a plain program's by a relative error of at most 0.0003.
Values sent between devices are 32-bit elements; how exact they have to be, the bound alone decides.
No kernel may reach another device: no remote copies, remote signals or barrier semaphores. Data moves between devices by JAX's collectives and lax.ppermute only.
A program may use at most 64 MiB of HBM per device.

v0:
```python
import jax
import jax.numpy as jnp
from jax import lax
from jax.sharding import PartitionSpec as P

SWEEPS = 2


AMAX = 50.0
QRAMP = 0.1
BETA = 0.5
STEP = 0.2
EPS = 1e-06


def with_halo(x, sides, width):
    for axis, dim in sides:
        size, length = (lax.axis_size(axis), x.shape[dim])
        up = [(i, (i + 1) % size) for i in range(size - 1)]
        down = [(j, i) for i, j in up]
        last = lax.slice_in_dim(x, length - width, length, axis=dim)
        first = lax.slice_in_dim(x, 0, width, axis=dim)
        before = lax.ppermute(last, axis, up)
        after = lax.ppermute(first, axis, down)
        x = jnp.concatenate([before, x, after], axis=dim)
    return x


def view(padded, dx, dy, dz):
    xs = padded.shape[-3] - 2
    ys = padded.shape[-2] - 2
    zs = padded.shape[-1] - 2
    return padded[..., 1 + dx : 1 + dx + xs, 1 + dy : 1 + dy + ys, 1 + dz : 1 + dz + zs]


def sweep(state, velocity, alpha, open_cells, outlet, viscosity, padded):
    offsets = [(1, 0, 0), (0, 1, 0), (0, 0, 1)]
    plus = [view(padded, a, b, c) for a, b, c in offsets]
    minus = [view(padded, -a, -b, -c) for a, b, c in offsets]
    lam = state[:3]
    neighbours = (
        plus[0][:3] + minus[0][:3] + plus[1][:3] + minus[1][:3] + plus[2][:3] + minus[2][:3]
    )
    advect = 0.5 * (
        velocity[0] * (plus[0][:3] - minus[0][:3])
        + velocity[1] * (plus[1][:3] - minus[1][:3])
        + velocity[2] * (plus[2][:3] - minus[2][:3])
    )
    gradient = jnp.stack([0.5 * (plus[d][3] - minus[d][3]) for d in range(3)])
    diverge = 0.5 * (
        plus[0][0] - minus[0][0] + (plus[1][1] - minus[1][1]) + (plus[2][2] - minus[2][2])
    )
    source = velocity * (outlet - alpha)
    lam_new = (
        open_cells
        * (lam + viscosity * neighbours + advect - gradient + source)
        / (1.0 + 6.0 * viscosity + alpha)
    )
    mu_new = state[3] - BETA * diverge
    return jnp.concatenate([lam_new, mu_new[None]], axis=0)


def filter_sum(padded):
    total = jnp.zeros(view(padded, 0, 0, 0).shape, jnp.float32)
    for dx in (-1, 0, 1):
        for dy in (-1, 0, 1):
            for dz in (-1, 0, 1):
                weight = (2.0 - abs(dx)) * (2.0 - abs(dy)) * (2.0 - abs(dz))
                total = total + weight * view(padded, dx, dy, dz)
    return total


def counts(length, offset, whole):
    where_at = offset + jnp.arange(length, dtype=jnp.int32)
    return 4.0 - (where_at == 0).astype(jnp.float32) - (where_at == whole - 1).astype(jnp.float32)


def denominator(shape, x_start, x_whole, y_start, y_whole):
    along_x = counts(shape[0], x_start, x_whole)
    along_y = counts(shape[1], y_start, y_whole)
    along_z = counts(shape[2], jnp.int32(0), shape[2])
    return along_x[:, None, None] * along_y[None, :, None] * along_z[None, None, :]


def pad_sides(field):
    return jnp.pad(field, ((0, 0), (0, 0), (0, 0), (1, 1), (1, 1)))


def shards(adjoint, fwd_velocity, reynolds, weights, porosity, flags):
    planes, rows, depth = porosity.shape
    per_device = adjoint.shape[0]
    x_whole = planes * lax.axis_size("space")
    x_start = lax.axis_index("space") * planes
    alpha = AMAX * QRAMP * (1.0 - porosity) / (QRAMP + porosity)
    dalpha = -AMAX * QRAMP * (1.0 + QRAMP) / (QRAMP + porosity) ** 2
    open_cells = (flags != 1).astype(jnp.float32)
    outlet = (flags == 2).astype(jnp.float32)
    viscosity = 20.0 / reynolds
    velocity = fwd_velocity.astype(jnp.float32)
    stepper = jax.vmap(sweep, in_axes=(0, 0, None, None, None, 0, 0))
    state = adjoint
    for step in range(SWEEPS):
        padded = with_halo(state, (("space", 2),), 1)
        state = stepper(state, velocity, alpha, open_cells, outlet, viscosity, pad_sides(padded))
    share = weights.astype(jnp.float32) / jnp.sum(weights.astype(jnp.float32))
    own_share = lax.dynamic_slice_in_dim(share, lax.axis_index("point") * per_device, per_device)
    partial_value = dalpha * jnp.sum(
        own_share[:, None, None, None] * jnp.sum(velocity * state[:, :3], axis=1), axis=0
    )
    part_rows = rows // lax.axis_size("point")
    y_start = lax.axis_index("point") * part_rows
    piece = lax.psum_scatter(partial_value, "point", scatter_dimension=1, tiled=True)
    rimmed = with_halo(piece, (("point", 1), ("space", 0)), 1)
    rimmed = jnp.pad(rimmed, ((0, 0), (0, 0), (1, 1)))
    filtered = filter_sum(rimmed) / denominator(piece.shape, x_start, x_whole, y_start, rows)
    gmax = lax.pmax(jnp.max(jnp.abs(filtered)), ("point", "space"))
    own_rows = lax.dynamic_slice_in_dim(porosity, y_start, part_rows, 1)
    updated = jnp.clip(own_rows - STEP * filtered / (gmax + EPS), 0.0, 1.0)
    porosity_new = lax.all_gather(updated, "point", axis=1, tiled=True)
    return (state, porosity_new)


def solution(mesh):
    return jax.shard_map(
        shards,
        mesh=mesh,
        in_specs=(
            P("point", None, "space", None, None),
            P("point", None, "space", None, None),
            P("point"),
            P(),
            P("space", None, None),
            P("space", None, None),
        ),
        out_specs=(P("point", None, "space", None, None), P("space", None, None)),
        check_vma=False,
    )
```

profile of v0, /device:TPU:1, one launch (start us, length us, event | category | flops | bytes accessed | tf_op | source)
XLA Modules:
  0.0 279.8 jit_solution(10787245673523211123)
XLA Ops:
  7.2 1.2 slice.397
  8.4 1.3 collective-permute-start
  9.7 1.1 slice.324
  10.8 4.7 %collective-permute-start.1 = (f32[1,4,1,256,128]{4,3,2,1,0:T(8,128)S(1)}, f32[1,4,1,256,128]{4,3,2,1,0:T(8,128)S(1)}, u32[]{:S(2)}, u32[]{:S(2)}) collective-permute-start(f32[1,4,1,256,128]{4,3,2,1,0:T(8,128)S(1)} %slice.324), channel_id=1, source_target_pairs={{0,1},{1,2},{2,3},{3,4},{4,5},{5,6},{6,7},{7,8},{8,9},{9,10},{10,1... | collective-permute-start | bytes 1572872 | tf_op jit(solution)/shard_map/ppermute | solution.py:23
  15.5 1.1 convert_element_type.61
  17.6 4.0 %collective-permute-done.1 = f32[1,4,1,256,128]{4,3,2,1,0:T(8,128)S(1)} collective-permute-done((f32[1,4,1,256,128]{4,3,2,1,0:T(8,128)S(1)}, f32[1,4,1,256,128]{4,3,2,1,0:T(8,128)S(1)}, u32[]{:S(2)}, u32[]{:S(2)}) %collective-permute-start.1) | collective-permute-done | bytes 524320 | tf_op jit(solution)/shard_map/ppermute | solution.py:23
  21.7 1.9 fusion.68
  26.5 1.3 collective-permute-start.2
  27.8 6.1 %collective-permute-start.3 = (f32[1,4,1,256,128]{4,3,2,0,1:T(8,128)S(1)}, f32[1,4,1,256,128]{4,3,2,0,1:T(8,128)S(1)}, u32[]{:S(2)}, u32[]{:S(2)}) collective-permute-start(f32[1,4,1,256,128]{4,3,2,0,1:T(8,128)S(1)} %get-tuple-element.16), channel_id=1, source_target_pairs={{0,1},{1,2},{2,3},{3,4},{4,5},{5,6},{6,7},{7,8},{8,9},{9,10},{10,1... | collective-permute-start | bytes 1572872 | tf_op jit(solution)/shard_map/ppermute | solution.py:23
  35.8 2.8 %collective-permute-done.2 = f32[1,4,1,256,128]{4,3,2,0,1:T(8,128)S(1)} collective-permute-done((f32[1,4,1,256,128]{4,3,2,0,1:T(8,128)}, f32[1,4,1,256,128]{4,3,2,0,1:T(8,128)S(1)}, u32[]{:S(2)}, u32[]{:S(2)}) %collective-permute-start.2) | collective-permute-done | bytes 524320 | tf_op jit(solution)/shard_map/ppermute | solution.py:24
  38.6 1.3 collective-permute-done.3
  39.9 2.4 select_maximum_fusion
  43.0 1.3 copy-done.1
  44.5 1.1 multiply_reduce_fusion
  45.6 1.4 multiply_multiply_fusion
  47.2 72.3 %reduce-scatter.2.cloned.1.call-done = f32[2,32,128]{2,1,0:T(8,128)} async-done(((f32[2,256,128]{2,1,0:T(8,128)}), f32[2,32,128]{2,1,0:T(8,128)}) %reduce-scatter.2.cloned.1.call-update) | async-done | bytes 32784 | tf_op jit(solution)/shard_map/reduce_scatter | solution.py:112
  120.2 3.1 %collective-permute-start.5 = (f32[2,1,128]{2,1,0:T(1,128)S(1)}, f32[2,1,128]{2,1,0:T(1,128)S(1)}, u32[]{:S(2)}, u32[]{:S(2)}) collective-permute-start(f32[2,1,128]{2,1,0:T(1,128)S(1)} %get-tuple-element.28), channel_id=1, source_target_pairs={{64,0},{128,64},{192,128},{256,192},{320,256},{384,320},{448,384},... | collective-permute-start | bytes 3080 | tf_op jit(solution)/shard_map/ppermute | solution.py:24
  123.3 6.4 %collective-permute-start.4 = (f32[2,1,128]{2,1,0:T(1,128)S(1)}, f32[2,1,128]{2,1,0:T(1,128)S(1)}, u32[]{:S(2)}, u32[]{:S(2)}) collective-permute-start(f32[2,1,128]{2,1,0:T(1,128)S(1)} %get-tuple-element.27), channel_id=1, source_target_pairs={{0,64},{64,128},{128,192},{192,256},{256,320},{320,384},{384,448},... | collective-permute-start | bytes 3080 | tf_op jit(solution)/shard_map/ppermute | solution.py:23
  129.7 1.7 fusion.25
  132.2 1.3 collective-permute-start.7
  133.5 4.0 %collective-permute-start.6 = (f32[1,34,128]{2,1,0:T(8,128)S(1)}, f32[1,34,128]{2,1,0:T(8,128)S(1)}, u32[]{:S(2)}, u32[]{:S(2)}) collective-permute-start(f32[1,34,128]{2,1,0:T(8,128)S(1)} %get-tuple-element.23), channel_id=1, source_target_pairs={{0,1},{1,2},{2,3},{3,4},{4,5},{5,6},{6,7},{7,8},{8,9},{9,10},{10,1... | collective-permute-start | bytes 52232 | tf_op jit(solution)/shard_map/ppermute | solution.py:23
  137.5 1.0 pad_maximum_fusion.1
  139.5 111.3 %pmax.7 = f32[]{:T(128)} all-reduce(f32[]{:T(128)} %get-tuple-element.2), channel_id=1, replica_groups=mesh['point'=8,'space'=64] {'point','space'}, use_global_device_ids=true, to_apply=%region_4.5 | all-reduce | flops 1 | bytes 8 | tf_op jit(solution)/shard_map/pmax | solution.py:116
  252.2 20.0 %all_gather.3 = f32[2,256,128]{2,1,0:T(8,128)S(1)} all-gather(f32[2,32,128]{2,1,0:T(8,128)S(1)} %subtract_clamp_fusion), channel_id=1, replica_groups=mesh['point'=8,'space'=64] {'point'}, dimensions={1}, use_global_device_ids=true | all-gather | bytes 294912 | tf_op jit(solution)/shard_map/all_gather | solution.py:119
  (68 shorter events, 10.0 us)
Async XLA Ops:
  7.2 14.5 %copy-start = (f32[1,4,2,256,128]{4,3,2,1,0:T(8,128)S(1)}, f32[1,4,2,256,128]{4,3,2,1,0:T(8,128)}, u32[]{:S(2)}) copy-start(f32[1,4,2,256,128]{4,3,2,1,0:T(8,128)} %param.6) | copy-start | bytes 3145732
  7.2 9.5 %copy-start.15 = (s32[2,256,128]{2,1,0:T(8,128)S(1)}, s32[2,256,128]{2,1,0:T(8,128)}, u32[]{:S(2)}) copy-start(s32[2,256,128]{2,1,0:T(8,128)} %param.11) | copy-start | bytes 786436
  7.2 10.2 %copy-start.13 = (f32[2,256,128]{2,1,0:T(8,128)S(1)}, f32[2,256,128]{2,1,0:T(8,128)}, u32[]{:S(2)}) copy-start(f32[2,256,128]{2,1,0:T(8,128)} %param.10) | copy-start | bytes 786436
  7.2 112.2 %reduce-scatter.2.cloned.1.call-start = ((), (), s32[]{:S(2)}) async-start(), calls=%async_computation.1 | async-start | bytes 294912 | tf_op jit(solution)/shard_map/reduce_scatter | solution.py:112
  8.4 13.3 %collective-permute-start = (f32[1,4,1,256,128]{4,3,2,0,1:T(8,128)S(1)}, f32[1,4,1,256,128]{4,3,2,0,1:T(8,128)S(1)}, u32[]{:S(2)}, u32[]{:S(2)}) collective-permute-start(f32[1,4,1,256,128]{4,3,2,0,1:T(8,128)S(1)} %slice.397), channel_id=1, source_target_pairs={{1,0},{2,1},{3,2},{4,3},{5,4},{6,5},{7,6},{8,7},{9,8},{10,9},{11,1... | collective-permute-start | bytes 1572872 | tf_op jit(solution)/shard_map/ppermute | solution.py:24
  10.8 10.8 %collective-permute-start.1 = (f32[1,4,1,256,128]{4,3,2,1,0:T(8,128)S(1)}, f32[1,4,1,256,128]{4,3,2,1,0:T(8,128)S(1)}, u32[]{:S(2)}, u32[]{:S(2)}) collective-permute-start(f32[1,4,1,256,128]{4,3,2,1,0:T(8,128)S(1)} %slice.324), channel_id=1, source_target_pairs={{0,1},{1,2},{2,3},{3,4},{4,5},{5,6},{6,7},{7,8},{8,9},{9,10},{10,1... | collective-permute-start | bytes 1572872 | tf_op jit(solution)/shard_map/ppermute | solution.py:23
  16.6 7.6 %copy-start.3 = (f32[2,256,128]{2,1,0:T(8,128)}, f32[2,256,128]{2,1,0:T(8,128)S(1)}, u32[]{:S(2)}) copy-start(f32[2,256,128]{2,1,0:T(8,128)S(1)} %get-tuple-element.18) | copy-start | bytes 786436
  16.7 7.6 %copy-start.5 = (f32[2,256,128]{2,1,0:T(8,128)}, f32[2,256,128]{2,1,0:T(8,128)S(1)}, u32[]{:S(2)}) copy-start(f32[2,256,128]{2,1,0:T(8,128)S(1)} %get-tuple-element.19) | copy-start | bytes 786436
  16.7 7.6 %copy-start.7 = (f32[2,256,128]{2,1,0:T(8,128)}, f32[2,256,128]{2,1,0:T(8,128)S(1)}, u32[]{:S(2)}) copy-start(f32[2,256,128]{2,1,0:T(8,128)S(1)} %get-tuple-element.20) | copy-start | bytes 786436
  17.5 6.7 %copy-start.9 = (f32[2,256,128]{2,1,0:T(8,128)}, f32[2,256,128]{2,1,0:T(8,128)S(1)}, u32[]{:S(2)}) copy-start(f32[2,256,128]{2,1,0:T(8,128)S(1)} %get-tuple-element.21) | copy-start | bytes 786436
  17.5 6.7 %copy-start.11 = (f32[2,256,128]{2,1,0:T(8,128)}, f32[2,256,128]{2,1,0:T(8,128)S(1)}, u32[]{:S(2)}) copy-start(f32[2,256,128]{2,1,0:T(8,128)S(1)} %get-tuple-element.22) | copy-start | bytes 786436
  24.6 9.2 %copy-start.17 = (s32[8]{0:T(128)S(1)}, s32[8]{0:T(128)}, u32[]{:S(2)}) copy-start(s32[8]{0:T(128)} %param.9) | copy-start | bytes 100
  26.5 12.2 %collective-permute-start.2 = (f32[1,4,1,256,128]{4,3,2,0,1:T(8,128)}, f32[1,4,1,256,128]{4,3,2,0,1:T(8,128)S(1)}, u32[]{:S(2)}, u32[]{:S(2)}) collective-permute-start(f32[1,4,1,256,128]{4,3,2,0,1:T(8,128)} %get-tuple-element.17), channel_id=1, source_target_pairs={{1,0},{2,1},{3,2},{4,3},{5,4},{6,5},{7,6},{8,7},{9,8},{10,9},{11,1... | collective-permute-start | bytes 1572872 | tf_op jit(solution)/shard_map/ppermute | solution.py:24
  27.8 12.1 %collective-permute-start.3 = (f32[1,4,1,256,128]{4,3,2,0,1:T(8,128)S(1)}, f32[1,4,1,256,128]{4,3,2,0,1:T(8,128)S(1)}, u32[]{:S(2)}, u32[]{:S(2)}) collective-permute-start(f32[1,4,1,256,128]{4,3,2,0,1:T(8,128)S(1)} %get-tuple-element.16), channel_id=1, source_target_pairs={{0,1},{1,2},{2,3},{3,4},{4,5},{5,6},{6,7},{7,8},{8,9},{9,10},{10,1... | collective-permute-start | bytes 1572872 | tf_op jit(solution)/shard_map/ppermute | solution.py:23
  42.3 2.0 copy-start.1
  42.3 2.0 copy-start.4
  42.3 2.0 copy-start.6
  42.3 2.0 copy-start.8
  42.3 2.2 copy-start.12
  119.4 19.1 %copy-start.16 = (f32[2,32,128]{2,1,0:T(8,128)S(1)}, f32[2,32,128]{2,1,0:T(8,128)}, u32[]{:S(2)}) copy-start(f32[2,32,128]{2,1,0:T(8,128)} %reduce-scatter.2.cloned.1.call-done) | copy-start | bytes 98308
  120.2 11.2 %collective-permute-start.5 = (f32[2,1,128]{2,1,0:T(1,128)S(1)}, f32[2,1,128]{2,1,0:T(1,128)S(1)}, u32[]{:S(2)}, u32[]{:S(2)}) collective-permute-start(f32[2,1,128]{2,1,0:T(1,128)S(1)} %get-tuple-element.28), channel_id=1, source_target_pairs={{64,0},{128,64},{192,128},{256,192},{320,256},{384,320},{448,384},... | collective-permute-start | bytes 3080 | tf_op jit(solution)/shard_map/ppermute | solution.py:24
  123.3 8.1 %collective-permute-start.4 = (f32[2,1,128]{2,1,0:T(1,128)S(1)}, f32[2,1,128]{2,1,0:T(1,128)S(1)}, u32[]{:S(2)}, u32[]{:S(2)}) collective-permute-start(f32[2,1,128]{2,1,0:T(1,128)S(1)} %get-tuple-element.27), channel_id=1, source_target_pairs={{0,64},{64,128},{128,192},{192,256},{256,320},{320,384},{384,448},... | collective-permute-start | bytes 3080 | tf_op jit(solution)/shard_map/ppermute | solution.py:23
  132.2 6.3 %collective-permute-start.7 = (f32[1,34,128]{2,1,0:T(8,128)S(1)}, f32[1,34,128]{2,1,0:T(8,128)S(1)}, u32[]{:S(2)}, u32[]{:S(2)}) collective-permute-start(f32[1,34,128]{2,1,0:T(8,128)S(1)} %get-tuple-element.24), channel_id=1, source_target_pairs={{1,0},{2,1},{3,2},{4,3},{5,4},{6,5},{7,6},{8,7},{9,8},{10,9},{11,1... | collective-permute-start | bytes 52232 | tf_op jit(solution)/shard_map/ppermute | solution.py:24
  133.5 5.0 %collective-permute-start.6 = (f32[1,34,128]{2,1,0:T(8,128)S(1)}, f32[1,34,128]{2,1,0:T(8,128)S(1)}, u32[]{:S(2)}, u32[]{:S(2)}) collective-permute-start(f32[1,34,128]{2,1,0:T(8,128)S(1)} %get-tuple-element.23), channel_id=1, source_target_pairs={{0,1},{1,2},{2,3},{3,4},{4,5},{5,6},{6,7},{7,8},{8,9},{9,10},{10,1... | collective-permute-start | bytes 52232 | tf_op jit(solution)/shard_map/ppermute | solution.py:23
  (3 other events, 4.1 us)
Sparse Core Ops, SparseCore 0:
  47.2 72.2 reduce-scatter.1
where the time goes:
time: 281 us; the launch traced here: 280 us
  blocking collectives  131 us (47%)
  waiting for transfers between devices  80.4 us (29%)
  starting transfers between devices  28.1 us (10%)
  other arithmetic  17.6 us (6%)
  between operations  15.8 us (6%)
  local copies, waits for them, and re-layouts  6.5 us (2%)
    pmax x1, blocking collectives, shards(): gmax = lax.pmax(jnp.max(jnp.abs(filtered)), ('point', 'space'))  111 us
    reduce_scatter x1, waiting for transfers between devices, shards(): lax.psum_scatter(partial_value, 'point', scatter_dimension=1, tiled=True)  72.3 us
    ppermute x4, starting transfers between devices, with_halo(): before = lax.ppermute(last, axis, up)  21.1 us
    all_gather x1, blocking collectives, shards(): porosity_new = lax.all_gather(updated, 'point', axis=1, tiled=True)  20 us
    ppermute x4, starting transfers between devices, with_halo(): after = lax.ppermute(first, axis, down)  6.93 us
  transfers between devices with their start and end apart: 9, of which 4 were waited for; matrix products, arithmetic and copies ran while one was open for 3% of the time, Pallas kernels for 0%

commit v1 on v0

v1 whole, which is shorter than its diff:
```python
import functools

import jax
import jax.numpy as jnp
from jax import lax
from jax.experimental import pallas as pl
from jax.experimental.pallas import tpu as pltpu
from jax.sharding import Mesh
from jax.sharding import PartitionSpec as P

AMAX = 50.0
QRAMP = 0.1
BETA = 0.5
STEP = 0.2
EPS = 1e-06

POINT = ("zhi", "core")
SPACE = ("zlo", "x", "y")
CHUNK = 32
VM = pl.BlockSpec(memory_space=pltpu.VMEM)
SM = pl.BlockSpec(memory_space=pltpu.SMEM)
F32 = jnp.float32


def shape(*dims):
    return jax.ShapeDtypeStruct(dims, F32)


def call(body, ins, outs, scratch=(), flops=1_000_000, moved=4_000_000):
    return pl.pallas_call(
        body,
        in_specs=ins,
        out_specs=[VM] * len(outs),
        out_shape=list(outs),
        scratch_shapes=list(scratch),
        compiler_params=pltpu.CompilerParams(vmem_limit_bytes=32 * 1024 * 1024),
        cost_estimate=pl.CostEstimate(flops=flops, bytes_accessed=moved, transcendentals=0),
    )


def row_shift(read, r, size, rows):
    at = lax.broadcasted_iota(jnp.int32, (size, 128), 0)
    if r == 0:
        before = jnp.where(at == 0, 0.0, pltpu.roll(read(0, size), 1, 0))
    else:
        before = read(r - 1, size)
    if r + size == rows:
        after = jnp.where(at == size - 1, 0.0, pltpu.roll(read(r, size), size - 1, 0))
    else:
        after = read(r + 1, size)
    return before, after


def lane_shift(value):
    at = lax.broadcasted_iota(jnp.int32, value.shape, 1)
    last = value.shape[1] - 1
    before = jnp.where(at == 0, 0.0, pltpu.roll(value, 1, 1))
    after = jnp.where(at == last, 0.0, pltpu.roll(value, last, 1))
    return before, after


def local_chunk(read, p, r, size, rows, vel, nu, scale, drive):
    u = [vel[0, d, p, r : r + size].astype(F32) for d in range(3)]
    ux, uy, uz = [0.5 * v for v in u]
    inner = nu + ux if p == 0 else nu - ux
    outer = nu - ux if p == 0 else nu + ux
    y_after, y_before = nu + uy, nu - uy
    z_after, z_before = nu + uz, nu - uz
    sign = 1.0 if p == 0 else -1.0
    mu = read(3, p, r, size)
    mu_in = read(3, 1 - p, r, size)
    mu_ym, mu_yp = row_shift(lambda a, n: read(3, p, a, n), r, size, rows)
    mu_zm, mu_zp = lane_shift(mu)
    gradient = [(0.5 * sign) * mu_in, 0.5 * (mu_yp - mu_ym), 0.5 * (mu_zp - mu_zm)]
    parts = []
    diverge = None
    for c in range(3):
        lam = read(c, p, r, size)
        lam_in = read(c, 1 - p, r, size)
        ym, yp = row_shift(lambda a, n: read(c, p, a, n), r, size, rows)
        zm, zp = lane_shift(lam)
        total = lam + inner * lam_in + y_after * yp + y_before * ym + z_after * zp + z_before * zm
        total = total - gradient[c] + u[c] * drive
        parts.append(scale * total)
        term = (sign * lam_in, yp - ym, zp - zm)[c]
        diverge = term if diverge is None else diverge + term
    parts.append(mu - (0.5 * BETA) * diverge)
    return parts, scale * outer, u


def viscosity_of(reynolds):
    return 20.0 / jnp.full((1, 128), reynolds[0], F32)


def first_local(reynolds, adjoint, vel, porosity, flags, part, factor, scaled):
    rows = adjoint.shape[3]
    nu = viscosity_of(reynolds)
    read = lambda c, p, r, n: adjoint[0, c, p, r : r + n]
    for p in range(2):
        for r in range(0, rows, CHUNK):
            now = slice(r, r + CHUNK)
            por = porosity[p, now]
            flag = flags[p, now]
            alpha = (AMAX * QRAMP) * (1.0 - por) / (QRAMP + por)
            scale = jnp.where(flag != 1, 1.0, 0.0) / (1.0 + 6.0 * nu + alpha)
            drive = jnp.where(flag == 2, 1.0, 0.0) - alpha
            parts, outer, _ = local_chunk(read, p, r, CHUNK, rows, vel, nu, scale, drive)
            for c in range(4):
                part[c, p, now] = parts[c]
            factor[p, now] = outer
            scaled[p, now] = scale


def join(part, factor, scaled, halo, p, now):
    sign = 1.0 if p == 0 else -1.0
    held = [halo[c, now] for c in range(4)]
    outer = factor[p, now]
    lam = [part[c, p, now] + outer * held[c] for c in range(3)]
    lam[0] = lam[0] + (0.5 * sign) * (scaled[p, now] * held[3])
    mu = part[3, p, now] + (0.5 * BETA * sign) * held[0]
    return lam, mu


def first_join(part, factor, scaled, before, after, plane0, plane1):
    rows = before.shape[1]
    for p, halo, out in ((0, before, plane0), (1, after, plane1)):
        for r in range(0, rows, CHUNK):
            now = slice(r, r + CHUNK)
            lam, mu = join(part, factor, scaled, halo, p, now)
            for c in range(3):
                out[c, now] = lam[c]
            out[3, now] = mu


def second_local(reynolds, weights, where, plane0, plane1, vel, porosity, flags, scaled, part, pull):
    rows = plane0.shape[1]
    nu = viscosity_of(reynolds)
    whole = weights[0]
    for i in range(1, weights.shape[0]):
        whole = whole + weights[i]
    share = jnp.full((1, 128), weights[where[0]].astype(F32), F32) / jnp.full(
        (1, 128), whole.astype(F32), F32
    )
    planes = (plane0, plane1)
    read = lambda c, p, r, n: planes[p][c, r : r + n]
    for p in range(2):
        for r in range(0, rows, CHUNK):
            now = slice(r, r + CHUNK)
            por = porosity[p, now]
            inverse = 1.0 / (QRAMP + por)
            alpha = (AMAX * QRAMP) * (1.0 - por) * inverse
            drive = jnp.where(flags[p, now] == 2, 1.0, 0.0) - alpha
            parts, _, u = local_chunk(read, p, r, CHUNK, rows, vel, nu, scaled[p, now], drive)
            slope = (-AMAX * QRAMP * (1.0 + QRAMP)) * (inverse * inverse) * share
            for c in range(4):
                part[c, p, now] = parts[c]
            for c in range(3):
                pull[c, p, now] = slope * u[c]


def counts(at, whole):
    return 4.0 - jnp.where(at == 0, 1.0, 0.0) - jnp.where(at == whole - 1, 1.0, 0.0)


def second_join(where, part, factor, scaled, pull, before, after, state, mine, theirs, sens):
    rows = before.shape[1]
    for p, halo in ((0, before), (1, after)):
        for r in range(0, rows, CHUNK):
            now = slice(r, r + CHUNK)
            lam, mu = join(part, factor, scaled, halo, p, now)
            for c in range(3):
                state[0, c, p, now] = lam[c]
            state[0, 3, p, now] = mu
            sens[p, now] = pull[0, p, now] * lam[0] + pull[1, p, now] * lam[1] + pull[2, p, now] * lam[2]
    half = rows // 2
    core = where[1]
    lane = lax.broadcasted_iota(jnp.int32, (CHUNK, 128), 1)
    row = lax.broadcasted_iota(jnp.int32, (CHUNK, 128), 0)
    for p in range(2):
        for r in range(0, rows, CHUNK):
            read = lambda a, n: sens[p, a : a + n]
            ym, yp = row_shift(read, r, CHUNK, rows)
            along = ym + yp + 2.0 * read(r, CHUNK)
            zm, zp = lane_shift(along)
            total = (zm + zp + 2.0 * along) / (counts(row + r, rows) * counts(lane, 128))
            owner = r // half
            to = slice(r - owner * half, r - owner * half + CHUNK)

            @pl.when(core == owner)
            def _():
                mine[p, to] = total

            @pl.when(core != owner)
            def _():
                theirs[p, to] = total


def add_cores(mine, other, blocks):
    n, _, part, _ = blocks.shape
    for q in range(n):
        now = slice(q * part, (q + 1) * part)
        blocks[q] = mine[:, now] + other[:, now]


def add_points(blocks, low, high):
    total = blocks[0]
    for q in range(1, blocks.shape[0]):
        total = total + blocks[q]
    low[...] = total[0]
    high[...] = total[1]


def filter_rows(where, low, high, before, after, packed, spread):
    part = low.shape[0]
    x = where[2]
    whole = where[3]
    first = low[...]
    second = high[...]
    none = jnp.zeros((part, 128), jnp.int32)
    one = (before[...] + 2.0 * first + second) / counts(none + x, whole)
    two = (first + 2.0 * second + after[...]) / counts(none + (x + 1), whole)
    packed[0:part] = one
    packed[part : 2 * part] = two
    largest = jnp.max(jnp.maximum(jnp.abs(one), jnp.abs(two)))
    packed[2 * part :] = jnp.full((8, 128), largest, F32)
    spread[...] = jnp.full(spread.shape, largest, F32)


def with_largest(packed, found, out):
    rows = packed.shape[0] - 8
    largest = jnp.full((8, 128), jnp.max(found[...]), F32)
    for q in range(out.shape[0]):
        out[q, 0:rows] = packed[0:rows]
        out[q, rows:] = largest


def update(where, porosity, own, other, out):
    n = own.shape[0]
    part = (own.shape[1] - 8) // 2
    half = n * part
    largest = jnp.max(jnp.maximum(own[:, 2 * part :], other[:, 2 * part :]))
    factor = STEP / jnp.full((1, 128), largest + EPS, F32)
    core = where[1]
    for held, base in ((own, core * half), (other, half - core * half)):
        for p in range(2):
            for q in range(n):
                to = pl.ds(pl.multiple_of(base + q * part, part), part)
                moved = porosity[p, to] - factor * held[q, p * part : (p + 1) * part]
                out[p, to] = jnp.clip(moved, 0.0, 1.0)


def shards(adjoint, fwd_velocity, reynolds, weights, porosity, flags):
    planes, rows, depth = porosity.shape
    points = lax.axis_size("zhi")
    cores = lax.axis_size("core")
    spaces = lax.axis_size("zlo") * lax.axis_size("x") * lax.axis_size("y")
    part = rows // (points * cores)
    core = lax.axis_index("core")
    place = (lax.axis_index("zlo") * lax.axis_size("x") + lax.axis_index("x")) * lax.axis_size("y")
    place = place + lax.axis_index("y")
    where = jnp.stack(
        [
            lax.axis_index("zhi") * cores + core,
            core,
            place * planes,
            jnp.int32(planes * spaces),
        ]
    ).astype(jnp.int32)
    up = [(i, i + 1) for i in range(spaces - 1)]
    down = [(j, i) for i, j in up]

    def neighbours(low, high):
        return lax.ppermute(high, SPACE, up), lax.ppermute(low, SPACE, down)

    before, after = neighbours(adjoint[0, :, 0], adjoint[0, :, 1])
    half_state = shape(4, planes, rows, depth)
    field = shape(planes, rows, depth)
    plane = shape(4, rows, depth)
    part1, factor, scaled = call(first_local, [SM, VM, VM, VM, VM], [half_state, field, field])(
        reynolds, adjoint, fwd_velocity, porosity, flags
    )
    plane0, plane1 = call(first_join, [VM] * 5, [plane, plane])(
        part1, factor, scaled, before, after
    )
    before, after = neighbours(plane0, plane1)
    part2, pull = call(
        second_local,
        [SM, SM, SM] + [VM] * 6,
        [half_state, shape(3, planes, rows, depth)],
    )(reynolds, weights, where, plane0, plane1, fwd_velocity, porosity, flags, scaled)
    half = shape(planes, rows // cores, depth)
    state, mine, theirs = call(
        second_join,
        [SM] + [VM] * 6,
        [shape(1, 4, planes, rows, depth), half, half],
        scratch=[pltpu.VMEM((planes, rows, depth), F32)],
    )(where, part2, factor, scaled, pull, before, after)
    other = lax.ppermute(theirs, "core", [(0, 1), (1, 0)])
    (blocks,) = call(add_cores, [VM, VM], [shape(points, planes, part, depth)])(mine, other)
    blocks = lax.all_to_all(blocks, "zhi", 0, 0, tiled=True)
    low, high = call(add_points, [VM], [shape(part, depth)] * 2)(blocks)
    before, after = neighbours(low, high)
    packed, spread = call(
        filter_rows,
        [SM] + [VM] * 4,
        [shape(planes * part + 8, depth), shape(spaces, 1, depth)],
    )(where, low, high, before, after)
    found = lax.all_to_all(spread, SPACE, 0, 0, tiled=True)
    (copies,) = call(with_largest, [VM, VM], [shape(points, planes * part + 8, depth)])(
        packed, found
    )
    own = lax.all_to_all(copies, "zhi", 0, 0, tiled=True)
    other = lax.ppermute(own, "core", [(0, 1), (1, 0)])
    (porosity_new,) = call(update, [SM, VM, VM, VM], [field])(where, porosity, own, other)
    return state, porosity_new


def solution(mesh):
    fine = Mesh(mesh.devices.reshape(4, 2, 4, 4, 4), POINT + SPACE)
    return jax.shard_map(
        shards,
        mesh=fine,
        in_specs=(
            P(POINT, None, SPACE, None, None),
            P(POINT, None, SPACE, None, None),
            P(POINT),
            P(),
            P(SPACE, None, None),
            P(SPACE, None, None),
        ),
        out_specs=(P(POINT, None, SPACE, None, None), P(SPACE, None, None)),
        check_vma=False,
    )
```

time: 281 us -> 136 us (0.48)
  waiting for transfers between devices: 80.4 us -> 11.6 us
  blocking collectives: 131 us -> 76.4 us
  other arithmetic: 17.6 us -> 0.08 us
  between operations: 15.8 us -> 1.49 us
  starting transfers between devices: 28.1 us -> 36 us
  Pallas kernels: 0 us -> 7.6 us
  local copies, waits for them, and re-layouts: 6.5 us -> 2 us
    pmax x1 -> x0, blocking collectives: 111 us -> none  [shards(): gmax = lax.pmax(jnp.max(jnp.abs(filtered)), ('point', 'space'))]
    all_to_all x0 -> x3, blocking collectives: none -> 76.4 us  [the longest x1 32.2 us: shards(): found = lax.all_to_all(spread, SPACE, 0, 0, tiled=True)]
    reduce_scatter x1 -> x0, waiting for transfers between devices: 72.3 us -> none  [shards(): lax.psum_scatter(partial_value, 'point', scatter_dimension=1, tiled=True)]
    all_gather x1 -> x0, blocking collectives: 20 us -> none  [shards(): porosity_new = lax.all_gather(updated, 'point', axis=1, tiled=True)]
    ppermute x8, starting transfers between devices: 28.1 us -> 36 us  [the longest x6 20.6 us: neighbours(): return (lax.ppermute(high, SPACE, up), lax.ppermute(low, SPACE, down))]
    pallas_call x0 -> x9, Pallas kernels: none -> 7.6 us  [the longest x1 2.94 us: shards(): call(second_join, [SM] + [VM] * 6, [shape(1, 4, planes, rows, depth), hal...]
    concatenate x7 -> x0, other arithmetic: 5.53 us -> none  [the longest x5 3.62 us: with_halo(): x = jnp.concatenate([before, x, after], axis=dim)]
    ppermute x8, waiting for transfers between devices: 8.15 us -> 11.6 us  [the longest x6 9.63 us: neighbours(): return (lax.ppermute(high, SPACE, up), lax.ppermute(low, SPACE, down))]
  transfers between devices with their start and end apart: 9 -> 8, of which waited for: 4 -> 7; matrix products, arithmetic and copies ran while one was open for 3% -> 0% of each run, Pallas kernels for 0% -> 2%
where the time goes in v1:
time: 136 us; the launch traced here: 135 us
  blocking collectives  76.4 us (56%)
  starting transfers between devices  36 us (26%)
  waiting for transfers between devices  11.6 us (9%)
  Pallas kernels  7.6 us (6%)
  local copies, waits for them, and re-layouts  2 us (1%)
  between operations  1.49 us (1%)
    all_to_all x1, blocking collectives, shards(): found = lax.all_to_all(spread, SPACE, 0, 0, tiled=True)  32.2 us
    all_to_all x1, blocking collectives, shards(): blocks = lax.all_to_all(blocks, 'zhi', 0, 0, tiled=True)  28.4 us
    ppermute x6, starting transfers between devices, neighbours(): return (lax.ppermute(high, SPACE, up), lax.ppermute(low, SPACE, down))  20.6 us
    all_to_all x1, blocking collectives, shards(): own = lax.all_to_all(copies, 'zhi', 0, 0, tiled=True)  15.7 us
    ppermute x6, waiting for transfers between devices, neighbours(): return (lax.ppermute(high, SPACE, up), lax.ppermute(low, SPACE, down))  9.63 us
    ppermute x1, starting transfers between devices, shards(): other = lax.ppermute(own, 'core', [(0, 1), (1, 0)])  7.74 us
    ppermute x1, starting transfers between devices, shards(): other = lax.ppermute(theirs, 'core', [(0, 1), (1, 0)])  7.62 us
    pallas_call x1, Pallas kernels, shards(): call(second_join, [SM] + [VM] * 6, [shape(1, 4, planes, rows, depth), hal...  2.94 us
  transfers between devices with their start and end apart: 8, of which 7 were waited for; matrix products, arithmetic and copies ran while one was open for 0% of the time, Pallas kernels for 2%

profile of v1, /device:TPU:1, one launch (start us, length us, event | category | flops | bytes accessed | tf_op | source)
XLA Modules:
  0.0 135.1 jit_solution(3984263948501307775)
XLA Ops:
  0.7 1.4 %slice_bitcast_fusion = (f32[4,256,128]{2,1,0:T(8,128)S(1)}, f32[4,256,128]{2,1,0:T(8,128)S(1)}) fusion(f32[1,4,2,256,128]{4,3,2,1,0:T(8,128)} %adjoint.1), kind=kLoop, calls=%fused_computation | loop fusion | bytes 2097152 | tf_op jit(solution)/shard_map/squeeze | solution.py:275
  2.1 1.3 collective-permute-start.1
  3.4 4.7 %collective-permute-start = (f32[4,256,128]{2,1,0:T(8,128)S(1)}, f32[4,256,128]{2,1,0:T(8,128)S(1)}, u32[]{:S(2)}, u32[]{:S(2)}) collective-permute-start(f32[4,256,128]{2,1,0:T(8,128)S(1)} %get-tuple-element.31), channel_id=1, source_target_pairs={{0,1},{1,2},{2,3},{3,4},{4,5},{5,6},{6,7},{7,8},{8,9},{9,10},{10,1... | collective-permute-start | bytes 1572872 | tf_op jit(solution)/shard_map/ppermute | solution.py:273
  8.8 0.9 shard_map.77
  9.7 3.0 %collective-permute-done.1.after = f32[4,256,128]{2,1,0:T(8,128)S(1)} collective-permute-done((f32[4,256,128]{2,1,0:T(8,128)S(1)}, f32[4,256,128]{2,1,0:T(8,128)S(1)}, u32[]{:S(2)}, u32[]{:S(2)}) %collective-permute-start.1) | collective-permute-done | bytes 524320 | tf_op jit(solution)/shard_map/ppermute | solution.py:273
  12.7 1.5 %collective-permute-done.before = f32[4,256,128]{2,1,0:T(8,128)S(1)} collective-permute-done((f32[4,256,128]{2,1,0:T(8,128)S(1)}, f32[4,256,128]{2,1,0:T(8,128)S(1)}, u32[]{:S(2)}, u32[]{:S(2)}) %collective-permute-start) | collective-permute-done | bytes 524320 | tf_op jit(solution)/shard_map/ppermute | solution.py:273
  14.3 1.3 collective-permute-start.3
  15.6 7.3 %collective-permute-start.2 = (f32[4,256,128]{2,1,0:T(8,128)S(1)}, f32[4,256,128]{2,1,0:T(8,128)S(1)}, u32[]{:S(2)}, u32[]{:S(2)}) collective-permute-start(f32[4,256,128]{2,1,0:T(8,128)S(1)} %get-tuple-element.20.plane1), channel_id=1, source_target_pairs={{0,1},{1,2},{2,3},{3,4},{4,5},{5,6},{6,7},{7,8},{8,9},{9,10},{10,1... | collective-permute-start | bytes 1572872 | tf_op jit(solution)/shard_map/ppermute | solution.py:273
  23.6 1.4 %shard_map.79 = (f32[4,2,256,128]{3,2,1,0:T(8,128)S(1)}, f32[3,2,256,128]{3,2,1,0:T(8,128)S(1)}) custom-call(f32[1]{0:T(128)S(6)} %copy.12.reynolds, s32[8]{0:T(128)S(1)} %copy-done.4, s32[4]{0:T(128)S(1)} %pad_add_fusion.where, f32[4,256,128]{2,1,0:T(8,128)S(1)} %get-tuple-element.19.plane0, f32[4,256,128]{2,1,0:T(8,128)S(1)} %get-tuple-element.20.plane1, ...), custom_call_target="tpu_custom_call" | custom-call | flops 1000000 | bytes 4000000 | tf_op jit(solution)/shard_map/pallas_call | solution.py:286
  25.0 3.4 %collective-permute-done.3.after = f32[4,256,128]{2,1,0:T(8,128)S(1)} collective-permute-done((f32[4,256,128]{2,1,0:T(8,128)S(1)}, f32[4,256,128]{2,1,0:T(8,128)S(1)}, u32[]{:S(2)}, u32[]{:S(2)}) %collective-permute-start.3) | collective-permute-done | bytes 524320 | tf_op jit(solution)/shard_map/ppermute | solution.py:273
  28.4 0.9 collective-permute-done.2.before
  29.3 2.9 %shard_map.80 = (f32[1,4,2,256,128]{4,3,2,1,0:T(8,128)}, f32[2,128,128]{2,1,0:T(8,128)S(1)}, f32[2,128,128]{2,1,0:T(8,128)S(1)}) custom-call(s32[4]{0:T(128)S(1)} %pad_add_fusion.where, f32[4,2,256,128]{3,2,1,0:T(8,128)S(1)} %get-tuple-element.21.part, f32[2,256,128]{2,1,0:T(8,128)S(1)} %get-tuple-element.17.factor, ...), custom_call_target="tpu_custom_call" | custom-call | flops 1000000 | bytes 4000000 | tf_op jit(solution)/shard_map/pallas_call | solution.py:292
  32.2 7.6 %collective-permute-start.4 = (f32[2,128,128]{2,1,0:T(8,128)S(1)}, f32[2,128,128]{2,1,0:T(8,128)S(1)}, u32[]{:S(2)}, u32[]{:S(2)}) collective-permute-start(f32[2,128,128]{2,1,0:T(8,128)S(1)} %get-tuple-element.25), channel_id=1, source_target_pairs={{0,64},{64,0},{1,65},{65,1},{2,66},{66,2},{3,67},{67,3},{4,68},{68... | collective-permute-start | bytes 393224 | tf_op jit(solution)/shard_map/ppermute | solution.py:298
  39.8 1.0 collective-permute-done.4.other
  40.8 28.4 %all_to_all.15.blocks = f32[4,2,32,128]{3,2,1,0:T(8,128)S(1)} all-to-all(f32[4,2,32,128]{3,2,1,0:T(8,128)S(1)} %shard_map.81), channel_id=1, replica_groups=mesh['zhi'=4,'core'=2,'zlo'=4,'x'=4,'y'=4] {'zhi'}, dimensions={0} | all-to-all | bytes 262144 | tf_op jit(solution)/shard_map/all_to_all | solution.py:300
  69.2 1.3 collective-permute-start.6
  70.5 4.7 %collective-permute-start.5 = (f32[32,128]{1,0:T(8,128)S(1)}, f32[32,128]{1,0:T(8,128)S(1)}, u32[]{:S(2)}, u32[]{:S(2)}) collective-permute-start(f32[32,128]{1,0:T(8,128)S(1)} %get-tuple-element.27.high), channel_id=1, source_target_pairs={{0,1},{1,2},{2,3},{3,4},{4,5},{5,6},{6,7},{7,8},{8,9},{9,10},{10,1... | collective-permute-start | bytes 49160 | tf_op jit(solution)/shard_map/ppermute | solution.py:273
  75.3 0.8 collective-permute-done.5.before
  76.1 0.7 shard_map.83
  76.8 32.2 %all_to_all.16.found = f32[64,1,128]{2,1,0:T(1,128)S(1)} all-to-all(f32[64,1,128]{2,1,0:T(1,128)S(1)} %get-tuple-element.29), channel_id=1, replica_groups=mesh['zhi'=4,'core'=2,'zlo'=4,'x'=4,'y'=4] {'zlo','x','y'}, dimensions={0} | all-to-all | bytes 65536 | tf_op jit(solution)/shard_map/all_to_all | solution.py:308
  109.2 15.7 %all_to_all.17.own = f32[4,72,128]{2,1,0:T(8,128)S(1)} all-to-all(f32[4,72,128]{2,1,0:T(8,128)S(1)} %shard_map.84), channel_id=1, replica_groups=mesh['zhi'=4,'core'=2,'zlo'=4,'x'=4,'y'=4] {'zhi'}, dimensions={0} | all-to-all | bytes 294912 | tf_op jit(solution)/shard_map/all_to_all | solution.py:312
  124.9 7.7 %collective-permute-start.7 = (f32[4,72,128]{2,1,0:T(8,128)S(1)}, f32[4,72,128]{2,1,0:T(8,128)S(1)}, u32[]{:S(2)}, u32[]{:S(2)}) collective-permute-start(f32[4,72,128]{2,1,0:T(8,128)S(1)} %all_to_all.17.own), channel_id=1, source_target_pairs={{0,64},{64,0},{1,65},{65,1},{2,66},{66,2},{3,67},{67,3},{4,68},{68... | collective-permute-start | bytes 442376 | tf_op jit(solution)/shard_map/ppermute | solution.py:313
  132.7 1.0 collective-permute-done.7.other
  133.7 1.4 %shard_map.85 = f32[2,256,128]{2,1,0:T(8,128)} custom-call(s32[4]{0:T(128)S(1)} %pad_add_fusion.where, f32[2,256,128]{2,1,0:T(8,128)S(1)} %copy-done.1, f32[4,72,128]{2,1,0:T(8,128)S(1)} %all_to_all.17.own, f32[4,72,128]{2,1,0:T(8,128)S(1)} %collective-permute-done.7.other), custom_call_target="tpu_custom_call" | custom-call | flops 1000000 | bytes 4000000 | tf_op jit(solution)/shard_map/pallas_call | solution.py:314
  (16 shorter events, 1.0 us)
Async XLA Ops:
  0.6 8.1 %copy-start = (f32[1,4,2,256,128]{4,3,2,1,0:T(8,128)S(1)}, f32[1,4,2,256,128]{4,3,2,1,0:T(8,128)}, u32[]{:S(2)}) copy-start(f32[1,4,2,256,128]{4,3,2,1,0:T(8,128)} %adjoint.1) | copy-start | bytes 3145732
  0.6 8.1 %copy-start.1 = (f32[2,256,128]{2,1,0:T(8,128)S(1)}, f32[2,256,128]{2,1,0:T(8,128)}, u32[]{:S(2)}) copy-start(f32[2,256,128]{2,1,0:T(8,128)} %porosity.5) | copy-start | bytes 786436
  0.7 8.1 %copy-start.3 = (s32[2,256,128]{2,1,0:T(8,128)S(1)}, s32[2,256,128]{2,1,0:T(8,128)}, u32[]{:S(2)}) copy-start(s32[2,256,128]{2,1,0:T(8,128)} %flags.3) | copy-start | bytes 786436
  0.7 8.1 %copy-start.2 = (bf16[1,3,2,256,128]{4,3,2,1,0:T(8,128)(2,1)S(1)}, bf16[1,3,2,256,128]{4,3,2,1,0:T(8,128)(2,1)}, u32[]{:S(2)}) copy-start(bf16[1,3,2,256,128]{4,3,2,1,0:T(8,128)(2,1)} %vel.3) | copy-start | bytes 1179652
  2.1 10.6 %collective-permute-start.1 = (f32[4,256,128]{2,1,0:T(8,128)S(1)}, f32[4,256,128]{2,1,0:T(8,128)S(1)}, u32[]{:S(2)}, u32[]{:S(2)}) collective-permute-start(f32[4,256,128]{2,1,0:T(8,128)S(1)} %get-tuple-element.30), channel_id=1, source_target_pairs={{1,0},{2,1},{3,2},{4,3},{5,4},{6,5},{7,6},{8,7},{9,8},{10,9},{11,1... | collective-permute-start | bytes 1572872 | tf_op jit(solution)/shard_map/ppermute | solution.py:273
  3.4 10.8 %collective-permute-start = (f32[4,256,128]{2,1,0:T(8,128)S(1)}, f32[4,256,128]{2,1,0:T(8,128)S(1)}, u32[]{:S(2)}, u32[]{:S(2)}) collective-permute-start(f32[4,256,128]{2,1,0:T(8,128)S(1)} %get-tuple-element.31), channel_id=1, source_target_pairs={{0,1},{1,2},{2,3},{3,4},{4,5},{5,6},{6,7},{7,8},{8,9},{9,10},{10,1... | collective-permute-start | bytes 1572872 | tf_op jit(solution)/shard_map/ppermute | solution.py:273
  14.3 14.1 %collective-permute-start.3 = (f32[4,256,128]{2,1,0:T(8,128)S(1)}, f32[4,256,128]{2,1,0:T(8,128)S(1)}, u32[]{:S(2)}, u32[]{:S(2)}) collective-permute-start(f32[4,256,128]{2,1,0:T(8,128)S(1)} %get-tuple-element.19.plane0), channel_id=1, source_target_pairs={{1,0},{2,1},{3,2},{4,3},{5,4},{6,5},{7,6},{8,7},{9,8},{10,9},{11,1... | collective-permute-start | bytes 1572872 | tf_op jit(solution)/shard_map/ppermute | solution.py:273
  15.6 13.7 %collective-permute-start.2 = (f32[4,256,128]{2,1,0:T(8,128)S(1)}, f32[4,256,128]{2,1,0:T(8,128)S(1)}, u32[]{:S(2)}, u32[]{:S(2)}) collective-permute-start(f32[4,256,128]{2,1,0:T(8,128)S(1)} %get-tuple-element.20.plane1), channel_id=1, source_target_pairs={{0,1},{1,2},{2,3},{3,4},{4,5},{5,6},{6,7},{7,8},{8,9},{9,10},{10,1... | collective-permute-start | bytes 1572872 | tf_op jit(solution)/shard_map/ppermute | solution.py:273
  22.9 0.7 copy-start.4
  32.2 8.6 %collective-permute-start.4 = (f32[2,128,128]{2,1,0:T(8,128)S(1)}, f32[2,128,128]{2,1,0:T(8,128)S(1)}, u32[]{:S(2)}, u32[]{:S(2)}) collective-permute-start(f32[2,128,128]{2,1,0:T(8,128)S(1)} %get-tuple-element.25), channel_id=1, source_target_pairs={{0,64},{64,0},{1,65},{65,1},{2,66},{66,2},{3,67},{67,3},{4,68},{68... | collective-permute-start | bytes 393224 | tf_op jit(solution)/shard_map/ppermute | solution.py:298
  69.2 6.0 %collective-permute-start.6 = (f32[32,128]{1,0:T(8,128)S(1)}, f32[32,128]{1,0:T(8,128)S(1)}, u32[]{:S(2)}, u32[]{:S(2)}) collective-permute-start(f32[32,128]{1,0:T(8,128)S(1)} %get-tuple-element.26.low), channel_id=1, source_target_pairs={{1,0},{2,1},{3,2},{4,3},{5,4},{6,5},{7,6},{8,7},{9,8},{10,9},{11,1... | collective-permute-start | bytes 49160 | tf_op jit(solution)/shard_map/ppermute | solution.py:273
  70.5 5.6 %collective-permute-start.5 = (f32[32,128]{1,0:T(8,128)S(1)}, f32[32,128]{1,0:T(8,128)S(1)}, u32[]{:S(2)}, u32[]{:S(2)}) collective-permute-start(f32[32,128]{1,0:T(8,128)S(1)} %get-tuple-element.27.high), channel_id=1, source_target_pairs={{0,1},{1,2},{2,3},{3,4},{4,5},{5,6},{6,7},{7,8},{8,9},{9,10},{10,1... | collective-permute-start | bytes 49160 | tf_op jit(solution)/shard_map/ppermute | solution.py:273
  124.9 8.7 %collective-permute-start.7 = (f32[4,72,128]{2,1,0:T(8,128)S(1)}, f32[4,72,128]{2,1,0:T(8,128)S(1)}, u32[]{:S(2)}, u32[]{:S(2)}) collective-permute-start(f32[4,72,128]{2,1,0:T(8,128)S(1)} %all_to_all.17.own), channel_id=1, source_target_pairs={{0,64},{64,0},{1,65},{65,1},{2,66},{66,2},{3,67},{67,3},{4,68},{68... | collective-permute-start | bytes 442376 | tf_op jit(solution)/shard_map/ppermute | solution.py:313

commit v2 on v1

v2 whole, which is shorter than its diff:
```python
import functools

import jax
import jax.numpy as jnp
from jax import lax
from jax.experimental import pallas as pl
from jax.experimental.pallas import tpu as pltpu
from jax.sharding import Mesh
from jax.sharding import PartitionSpec as P

AMAX = 50.0
QRAMP = 0.1
BETA = 0.5
STEP = 0.2
EPS = 1e-06

POINT = ("zhi", "core")
SPACE = ("zlo", "x", "y")
CHUNK = 32
VM = pl.BlockSpec(memory_space=pltpu.VMEM)
SM = pl.BlockSpec(memory_space=pltpu.SMEM)
HB = pl.BlockSpec(memory_space=pltpu.HBM)
F32 = jnp.float32


def shape(*dims):
    return jax.ShapeDtypeStruct(dims, F32)


def call(body, ins, outs, specs=None, scratch=(), flops=1_000_000, moved=4_000_000):
    return pl.pallas_call(
        body,
        in_specs=ins,
        out_specs=[VM] * len(outs) if specs is None else specs,
        out_shape=list(outs),
        scratch_shapes=list(scratch),
        compiler_params=pltpu.CompilerParams(vmem_limit_bytes=32 * 1024 * 1024),
        cost_estimate=pl.CostEstimate(flops=flops, bytes_accessed=moved, transcendentals=0),
    )


def row_shift(read, r, size, rows):
    at = lax.broadcasted_iota(jnp.int32, (size, 128), 0)
    if r == 0:
        before = jnp.where(at == 0, 0.0, pltpu.roll(read(0, size), 1, 0))
    else:
        before = read(r - 1, size)
    if r + size == rows:
        after = jnp.where(at == size - 1, 0.0, pltpu.roll(read(r, size), size - 1, 0))
    else:
        after = read(r + 1, size)
    return before, after


def lane_shift(value):
    at = lax.broadcasted_iota(jnp.int32, value.shape, 1)
    last = value.shape[1] - 1
    before = jnp.where(at == 0, 0.0, pltpu.roll(value, 1, 1))
    after = jnp.where(at == last, 0.0, pltpu.roll(value, last, 1))
    return before, after


def side(where, p):
    odd = where[4]
    index = odd if p == 0 else 1 - odd
    return index, (1 - 2 * index).astype(F32)


def take_planes(where, adjoint, near, far, sems):
    copies = [
        pltpu.make_async_copy(adjoint.at[0, :, side(where, p)[0]], out, sems.at[p])
        for p, out in ((0, near), (1, far))
    ]
    for copy in copies:
        copy.start()
    for copy in copies:
        copy.wait()


def local_chunk(read, p, sign, r, size, rows, u, nu, scale, drive):
    ux, uy, uz = [0.5 * v for v in u]
    inner = nu + sign * ux
    outer = nu - sign * ux
    y_after, y_before = nu + uy, nu - uy
    z_after, z_before = nu + uz, nu - uz
    mu = read(3, p, r, size)
    mu_in = read(3, 1 - p, r, size)
    mu_ym, mu_yp = row_shift(lambda a, n: read(3, p, a, n), r, size, rows)
    mu_zm, mu_zp = lane_shift(mu)
    gradient = [(0.5 * sign) * mu_in, 0.5 * (mu_yp - mu_ym), 0.5 * (mu_zp - mu_zm)]
    parts = []
    diverge = None
    for c in range(3):
        lam = read(c, p, r, size)
        lam_in = read(c, 1 - p, r, size)
        ym, yp = row_shift(lambda a, n: read(c, p, a, n), r, size, rows)
        zm, zp = lane_shift(lam)
        total = lam + inner * lam_in + y_after * yp + y_before * ym + z_after * zp + z_before * zm
        total = total - gradient[c] + u[c] * drive
        parts.append(scale * total)
        term = (sign * lam_in, yp - ym, zp - zm)[c]
        diverge = term if diverge is None else diverge + term
    parts.append(mu - (0.5 * BETA) * diverge)
    return parts, scale * outer


def viscosity_of(reynolds):
    return 20.0 / jnp.full((1, 128), reynolds[0], F32)


def first_local(reynolds, where, near, far, vel, porosity, flags, part, factor, scaled):
    rows = near.shape[1]
    nu = viscosity_of(reynolds)
    planes = (near, far)
    read = lambda c, p, r, n: planes[p][c, r : r + n]
    for p in range(2):
        index, sign = side(where, p)
        for r in range(0, rows, CHUNK):
            now = slice(r, r + CHUNK)
            por = porosity[index, now]
            flag = flags[index, now]
            alpha = (AMAX * QRAMP) * (1.0 - por) / (QRAMP + por)
            scale = jnp.where(flag != 1, 1.0, 0.0) / (1.0 + 6.0 * nu + alpha)
            drive = jnp.where(flag == 2, 1.0, 0.0) - alpha
            u = [vel[0, d, index, now].astype(F32) for d in range(3)]
            parts, outer = local_chunk(read, p, sign, r, CHUNK, rows, u, nu, scale, drive)
            for c in range(4):
                part[c, p, now] = parts[c]
            factor[p, now] = outer
            scaled[p, now] = scale


def join(part, factor, scaled, halo, p, sign, now):
    held = [halo[c, now] for c in range(4)]
    outer = factor[p, now]
    lam = [part[c, p, now] + outer * held[c] for c in range(3)]
    lam[0] = lam[0] + (0.5 * sign) * (scaled[p, now] * held[3])
    mu = part[3, p, now] + (0.5 * BETA * sign) * held[0]
    return lam, mu


def first_join(p, where, part, factor, scaled, halo, out):
    _, sign = side(where, p)
    for r in range(0, halo.shape[1], CHUNK):
        now = slice(r, r + CHUNK)
        lam, mu = join(part, factor, scaled, halo, p, sign, now)
        for c in range(3):
            out[c, now] = lam[c]
        out[3, now] = mu


def second_local(reynolds, weights, where, near, far, vel, porosity, flags, scaled, part, pull):
    rows = near.shape[1]
    nu = viscosity_of(reynolds)
    whole = weights[0]
    for i in range(1, weights.shape[0]):
        whole = whole + weights[i]
    share = jnp.full((1, 128), weights[where[0]].astype(F32), F32) / jnp.full(
        (1, 128), whole.astype(F32), F32
    )
    planes = (near, far)
    read = lambda c, p, r, n: planes[p][c, r : r + n]
    for p in range(2):
        index, sign = side(where, p)
        for r in range(0, rows, CHUNK):
            now = slice(r, r + CHUNK)
            por = porosity[index, now]
            inverse = 1.0 / (QRAMP + por)
            alpha = (AMAX * QRAMP) * (1.0 - por) * inverse
            drive = jnp.where(flags[index, now] == 2, 1.0, 0.0) - alpha
            u = [vel[0, d, index, now].astype(F32) for d in range(3)]
            parts, _ = local_chunk(read, p, sign, r, CHUNK, rows, u, nu, scaled[p, now], drive)
            slope = (-AMAX * QRAMP * (1.0 + QRAMP)) * (inverse * inverse) * share
            for c in range(4):
                part[c, p, now] = parts[c]
            for c in range(3):
                pull[c, p, now] = slope * u[c]


def counts(at, whole):
    return 4.0 - jnp.where(at == 0, 1.0, 0.0) - jnp.where(at == whole - 1, 1.0, 0.0)


def second_join(where, part, factor, scaled, pull, near, far, state, mine, theirs, held, sens, sems):
    rows = near.shape[1]
    copies = []
    for p, halo in ((0, near), (1, far)):
        index, sign = side(where, p)
        for r in range(0, rows, CHUNK):
            now = slice(r, r + CHUNK)
            lam, mu = join(part, factor, scaled, halo, p, sign, now)
            for c in range(3):
                held[p, c, now] = lam[c]
            held[p, 3, now] = mu
            sens[p, now] = pull[0, p, now] * lam[0] + pull[1, p, now] * lam[1] + pull[2, p, now] * lam[2]
        copy = pltpu.make_async_copy(held.at[p], state.at[0, :, index], sems.at[p])
        copy.start()
        copies.append(copy)
    half = rows // 2
    core = where[1]
    lane = lax.broadcasted_iota(jnp.int32, (CHUNK, 128), 1)
    row = lax.broadcasted_iota(jnp.int32, (CHUNK, 128), 0)
    for p in range(2):
        index, _ = side(where, p)
        for r in range(0, rows, CHUNK):
            read = lambda a, n: sens[p, a : a + n]
            ym, yp = row_shift(read, r, CHUNK, rows)
            along = ym + yp + 2.0 * read(r, CHUNK)
            zm, zp = lane_shift(along)
            total = (zm + zp + 2.0 * along) / (counts(row + r, rows) * counts(lane, 128))
            owner = r // half
            to = slice(r - owner * half, r - owner * half + CHUNK)

            @pl.when(core == owner)
            def _():
                mine[index, to] = total

            @pl.when(core != owner)
            def _():
                theirs[index, to] = total

    for copy in copies:
        copy.wait()


def left_half(shape):
    return lax.broadcasted_iota(jnp.int32, shape, 1) < shape[1] // 2


def swap_halves(value):
    return pltpu.roll(value, value.shape[1] // 2, 1)


def interleave(one, two):
    left = left_half(one.shape)
    return jnp.where(left, one, swap_halves(two)), jnp.where(left, swap_halves(one), two)


def add_cores(mine, other, blocks):
    half = mine.shape[1]
    for r in range(0, half, CHUNK):
        now = slice(r, r + CHUNK)
        first, second = interleave(mine[0, now] + other[0, now], mine[1, now] + other[1, now])
        blocks[now] = first
        blocks[half + r : half + r + CHUNK] = second


def filter_planes(points, blocks, out):
    slabs = blocks.shape[0] // points
    total = blocks[0:slabs]
    for q in range(1, points):
        total = total + blocks[q * slabs : (q + 1) * slabs]
    swapped = swap_halves(total)
    at = lax.broadcasted_iota(jnp.int32, total.shape, 0)
    left = left_half(total.shape)
    below = jnp.where(at == 0, 0.0, pltpu.roll(swapped, 1, 0))
    above = jnp.where(at == slabs - 1, 0.0, pltpu.roll(swapped, slabs - 1, 0))
    plane = 2 * at + jnp.where(left, 0, 1)
    filtered = (2.0 * total + swapped + jnp.where(left, below, above)) / counts(plane, 2 * slabs)
    largest = jnp.full(total.shape, jnp.max(jnp.abs(filtered)), F32)
    for q in range(points):
        out[pl.ds(2 * q * slabs, slabs, stride=2)] = filtered
        out[pl.ds(2 * q * slabs + 1, slabs, stride=2)] = largest


def update(where, porosity, own, other, out):
    n = own.shape[0] // 2
    half = n // 2
    ends = [ref[pl.ds(1, n, stride=2)] for ref in (own, other)]
    largest = jnp.max(jnp.maximum(ends[0], ends[1]))
    factor = STEP / jnp.full((1, 128), largest + EPS, F32)
    core = where[1]
    for held, base in ((own, core * half), (other, half - core * half)):
        for r in range(0, half, CHUNK):
            to = pl.ds(pl.multiple_of(base + r, CHUNK), CHUNK)
            first = held[pl.ds(2 * r, CHUNK, stride=2)]
            second = held[pl.ds(2 * (half + r), CHUNK, stride=2)]
            for p, moved in enumerate(interleave(first, second)):
                out[p, to] = jnp.clip(porosity[p, to] - factor * moved, 0.0, 1.0)


def shards(adjoint, fwd_velocity, reynolds, weights, porosity, flags):
    planes, rows, depth = porosity.shape
    points = lax.axis_size("zhi")
    cores = lax.axis_size("core")
    spaces = lax.axis_size("zlo") * lax.axis_size("x") * lax.axis_size("y")
    core = lax.axis_index("core")
    place = (lax.axis_index("zlo") * lax.axis_size("x") + lax.axis_index("x")) * lax.axis_size("y")
    place = place + lax.axis_index("y")
    where = jnp.stack(
        [
            lax.axis_index("zhi") * cores + core,
            core,
            place * planes,
            jnp.int32(planes * spaces),
            place % 2,
        ]
    ).astype(jnp.int32)

    def pairs(start):
        there = [(i, i + 1) for i in range(start, spaces - 1, 2)]
        return there + [(j, i) for i, j in there]

    def swap(value, start):
        return lax.ppermute(value, SPACE, pairs(start))

    half_state = shape(4, planes, rows, depth)
    field = shape(planes, rows, depth)
    plane = shape(4, rows, depth)
    near, far = call(
        take_planes,
        [SM, HB],
        [plane, plane],
        scratch=[pltpu.SemaphoreType.DMA((2,))],
    )(where, adjoint)
    halo_near = swap(near, 1)
    halo_far = swap(far, 0)
    part, factor, scaled = call(first_local, [SM, SM] + [VM] * 5, [half_state, field, field])(
        reynolds, where, near, far, fwd_velocity, porosity, flags
    )
    ins = [SM] + [VM] * 4
    (near,) = call(functools.partial(first_join, 0), ins, [plane])(
        where, part, factor, scaled, halo_near
    )
    halo_near = swap(near, 1)
    (far,) = call(functools.partial(first_join, 1), ins, [plane])(
        where, part, factor, scaled, halo_far
    )
    halo_far = swap(far, 0)
    part, pull = call(
        second_local,
        [SM, SM, SM] + [VM] * 6,
        [half_state, shape(3, planes, rows, depth)],
    )(reynolds, weights, where, near, far, fwd_velocity, porosity, flags, scaled)
    half = shape(planes, rows // cores, depth)
    state, mine, theirs = call(
        second_join,
        [SM] + [VM] * 6,
        [shape(1, 4, planes, rows, depth), half, half],
        specs=[HB, VM, VM],
        scratch=[
            pltpu.VMEM((planes, 4, rows, depth), F32),
            pltpu.VMEM((planes, rows, depth), F32),
            pltpu.SemaphoreType.DMA((2,)),
        ],
    )(where, part, factor, scaled, pull, halo_near, halo_far)
    other = lax.ppermute(theirs, "core", [(0, 1), (1, 0)])
    group = points * spaces
    (blocks,) = call(add_cores, [VM, VM], [shape(group, depth)])(mine, other)
    blocks = lax.all_to_all(blocks.reshape(group, 1, depth), ("zhi",) + SPACE, 0, 0, tiled=True)
    (copies,) = call(functools.partial(filter_planes, points), [VM], [shape(2 * group, depth)])(
        blocks.reshape(group, depth)
    )
    own = lax.all_to_all(copies.reshape(group, 2, depth), ("zhi",) + SPACE, 0, 0, tiled=True)
    own = own.reshape(2 * group, depth)
    other = lax.ppermute(own, "core", [(0, 1), (1, 0)])
    (porosity_new,) = call(update, [SM, VM, VM, VM], [field])(where, porosity, own, other)
    return state, porosity_new


def solution(mesh):
    fine = Mesh(mesh.devices.reshape(4, 2, 4, 4, 4), POINT + SPACE)
    return jax.shard_map(
        shards,
        mesh=fine,
        in_specs=(
            P(POINT, None, SPACE, None, None),
            P(POINT, None, SPACE, None, None),
            P(POINT),
            P(),
            P(SPACE, None, None),
            P(SPACE, None, None),
        ),
        out_specs=(P(POINT, None, SPACE, None, None), P(SPACE, None, None)),
        check_vma=False,
    )
```

time: 136 us -> 127 us (0.934)
  starting transfers between devices: 36 us -> 24.4 us
  waiting for transfers between devices: 11.6 us -> 16.6 us
  blocking collectives: 76.4 us -> 73.7 us
    ppermute x6 -> x4, starting transfers between devices: 20.6 us -> 14 us  [swap(): return lax.ppermute(value, SPACE, pairs(start))]
    ppermute x6 -> x4, waiting for transfers between devices: 9.63 us -> 14.5 us  [swap(): return lax.ppermute(value, SPACE, pairs(start))]
    ppermute x1, starting transfers between devices: 7.62 us -> 4.38 us  [shards(): other = lax.ppermute(theirs, 'core', [(0, 1), (1, 0)])]
    all_to_all x3 -> x2, blocking collectives: 76.4 us -> 73.7 us  [the longest x1 44 us: shards(): lax.all_to_all(blocks.reshape(group, 1, depth), ('zhi',) + SPACE, 0, 0, t...]
    pallas_call x6, Pallas kernels: 1.87 us -> 3.74 us  [the longest x1 1.58 us: shards(): call(first_local, [SM, SM] + [VM] * 5, [half_state, field, field])]
    ppermute x1, starting transfers between devices: 7.74 us -> 5.98 us  [shards(): other = lax.ppermute(own, 'core', [(0, 1), (1, 0)])]
    squeeze x1 -> x0, local copies, waits for them, and re-layouts: 1.41 us -> none  [shards(): before, after = neighbours(adjoint[0, :, 0], adjoint[0, :, 1])]
  transfers between devices with their start and end apart: 8 -> 6, of which waited for: 7 -> 4; matrix products, arithmetic and copies ran while one was open for 0% -> 0% of each run, Pallas kernels for 2% -> 3%
where the time goes in v2:
time: 127 us; the launch traced here: 126 us
  blocking collectives  73.7 us (58%)
  starting transfers between devices  24.4 us (19%)
  waiting for transfers between devices  16.6 us (13%)
  Pallas kernels  8.68 us (7%)
  between operations  1.46 us (1%)
  local copies, waits for them, and re-layouts  1.33 us (1%)
    all_to_all x1, blocking collectives, shards(): lax.all_to_all(blocks.reshape(group, 1, depth), ('zhi',) + SPACE, 0, 0, t...  44 us
    all_to_all x1, blocking collectives, shards(): lax.all_to_all(copies.reshape(group, 2, depth), ('zhi',) + SPACE, 0, 0, t...  29.7 us
    ppermute x4, waiting for transfers between devices, swap(): return lax.ppermute(value, SPACE, pairs(start))  14.5 us
    ppermute x4, starting transfers between devices, swap(): return lax.ppermute(value, SPACE, pairs(start))  14 us
    ppermute x1, starting transfers between devices, shards(): other = lax.ppermute(own, 'core', [(0, 1), (1, 0)])  5.98 us
    ppermute x1, starting transfers between devices, shards(): other = lax.ppermute(theirs, 'core', [(0, 1), (1, 0)])  4.38 us
  transfers between devices with their start and end apart: 6, of which 4 were waited for; matrix products, arithmetic and copies ran while one was open for 0% of the time, Pallas kernels for 3%

profile of v2, /device:TPU:1, one launch (start us, length us, event | category | flops | bytes accessed | tf_op | source)
XLA Modules:
  0.0 126.1 jit_solution(13959304324989104171)
XLA Ops:
  0.6 0.1 stack.19.where
  0.7 1.2 copy-done.3
  2.0 0.6 shard_map.77
  2.6 0.7 collective-permute-start
  3.3 6.5 %collective-permute-start.1 = (f32[4,256,128]{2,1,0:T(8,128)S(1)}, f32[4,256,128]{2,1,0:T(8,128)S(1)}, u32[]{:S(2)}, u32[]{:S(2)}) collective-permute-start(f32[4,256,128]{2,1,0:T(8,128)S(1)} %get-tuple-element.13.far), channel_id=1, source_target_pairs={{0,1},{2,3},{4,5},{6,7},{8,9},{10,11},{12,13},{14,15},{16,17},{18,... | collective-permute-start | bytes 1572872 | tf_op jit(solution)/shard_map/ppermute | solution.py:305
  10.5 1.6 %shard_map.78 = (f32[4,2,256,128]{3,2,1,0:T(8,128)S(1)}, f32[2,256,128]{2,1,0:T(8,128)S(1)}, f32[2,256,128]{2,1,0:T(8,128)S(1)}) custom-call(f32[1]{0:T(128)S(6)} %copy.9.reynolds, s32[5]{0:T(128)S(1)} %stack.19.where, f32[4,256,128]{2,1,0:T(8,128)S(1)} %get-tuple-element.12.near, f32[4,256,128]{2,1,0:T(8,128)S(1)} %get-tuple-element.13.far, ...), custom_call_target="tpu_custom_call" | custom-call | flops 1000000 | bytes 4000000 | tf_op jit(solution)/shard_map/pallas_call | solution.py:318
  12.1 0.6 shard_map.79.near
  12.7 0.0 copy-start.4
  12.8 0.7 collective-permute-start.2
  13.5 5.6 %collective-permute-done.1.halo = f32[4,256,128]{2,1,0:T(8,128)S(1)} collective-permute-done((f32[4,256,128]{2,1,0:T(8,128)S(1)}, f32[4,256,128]{2,1,0:T(8,128)S(1)}, u32[]{:S(2)}, u32[]{:S(2)}) %collective-permute-start.1) | collective-permute-done | bytes 524320 | tf_op jit(solution)/shard_map/ppermute | solution.py:305
  19.1 0.6 shard_map.80.far
  19.7 6.1 %collective-permute-start.3 = (f32[4,256,128]{2,1,0:T(8,128)S(1)}, f32[4,256,128]{2,1,0:T(8,128)S(1)}, u32[]{:S(2)}, u32[]{:S(2)}) collective-permute-start(f32[4,256,128]{2,1,0:T(8,128)S(1)} %shard_map.80.far), channel_id=1, source_target_pairs={{0,1},{2,3},{4,5},{6,7},{8,9},{10,11},{12,13},{14,15},{16,17},{18,... | collective-permute-start | bytes 1572872 | tf_op jit(solution)/shard_map/ppermute | solution.py:305
  25.8 1.5 %shard_map.81 = (f32[4,2,256,128]{3,2,1,0:T(8,128)S(1)}, f32[3,2,256,128]{3,2,1,0:T(8,128)S(1)}) custom-call(f32[1]{0:T(128)S(6)} %copy.9.reynolds, s32[8]{0:T(128)S(1)} %copy-done.4, s32[5]{0:T(128)S(1)} %stack.19.where, f32[4,256,128]{2,1,0:T(8,128)S(1)} %shard_map.79.near, f32[4,256,128]{2,1,0:T(8,128)S(1)} %shard_map.80.far, ...), custom_call_target="tpu_custom_call" | custom-call | flops 1000000 | bytes 4000000 | tf_op jit(solution)/shard_map/pallas_call | solution.py:330
  27.4 8.8 %collective-permute-done.3.far = f32[4,256,128]{2,1,0:T(8,128)S(1)} collective-permute-done((f32[4,256,128]{2,1,0:T(8,128)S(1)}, f32[4,256,128]{2,1,0:T(8,128)S(1)}, u32[]{:S(2)}, u32[]{:S(2)}) %collective-permute-start.3) | collective-permute-done | bytes 524320 | tf_op jit(solution)/shard_map/ppermute | solution.py:305
  36.2 2.0 %shard_map.82 = (f32[1,4,2,256,128]{4,3,2,1,0:T(8,128)}, f32[2,128,128]{2,1,0:T(8,128)S(1)}, f32[2,128,128]{2,1,0:T(8,128)S(1)}) custom-call(s32[5]{0:T(128)S(1)} %stack.19.where, f32[4,2,256,128]{3,2,1,0:T(8,128)S(1)} %get-tuple-element.17.part, f32[2,256,128]{2,1,0:T(8,128)S(1)} %get-tuple-element.15.factor, f32[2,256,128]{2,1,0:T(8,128)S(1)} %get-tuple-element.16.scaled, ...), custom_call_target="tpu_custom_call" | custom-call | flops 1000000 | bytes 4000000 | tf_op jit(solution)/shard_map/pallas_call | solution.py:336
  38.2 4.4 %collective-permute-start.4 = (f32[2,128,128]{2,1,0:T(8,128)S(1)}, f32[2,128,128]{2,1,0:T(8,128)S(1)}, u32[]{:S(2)}, u32[]{:S(2)}) collective-permute-start(f32[2,128,128]{2,1,0:T(8,128)S(1)} %get-tuple-element.21), channel_id=1, source_target_pairs={{0,64},{64,0},{1,65},{65,1},{2,66},{66,2},{3,67},{67,3},{4,68},{68... | collective-permute-start | bytes 393224 | tf_op jit(solution)/shard_map/ppermute | solution.py:347
  42.6 1.0 collective-permute-done.4.other
  43.5 0.1 shard_map.83
  43.6 44.0 %all_to_all.10 = f32[256,1,128]{2,1,0:T(1,128)S(1)} all-to-all(f32[256,1,128]{2,1,0:T(1,128)S(1)} %bitcast.13), channel_id=1, replica_groups=mesh['zhi'=4,'core'=2,'zlo'=4,'x'=4,'y'=4] {'zhi','zlo','x','y'}, dimensions={0} | all-to-all | bytes 262144 | tf_op jit(solution)/shard_map/all_to_all | solution.py:350
  87.6 0.2 shard_map.84
  87.9 29.7 %all_to_all.11 = f32[256,2,128]{2,1,0:T(2,128)S(1)} all-to-all(f32[256,2,128]{2,1,0:T(2,128)S(1)} %bitcast.10), channel_id=1, replica_groups=mesh['zhi'=4,'core'=2,'zlo'=4,'x'=4,'y'=4] {'zhi','zlo','x','y'}, dimensions={0} | all-to-all | bytes 524288 | tf_op jit(solution)/shard_map/all_to_all | solution.py:354
  117.6 6.0 %collective-permute-start.5 = (f32[512,128]{1,0:T(8,128)S(1)}, f32[512,128]{1,0:T(8,128)S(1)}, u32[]{:S(2)}, u32[]{:S(2)}) collective-permute-start(f32[512,128]{1,0:T(8,128)S(1)} %bitcast.11), channel_id=1, source_target_pairs={{0,64},{64,0},{1,65},{65,1},{2,66},{66,2},{3,67},{67,3},{4,68},{68... | collective-permute-start | bytes 786440 | tf_op jit(solution)/shard_map/ppermute | solution.py:356
  123.5 1.1 collective-permute-done.5.other
  124.7 1.4 %shard_map.85 = f32[2,256,128]{2,1,0:T(8,128)} custom-call(s32[5]{0:T(128)S(1)} %stack.19.where, f32[2,256,128]{2,1,0:T(8,128)S(1)} %copy-done, f32[512,128]{1,0:T(8,128)S(1)} %bitcast.12, f32[512,128]{1,0:T(8,128)S(1)} %collective-permute-done.5.other), custom_call_target="tpu_custom_call" | custom-call | flops 1000000 | bytes 4000000 | tf_op jit(solution)/shard_map/pallas_call | solution.py:357
  (10 shorter events, 0.0 us)
Async XLA Ops:
  0.7 1.2 copy-start.3
  2.0 8.6 %copy-start = (f32[2,256,128]{2,1,0:T(8,128)S(1)}, f32[2,256,128]{2,1,0:T(8,128)}, u32[]{:S(2)}) copy-start(f32[2,256,128]{2,1,0:T(8,128)} %porosity.5) | copy-start | bytes 786436
  2.0 8.6 %copy-start.1 = (bf16[1,3,2,256,128]{4,3,2,1,0:T(8,128)(2,1)S(1)}, bf16[1,3,2,256,128]{4,3,2,1,0:T(8,128)(2,1)}, u32[]{:S(2)}) copy-start(bf16[1,3,2,256,128]{4,3,2,1,0:T(8,128)(2,1)} %vel.3) | copy-start | bytes 1179652
  2.0 8.6 %copy-start.2 = (s32[2,256,128]{2,1,0:T(8,128)S(1)}, s32[2,256,128]{2,1,0:T(8,128)}, u32[]{:S(2)}) copy-start(s32[2,256,128]{2,1,0:T(8,128)} %flags.3) | copy-start | bytes 786436
  2.6 9.5 %collective-permute-start = (f32[4,256,128]{2,1,0:T(8,128)S(1)}, f32[4,256,128]{2,1,0:T(8,128)S(1)}, u32[]{:S(2)}, u32[]{:S(2)}) collective-permute-start(f32[4,256,128]{2,1,0:T(8,128)S(1)} %get-tuple-element.12.near), channel_id=1, source_target_pairs={{1,2},{3,4},{5,6},{7,8},{9,10},{11,12},{13,14},{15,16},{17,18},{19... | collective-permute-start | bytes 1572872 | tf_op jit(solution)/shard_map/ppermute | solution.py:305
  3.3 15.8 %collective-permute-start.1 = (f32[4,256,128]{2,1,0:T(8,128)S(1)}, f32[4,256,128]{2,1,0:T(8,128)S(1)}, u32[]{:S(2)}, u32[]{:S(2)}) collective-permute-start(f32[4,256,128]{2,1,0:T(8,128)S(1)} %get-tuple-element.13.far), channel_id=1, source_target_pairs={{0,1},{2,3},{4,5},{6,7},{8,9},{10,11},{12,13},{14,15},{16,17},{18,... | collective-permute-start | bytes 1572872 | tf_op jit(solution)/shard_map/ppermute | solution.py:305
  12.7 13.1 %copy-start.4 = (s32[8]{0:T(128)S(1)}, s32[8]{0:T(128)}, u32[]{:S(2)}) copy-start(s32[8]{0:T(128)} %weights.1) | copy-start | bytes 100
  12.8 14.6 %collective-permute-start.2 = (f32[4,256,128]{2,1,0:T(8,128)S(1)}, f32[4,256,128]{2,1,0:T(8,128)S(1)}, u32[]{:S(2)}, u32[]{:S(2)}) collective-permute-start(f32[4,256,128]{2,1,0:T(8,128)S(1)} %shard_map.79.near), channel_id=1, source_target_pairs={{1,2},{3,4},{5,6},{7,8},{9,10},{11,12},{13,14},{15,16},{17,18},{19... | collective-permute-start | bytes 1572872 | tf_op jit(solution)/shard_map/ppermute | solution.py:305
  19.7 16.5 %collective-permute-start.3 = (f32[4,256,128]{2,1,0:T(8,128)S(1)}, f32[4,256,128]{2,1,0:T(8,128)S(1)}, u32[]{:S(2)}, u32[]{:S(2)}) collective-permute-start(f32[4,256,128]{2,1,0:T(8,128)S(1)} %shard_map.80.far), channel_id=1, source_target_pairs={{0,1},{2,3},{4,5},{6,7},{8,9},{10,11},{12,13},{14,15},{16,17},{18,... | collective-permute-start | bytes 1572872 | tf_op jit(solution)/shard_map/ppermute | solution.py:305
  38.2 5.3 %collective-permute-start.4 = (f32[2,128,128]{2,1,0:T(8,128)S(1)}, f32[2,128,128]{2,1,0:T(8,128)S(1)}, u32[]{:S(2)}, u32[]{:S(2)}) collective-permute-start(f32[2,128,128]{2,1,0:T(8,128)S(1)} %get-tuple-element.21), channel_id=1, source_target_pairs={{0,64},{64,0},{1,65},{65,1},{2,66},{66,2},{3,67},{67,3},{4,68},{68... | collective-permute-start | bytes 393224 | tf_op jit(solution)/shard_map/ppermute | solution.py:347
  117.6 7.1 %collective-permute-start.5 = (f32[512,128]{1,0:T(8,128)S(1)}, f32[512,128]{1,0:T(8,128)S(1)}, u32[]{:S(2)}, u32[]{:S(2)}) collective-permute-start(f32[512,128]{1,0:T(8,128)S(1)} %bitcast.11), channel_id=1, source_target_pairs={{0,64},{64,0},{1,65},{65,1},{2,66},{66,2},{3,67},{67,3},{4,68},{68... | collective-permute-start | bytes 786440 | tf_op jit(solution)/shard_map/ppermute | solution.py:356

commit v3 on v2

--- a/solution.py
+++ b/solution.py
@@ -27,15 +27,15 @@
     return jax.ShapeDtypeStruct(dims, F32)
 
 
-def call(body, ins, outs, specs=None, scratch=(), flops=1_000_000, moved=4_000_000):
+def call(body, ins, outs, specs=None, scratch=(), vmem=32.0):
     return pl.pallas_call(
         body,
         in_specs=ins,
         out_specs=[VM] * len(outs) if specs is None else specs,
         out_shape=list(outs),
         scratch_shapes=list(scratch),
-        compiler_params=pltpu.CompilerParams(vmem_limit_bytes=32 * 1024 * 1024),
-        cost_estimate=pl.CostEstimate(flops=flops, bytes_accessed=moved, transcendentals=0),
+        compiler_params=pltpu.CompilerParams(vmem_limit_bytes=int(vmem * 2**20)),
+        cost_estimate=pl.CostEstimate(flops=1_000_000, bytes_accessed=4_000_000, transcendentals=0),
     )
 
 
@@ -60,21 +60,34 @@
     return before, after
 
 
-def side(where, p):
-    odd = where[4]
+def side(p):
+    place = lax.axis_index("zlo") * lax.axis_size("x") + lax.axis_index("x")
+    odd = lax.rem(place * lax.axis_size("y") + lax.axis_index("y"), 2)
     index = odd if p == 0 else 1 - odd
     return index, (1 - 2 * index).astype(F32)
 
 
-def take_planes(where, adjoint, near, far, sems):
-    copies = [
-        pltpu.make_async_copy(adjoint.at[0, :, side(where, p)[0]], out, sems.at[p])
-        for p, out in ((0, near), (1, far))
-    ]
-    for copy in copies:
-        copy.start()
-    for copy in copies:
-        copy.wait()
+def reader(first, second, far):
+    def read(c, p, r, n):
+        if p == 1:
+            return far[c, r : r + n]
+        if c in (1, 2):
+            return second[c - 1, r : r + n]
+        return first[min(c, 1), r : r + n]
+
+    return read
+
+
+def take_planes(adjoint, first, second, far):
+    index, _ = side(0)
+    for r in range(0, far.shape[1], CHUNK):
+        now = slice(r, r + CHUNK)
+        first[0, now] = adjoint[0, 0, index, now]
+        first[1, now] = adjoint[0, 3, index, now]
+        for c in range(2):
+            second[c, now] = adjoint[0, c + 1, index, now]
+        for c in range(4):
+            far[c, now] = adjoint[0, c, 1 - index, now]
 
 
 def local_chunk(read, p, sign, r, size, rows, u, nu, scale, drive):
@@ -108,13 +121,12 @@
     return 20.0 / jnp.full((1, 128), reynolds[0], F32)
 
 
-def first_local(reynolds, where, near, far, vel, porosity, flags, part, factor, scaled):
-    rows = near.shape[1]
+def first_local(reynolds, first, second, far, vel, porosity, flags, part, factor, scaled):
+    rows = far.shape[1]
     nu = viscosity_of(reynolds)
-    planes = (near, far)
-    read = lambda c, p, r, n: planes[p][c, r : r + n]
+    read = reader(first, second, far)
     for p in range(2):
-        index, sign = side(where, p)
+        index, sign = side(p)
         for r in range(0, rows, CHUNK):
             now = slice(r, r + CHUNK)
             por = porosity[index, now]
@@ -130,38 +142,57 @@
             scaled[p, now] = scale
 
 
-def join(part, factor, scaled, halo, p, sign, now):
-    held = [halo[c, now] for c in range(4)]
+def join_first(part, factor, scaled, halo, p, sign, now):
+    lam, mu = halo
+    outer = part[0, p, now] + factor[p, now] * lam + (0.5 * sign) * (scaled[p, now] * mu)
+    return outer, part[3, p, now] + (0.5 * BETA * sign) * lam
+
+
+def join_second(part, factor, halo, p, now):
     outer = factor[p, now]
-    lam = [part[c, p, now] + outer * held[c] for c in range(3)]
-    lam[0] = lam[0] + (0.5 * sign) * (scaled[p, now] * held[3])
-    mu = part[3, p, now] + (0.5 * BETA * sign) * held[0]
-    return lam, mu
-
-
-def first_join(p, where, part, factor, scaled, halo, out):
-    _, sign = side(where, p)
+    return [part[c + 1, p, now] + outer * halo[c] for c in range(2)]
+
+
+def near_first(part, factor, scaled, halo, out):
+    _, sign = side(0)
     for r in range(0, halo.shape[1], CHUNK):
         now = slice(r, r + CHUNK)
-        lam, mu = join(part, factor, scaled, halo, p, sign, now)
-        for c in range(3):
-            out[c, now] = lam[c]
-        out[3, now] = mu
-
-
-def second_local(reynolds, weights, where, near, far, vel, porosity, flags, scaled, part, pull):
-    rows = near.shape[1]
+        out[0, now], out[1, now] = join_first(
+            part, factor, scaled, (halo[0, now], halo[1, now]), 0, sign, now
+        )
+
+
+def near_second(part, factor, halo, after, out):
+    for r in range(0, halo.shape[1], CHUNK):
+        now = slice(r, r + CHUNK)
+        out[0, now], out[1, now] = join_second(part, factor, (halo[0, now], halo[1, now]), 0, now)
+
+
+def far_all(part, factor, scaled, halo, after, out):
+    _, sign = side(1)
+    for r in range(0, halo.shape[1], CHUNK):
+        now = slice(r, r + CHUNK)
+        out[0, now], out[3, now] = join_first(
+            part, factor, scaled, (halo[0, now], halo[3, now]), 1, sign, now
+        )
+        out[1, now], out[2, now] = join_second(part, factor, (halo[1, now], halo[2, now]), 1, now)
+
+
+def second_local(
+    reynolds, weights, first, second, far, vel, porosity, flags, scaled, part, pull
+):
+    rows = far.shape[1]
+    point = lax.axis_index("zhi") * lax.axis_size("core") + lax.axis_index("core")
     nu = viscosity_of(reynolds)
     whole = weights[0]
     for i in range(1, weights.shape[0]):
         whole = whole + weights[i]
-    share = jnp.full((1, 128), weights[where[0]].astype(F32), F32) / jnp.full(
+    share = jnp.full((1, 128), weights[point].astype(F32), F32) / jnp.full(
         (1, 128), whole.astype(F32), F32
     )
-    planes = (near, far)
-    read = lambda c, p, r, n: planes[p][c, r : r + n]
+    read = reader(first, second, far)
     for p in range(2):
-        index, sign = side(where, p)
+        index, sign = side(p)
         for r in range(0, rows, CHUNK):
             now = slice(r, r + CHUNK)
             por = porosity[index, now]
@@ -181,27 +212,33 @@
     return 4.0 - jnp.where(at == 0, 1.0, 0.0) - jnp.where(at == whole - 1, 1.0, 0.0)
 
 
-def second_join(where, part, factor, scaled, pull, near, far, state, mine, theirs, held, sens, sems):
-    rows = near.shape[1]
+def second_join(
+    part, factor, scaled, pull, first, second, far, state, mine, theirs, held, sens, sems
+):
+    rows = far.shape[1]
+    read = reader(first, second, far)
     copies = []
-    for p, halo in ((0, near), (1, far)):
-        index, sign = side(where, p)
+    for p in range(2):
+        index, sign = side(p)
         for r in range(0, rows, CHUNK):
             now = slice(r, r + CHUNK)
-            lam, mu = join(part, factor, scaled, halo, p, sign, now)
-            for c in range(3):
-                held[p, c, now] = lam[c]
+            halo = [read(c, p, r, CHUNK) for c in range(4)]
+            lam0, mu = join_first(part, factor, scaled, (halo[0], halo[3]), p, sign, now)
+            lam1, lam2 = join_second(part, factor, halo[1:3], p, now)
+            held[p, 0, now] = lam0
+            held[p, 1, now] = lam1
+            held[p, 2, now] = lam2
             held[p, 3, now] = mu
-            sens[p, now] = pull[0, p, now] * lam[0] + pull[1, p, now] * lam[1] + pull[2, p, now] * lam[2]
+            sens[p, now] = pull[0, p, now] * lam0 + pull[1, p, now] * lam1 + pull[2, p, now] * lam2
         copy = pltpu.make_async_copy(held.at[p], state.at[0, :, index], sems.at[p])
         copy.start()
         copies.append(copy)
     half = rows // 2
-    core = where[1]
+    core = lax.axis_index("core")
     lane = lax.broadcasted_iota(jnp.int32, (CHUNK, 128), 1)
     row = lax.broadcasted_iota(jnp.int32, (CHUNK, 128), 0)
     for p in range(2):
-        index, _ = side(where, p)
+        index, _ = side(p)
         for r in range(0, rows, CHUNK):
             read = lambda a, n: sens[p, a : a + n]
             ym, yp = row_shift(read, r, CHUNK, rows)
@@ -247,9 +284,9 @@
 
 def filter_planes(points, blocks, out):
     slabs = blocks.shape[0] // points
-    total = blocks[0:slabs]
+    total = blocks[pl.ds(0, slabs, stride=points)]
     for q in range(1, points):
-        total = total + blocks[q * slabs : (q + 1) * slabs]
+        total = total + blocks[pl.ds(q, slabs, stride=points)]
     swapped = swap_halves(total)
     at = lax.broadcasted_iota(jnp.int32, total.shape, 0)
     left = left_half(total.shape)
@@ -259,17 +296,17 @@
     filtered = (2.0 * total + swapped + jnp.where(left, below, above)) / counts(plane, 2 * slabs)
     largest = jnp.full(total.shape, jnp.max(jnp.abs(filtered)), F32)
     for q in range(points):
-        out[pl.ds(2 * q * slabs, slabs, stride=2)] = filtered
-        out[pl.ds(2 * q * slabs + 1, slabs, stride=2)] = largest
-
-
-def update(where, porosity, own, other, out):
+        out[pl.ds(2 * q, slabs, stride=2 * points)] = filtered
+        out[pl.ds(2 * q + 1, slabs, stride=2 * points)] = largest
+
+
+def update(porosity, own, other, out):
     n = own.shape[0] // 2
     half = n // 2
     ends = [ref[pl.ds(1, n, stride=2)] for ref in (own, other)]
     largest = jnp.max(jnp.maximum(ends[0], ends[1]))
     factor = STEP / jnp.full((1, 128), largest + EPS, F32)
-    core = where[1]
+    core = lax.axis_index("core")
     for held, base in ((own, core * half), (other, half - core * half)):
         for r in range(0, half, CHUNK):
             to = pl.ds(pl.multiple_of(base + r, CHUNK), CHUNK)
@@ -284,18 +321,6 @@
     points = lax.axis_size("zhi")
     cores = lax.axis_size("core")
     spaces = lax.axis_size("zlo") * lax.axis_size("x") * lax.axis_size("y")
-    core = lax.axis_index("core")
-    place = (lax.axis_index("zlo") * lax.axis_size("x") + lax.axis_index("x")) * lax.axis_size("y")
-    place = place + lax.axis_index("y")
-    where = jnp.stack(
-        [
-            lax.axis_index("zhi") * cores + core,
-            core,
-            place * planes,
-            jnp.int32(planes * spaces),
-            place % 2,
-        ]
-    ).astype(jnp.int32)
 
     def pairs(start):
         there = [(i, i + 1) for i in range(start, spaces - 1, 2)]
@@ -307,35 +332,33 @@
     half_state = shape(4, planes, rows, depth)
     field = shape(planes, rows, depth)
     plane = shape(4, rows, depth)
-    near, far = call(
+    pair = shape(2, rows, depth)
+    first, second, far = call(
         take_planes,
-        [SM, HB],
-        [plane, plane],
-        scratch=[pltpu.SemaphoreType.DMA((2,))],
-    )(where, adjoint)
-    halo_near = swap(near, 1)
+        [VM],
+        [pair, pair, plane],
+    )(adjoint)
+    halo_first = swap(first, 1)
     halo_far = swap(far, 0)
-    part, factor, scaled = call(first_local, [SM, SM] + [VM] * 5, [half_state, field, field])(
-        reynolds, where, near, far, fwd_velocity, porosity, flags
-    )
-    ins = [SM] + [VM] * 4
-    (near,) = call(functools.partial(first_join, 0), ins, [plane])(
-        where, part, factor, scaled, halo_near
-    )
-    halo_near = swap(near, 1)
-    (far,) = call(functools.partial(first_join, 1), ins, [plane])(
-        where, part, factor, scaled, halo_far
-    )
+    halo_second = swap(second, 1)
+    part, factor, scaled = call(first_local, [SM] + [VM] * 6, [half_state, field, field])(
+        reynolds, first, second, far, fwd_velocity, porosity, flags
+    )
+    (first,) = call(near_first, [VM] * 4, [pair])(part, factor, scaled, halo_first)
+    halo_first = swap(first, 1)
+    (far,) = call(far_all, [VM] * 5, [plane])(part, factor, scaled, halo_far, first)
     halo_far = swap(far, 0)
+    (second,) = call(near_second, [VM] * 4, [pair])(part, factor, halo_second, far)
+    halo_second = swap(second, 1)
     part, pull = call(
         second_local,
-        [SM, SM, SM] + [VM] * 6,
+        [SM, SM] + [VM] * 7,
         [half_state, shape(3, planes, rows, depth)],
-    )(reynolds, weights, where, near, far, fwd_velocity, porosity, flags, scaled)
+    )(reynolds, weights, first, second, far, fwd_velocity, porosity, flags, scaled)
     half = shape(planes, rows // cores, depth)
     state, mine, theirs = call(
         second_join,
-        [SM] + [VM] * 6,
+        [VM] * 7,
         [shape(1, 4, planes, rows, depth), half, half],
         specs=[HB, VM, VM],
         scratch=[
@@ -343,18 +366,18 @@
             pltpu.VMEM((planes, rows, depth), F32),
             pltpu.SemaphoreType.DMA((2,)),
         ],
-    )(where, part, factor, scaled, pull, halo_near, halo_far)
+    )(part, factor, scaled, pull, halo_first, halo_second, halo_far)
     other = lax.ppermute(theirs, "core", [(0, 1), (1, 0)])
     group = points * spaces
     (blocks,) = call(add_cores, [VM, VM], [shape(group, depth)])(mine, other)
-    blocks = lax.all_to_all(blocks.reshape(group, 1, depth), ("zhi",) + SPACE, 0, 0, tiled=True)
+    blocks = lax.all_to_all(blocks.reshape(group, 1, depth), SPACE + ("zhi",), 0, 0, tiled=True)
     (copies,) = call(functools.partial(filter_planes, points), [VM], [shape(2 * group, depth)])(
         blocks.reshape(group, depth)
     )
-    own = lax.all_to_all(copies.reshape(group, 2, depth), ("zhi",) + SPACE, 0, 0, tiled=True)
+    own = lax.all_to_all(copies.reshape(group, 2, depth), SPACE + ("zhi",), 0, 0, tiled=True)
     own = own.reshape(2 * group, depth)
     other = lax.ppermute(own, "core", [(0, 1), (1, 0)])
-    (porosity_new,) = call(update, [SM, VM, VM, VM], [field])(where, porosity, own, other)
+    (porosity_new,) = call(update, [VM] * 3, [field])(porosity, own, other)
     return state, porosity_new
 
 

time: 127 us -> 122 us (0.961)
  waiting for transfers between devices: 16.6 us -> 10.9 us
  Pallas kernels: 8.68 us -> 5.17 us
  blocking collectives: 73.7 us -> 76.3 us
  starting transfers between devices: 24.4 us -> 26.4 us
    ppermute x4 -> x6, waiting for transfers between devices: 14.5 us -> 8.75 us  [swap(): return lax.ppermute(value, SPACE, pairs(start))]
    ppermute x1, starting transfers between devices: 4.38 us -> 9.45 us  [shards(): other = lax.ppermute(theirs, 'core', [(0, 1), (1, 0)])]
    pallas_call x7 -> x8, Pallas kernels: 8.36 us -> 4.85 us  [the longest x1 1.44 us: shards(): call(second_join, [VM] * 7, [shape(1, 4, planes, rows, depth), half, half...]
    ppermute x4 -> x6, starting transfers between devices: 14 us -> 10.9 us  [swap(): return lax.ppermute(value, SPACE, pairs(start))]
    all_to_all x2, blocking collectives: 73.7 us -> 76.3 us  [the longest x1 47.7 us: shards(): lax.all_to_all(blocks.reshape(group, 1, depth), SPACE + ('zhi',), 0, 0, t...]
  transfers between devices with their start and end apart: 6 -> 8, of which waited for: 4 -> 4; matrix products, arithmetic and copies ran while one was open for 0% -> 0% of each run, Pallas kernels for 3% -> 2%
where the time goes in v3:
time: 122 us; the launch traced here: 121 us
  blocking collectives  76.3 us (63%)
  starting transfers between devices  26.4 us (22%)
  waiting for transfers between devices  10.9 us (9%)
  Pallas kernels  5.17 us (4%)
  between operations  1.5 us (1%)
  local copies, waits for them, and re-layouts  1.3 us (1%)
    all_to_all x1, blocking collectives, shards(): lax.all_to_all(blocks.reshape(group, 1, depth), SPACE + ('zhi',), 0, 0, t...  47.7 us
    all_to_all x1, blocking collectives, shards(): lax.all_to_all(copies.reshape(group, 2, depth), SPACE + ('zhi',), 0, 0, t...  28.5 us
    ppermute x6, starting transfers between devices, swap(): return lax.ppermute(value, SPACE, pairs(start))  10.9 us
    ppermute x1, starting transfers between devices, shards(): other = lax.ppermute(theirs, 'core', [(0, 1), (1, 0)])  9.45 us
    ppermute x6, waiting for transfers between devices, swap(): return lax.ppermute(value, SPACE, pairs(start))  8.75 us
    ppermute x1, starting transfers between devices, shards(): other = lax.ppermute(own, 'core', [(0, 1), (1, 0)])  6.09 us
  transfers between devices with their start and end apart: 8, of which 4 were waited for; matrix products, arithmetic and copies ran while one was open for 0% of the time, Pallas kernels for 2%

profile of v3, /device:TPU:1, one launch (start us, length us, event | category | flops | bytes accessed | tf_op | source)
XLA Modules:
  0.0 121.5 jit_solution(8437743768449463542)
XLA Ops:
  0.7 1.3 %copy-done.2 = f32[1,4,2,256,128]{4,3,2,1,0:T(8,128)S(1)} copy-done((f32[1,4,2,256,128]{4,3,2,1,0:T(8,128)S(1)}, f32[1,4,2,256,128]{4,3,2,1,0:T(8,128)}, u32[]{:S(2)}) %copy-start.2) | copy-done | bytes 1048600
  1.9 0.1 shard_map.77
  2.0 4.0 %collective-permute-start.2 = (f32[4,256,128]{2,1,0:T(8,128)S(1)}, f32[4,256,128]{2,1,0:T(8,128)S(1)}, u32[]{:S(2)}, u32[]{:S(2)}) collective-permute-start(f32[4,256,128]{2,1,0:T(8,128)S(1)} %get-tuple-element.15.far), channel_id=1, source_target_pairs={{0,1},{2,3},{4,5},{6,7},{8,9},{10,11},{12,13},{14,15},{16,17},{18,... | collective-permute-start | bytes 1572872 | tf_op jit(solution)/shard_map/ppermute | solution.py:330
  6.1 0.7 collective-permute-start
  6.7 0.7 collective-permute-start.1
  8.1 0.9 shard_map.78
  9.1 3.7 %collective-permute-done.2.halo = f32[4,256,128]{2,1,0:T(8,128)S(1)} collective-permute-done((f32[4,256,128]{2,1,0:T(8,128)S(1)}, f32[4,256,128]{2,1,0:T(8,128)S(1)}, u32[]{:S(2)}, u32[]{:S(2)}) %collective-permute-start.2) | collective-permute-done | bytes 524320 | tf_op jit(solution)/shard_map/ppermute | solution.py:330
  12.8 0.1 shard_map.80.after.far
  12.8 0.0 copy-start.4
  12.8 4.1 %collective-permute-start.5 = (f32[4,256,128]{2,1,0:T(8,128)S(1)}, f32[4,256,128]{2,1,0:T(8,128)S(1)}, u32[]{:S(2)}, u32[]{:S(2)}) collective-permute-start(f32[4,256,128]{2,1,0:T(8,128)S(1)} %shard_map.80.after.far), channel_id=1, source_target_pairs={{0,1},{2,3},{4,5},{6,7},{8,9},{10,11},{12,13},{14,15},{16,17},{18,... | collective-permute-start | bytes 1572872 | tf_op jit(solution)/shard_map/ppermute | solution.py:330
  17.0 0.7 collective-permute-start.3
  17.7 0.7 collective-permute-start.4
  18.4 1.4 %shard_map.82 = (f32[4,2,256,128]{3,2,1,0:T(8,128)S(1)}, f32[3,2,256,128]{3,2,1,0:T(8,128)S(1)}) custom-call(f32[1]{0:T(128)S(6)} %copy.9.reynolds, s32[8]{0:T(128)S(1)} %copy-done.4, f32[2,256,128]{2,1,0:T(8,128)S(1)} %shard_map.79.after.first, f32[2,256,128]{2,1,0:T(8,128)S(1)} %shard_map.81.second, f32[4,256,128]{2,1,0:T(8,128)S(1)} %shard_map.80.after.far, ...), custom_call_target="tpu_custom_call" | custom-call | flops 1000000 | bytes 4000000 | tf_op jit(solution)/shard_map/pallas_call | solution.py:353
  19.8 5.1 %collective-permute-done.5.far = f32[4,256,128]{2,1,0:T(8,128)S(1)} collective-permute-done((f32[4,256,128]{2,1,0:T(8,128)S(1)}, f32[4,256,128]{2,1,0:T(8,128)S(1)}, u32[]{:S(2)}, u32[]{:S(2)}) %collective-permute-start.5) | collective-permute-done | bytes 524320 | tf_op jit(solution)/shard_map/ppermute | solution.py:330
  24.9 1.4 %shard_map.83 = (f32[1,4,2,256,128]{4,3,2,1,0:T(8,128)}, f32[2,128,128]{2,1,0:T(8,128)S(1)}, f32[2,128,128]{2,1,0:T(8,128)S(1)}) custom-call(f32[4,2,256,128]{3,2,1,0:T(8,128)S(1)} %get-tuple-element.19.part, f32[2,256,128]{2,1,0:T(8,128)S(1)} %get-tuple-element.17.factor, f32[2,256,128]{2,1,0:T(8,128)S(1)} %get-tuple-element.18.scaled, ...), custom_call_target="tpu_custom_call" | custom-call | flops 1000000 | bytes 4000000 | tf_op jit(solution)/shard_map/pallas_call | solution.py:359
  26.3 9.4 %collective-permute-start.6 = (f32[2,128,128]{2,1,0:T(8,128)S(1)}, f32[2,128,128]{2,1,0:T(8,128)S(1)}, u32[]{:S(2)}, u32[]{:S(2)}) collective-permute-start(f32[2,128,128]{2,1,0:T(8,128)S(1)} %get-tuple-element.23), channel_id=1, source_target_pairs={{0,64},{64,0},{1,65},{65,1},{2,66},{66,2},{3,67},{67,3},{4,68},{68... | collective-permute-start | bytes 393224 | tf_op jit(solution)/shard_map/ppermute | solution.py:370
  35.8 1.0 collective-permute-done.6.other
  36.8 0.1 shard_map.84
  36.9 47.7 %all_to_all.10 = f32[256,1,128]{2,1,0:T(1,128)S(1)} all-to-all(f32[256,1,128]{2,1,0:T(1,128)S(1)} %bitcast.9), channel_id=1, replica_groups=mesh['zhi'=4,'core'=2,'zlo'=4,'x'=4,'y'=4] {'zlo','x','y','zhi'}, dimensions={0} | all-to-all | bytes 262144 | tf_op jit(solution)/shard_map/all_to_all | solution.py:373
  84.6 0.2 shard_map.85
  84.8 28.5 %all_to_all.11 = f32[256,2,128]{2,1,0:T(2,128)S(1)} all-to-all(f32[256,2,128]{2,1,0:T(2,128)S(1)} %bitcast.6), channel_id=1, replica_groups=mesh['zhi'=4,'core'=2,'zlo'=4,'x'=4,'y'=4] {'zlo','x','y','zhi'}, dimensions={0} | all-to-all | bytes 524288 | tf_op jit(solution)/shard_map/all_to_all | solution.py:377
  113.4 6.1 %collective-permute-start.7 = (f32[512,128]{1,0:T(8,128)S(1)}, f32[512,128]{1,0:T(8,128)S(1)}, u32[]{:S(2)}, u32[]{:S(2)}) collective-permute-start(f32[512,128]{1,0:T(8,128)S(1)} %bitcast.7), channel_id=1, source_target_pairs={{0,64},{64,0},{1,65},{65,1},{2,66},{66,2},{3,67},{67,3},{4,68},{68... | collective-permute-start | bytes 786440 | tf_op jit(solution)/shard_map/ppermute | solution.py:379
  119.5 1.1 collective-permute-done.7.other
  120.6 0.9 shard_map.86
  (14 shorter events, 0.1 us)
Async XLA Ops:
  0.6 7.4 %copy-start = (f32[2,256,128]{2,1,0:T(8,128)S(1)}, f32[2,256,128]{2,1,0:T(8,128)}, u32[]{:S(2)}) copy-start(f32[2,256,128]{2,1,0:T(8,128)} %porosity.5) | copy-start | bytes 786436
  0.6 7.4 %copy-start.1 = (bf16[1,3,2,256,128]{4,3,2,1,0:T(8,128)(2,1)S(1)}, bf16[1,3,2,256,128]{4,3,2,1,0:T(8,128)(2,1)}, u32[]{:S(2)}) copy-start(bf16[1,3,2,256,128]{4,3,2,1,0:T(8,128)(2,1)} %vel.3) | copy-start | bytes 1179652
  0.7 1.3 %copy-start.2 = (f32[1,4,2,256,128]{4,3,2,1,0:T(8,128)S(1)}, f32[1,4,2,256,128]{4,3,2,1,0:T(8,128)}, u32[]{:S(2)}) copy-start(f32[1,4,2,256,128]{4,3,2,1,0:T(8,128)} %adjoint.1) | copy-start | bytes 3145732
  1.9 6.2 %copy-start.3 = (s32[2,256,128]{2,1,0:T(8,128)S(1)}, s32[2,256,128]{2,1,0:T(8,128)}, u32[]{:S(2)}) copy-start(s32[2,256,128]{2,1,0:T(8,128)} %flags.3) | copy-start | bytes 786436
  2.0 10.7 %collective-permute-start.2 = (f32[4,256,128]{2,1,0:T(8,128)S(1)}, f32[4,256,128]{2,1,0:T(8,128)S(1)}, u32[]{:S(2)}, u32[]{:S(2)}) collective-permute-start(f32[4,256,128]{2,1,0:T(8,128)S(1)} %get-tuple-element.15.far), channel_id=1, source_target_pairs={{0,1},{2,3},{4,5},{6,7},{8,9},{10,11},{12,13},{14,15},{16,17},{18,... | collective-permute-start | bytes 1572872 | tf_op jit(solution)/shard_map/ppermute | solution.py:330
  6.1 3.0 %collective-permute-start = (f32[2,256,128]{2,1,0:T(8,128)S(1)}, f32[2,256,128]{2,1,0:T(8,128)S(1)}, u32[]{:S(2)}, u32[]{:S(2)}) collective-permute-start(f32[2,256,128]{2,1,0:T(8,128)S(1)} %get-tuple-element.13.first), channel_id=1, source_target_pairs={{1,2},{3,4},{5,6},{7,8},{9,10},{11,12},{13,14},{15,16},{17,18},{19... | collective-permute-start | bytes 786440 | tf_op jit(solution)/shard_map/ppermute | solution.py:330
  6.7 10.9 %collective-permute-start.1 = (f32[2,256,128]{2,1,0:T(8,128)S(1)}, f32[2,256,128]{2,1,0:T(8,128)S(1)}, u32[]{:S(2)}, u32[]{:S(2)}) collective-permute-start(f32[2,256,128]{2,1,0:T(8,128)S(1)} %get-tuple-element.14.second), channel_id=1, source_target_pairs={{1,2},{3,4},{5,6},{7,8},{9,10},{11,12},{13,14},{15,16},{17,18},{19... | collective-permute-start | bytes 786440 | tf_op jit(solution)/shard_map/ppermute | solution.py:330
  12.8 5.6 %copy-start.4 = (s32[8]{0:T(128)S(1)}, s32[8]{0:T(128)}, u32[]{:S(2)}) copy-start(s32[8]{0:T(128)} %weights.1) | copy-start | bytes 100
  12.8 12.1 %collective-permute-start.5 = (f32[4,256,128]{2,1,0:T(8,128)S(1)}, f32[4,256,128]{2,1,0:T(8,128)S(1)}, u32[]{:S(2)}, u32[]{:S(2)}) collective-permute-start(f32[4,256,128]{2,1,0:T(8,128)S(1)} %shard_map.80.after.far), channel_id=1, source_target_pairs={{0,1},{2,3},{4,5},{6,7},{8,9},{10,11},{12,13},{14,15},{16,17},{18,... | collective-permute-start | bytes 1572872 | tf_op jit(solution)/shard_map/ppermute | solution.py:330
  17.0 2.9 %collective-permute-start.3 = (f32[2,256,128]{2,1,0:T(8,128)S(1)}, f32[2,256,128]{2,1,0:T(8,128)S(1)}, u32[]{:S(2)}, u32[]{:S(2)}) collective-permute-start(f32[2,256,128]{2,1,0:T(8,128)S(1)} %shard_map.79.after.first), channel_id=1, source_target_pairs={{1,2},{3,4},{5,6},{7,8},{9,10},{11,12},{13,14},{15,16},{17,18},{19... | collective-permute-start | bytes 786440 | tf_op jit(solution)/shard_map/ppermute | solution.py:330
  17.7 2.1 %collective-permute-start.4 = (f32[2,256,128]{2,1,0:T(8,128)S(1)}, f32[2,256,128]{2,1,0:T(8,128)S(1)}, u32[]{:S(2)}, u32[]{:S(2)}) collective-permute-start(f32[2,256,128]{2,1,0:T(8,128)S(1)} %shard_map.81.second), channel_id=1, source_target_pairs={{1,2},{3,4},{5,6},{7,8},{9,10},{11,12},{13,14},{15,16},{17,18},{19... | collective-permute-start | bytes 786440 | tf_op jit(solution)/shard_map/ppermute | solution.py:330
  26.3 10.4 %collective-permute-start.6 = (f32[2,128,128]{2,1,0:T(8,128)S(1)}, f32[2,128,128]{2,1,0:T(8,128)S(1)}, u32[]{:S(2)}, u32[]{:S(2)}) collective-permute-start(f32[2,128,128]{2,1,0:T(8,128)S(1)} %get-tuple-element.23), channel_id=1, source_target_pairs={{0,64},{64,0},{1,65},{65,1},{2,66},{66,2},{3,67},{67,3},{4,68},{68... | collective-permute-start | bytes 393224 | tf_op jit(solution)/shard_map/ppermute | solution.py:370
  113.4 7.2 %collective-permute-start.7 = (f32[512,128]{1,0:T(8,128)S(1)}, f32[512,128]{1,0:T(8,128)S(1)}, u32[]{:S(2)}, u32[]{:S(2)}) collective-permute-start(f32[512,128]{1,0:T(8,128)S(1)} %bitcast.7), channel_id=1, source_target_pairs={{0,64},{64,0},{1,65},{65,1},{2,66},{66,2},{3,67},{67,3},{4,68},{68... | collective-permute-start | bytes 786440 | tf_op jit(solution)/shard_map/ppermute | solution.py:379

commit v4 on v3

--- a/solution.py
+++ b/solution.py
@@ -27,7 +27,7 @@
     return jax.ShapeDtypeStruct(dims, F32)
 
 
-def call(body, ins, outs, specs=None, scratch=(), vmem=32.0):
+def call(body, ins, outs, specs=None, scratch=(), vmem=32.0, flops=1_000_000):
     return pl.pallas_call(
         body,
         in_specs=ins,
@@ -35,7 +35,7 @@
         out_shape=list(outs),
         scratch_shapes=list(scratch),
         compiler_params=pltpu.CompilerParams(vmem_limit_bytes=int(vmem * 2**20)),
-        cost_estimate=pl.CostEstimate(flops=1_000_000, bytes_accessed=4_000_000, transcendentals=0),
+        cost_estimate=pl.CostEstimate(flops=flops, bytes_accessed=4_000_000, transcendentals=0),
     )
 
 
@@ -213,7 +213,7 @@
 
 
 def second_join(
-    part, factor, scaled, pull, first, second, far, state, mine, theirs, held, sens, sems
+    part, factor, scaled, pull, first, second, far, state, mine, theirs, held, sens, weighted, sems
 ):
     rows = far.shape[1]
     read = reader(first, second, far)
@@ -235,8 +235,10 @@
         copies.append(copy)
     half = rows // 2
     core = lax.axis_index("core")
-    lane = lax.broadcasted_iota(jnp.int32, (CHUNK, 128), 1)
+    lane = lax.broadcasted_iota(jnp.int32, (1, 128), 1)
     row = lax.broadcasted_iota(jnp.int32, (CHUNK, 128), 0)
+    along_z = 1.0 / counts(lane, 128)
+    inner = along_z * 0.25
     for p in range(2):
         index, _ = side(p)
         for r in range(0, rows, CHUNK):
@@ -244,17 +246,18 @@
             ym, yp = row_shift(read, r, CHUNK, rows)
             along = ym + yp + 2.0 * read(r, CHUNK)
             zm, zp = lane_shift(along)
-            total = (zm + zp + 2.0 * along) / (counts(row + r, rows) * counts(lane, 128))
-            owner = r // half
-            to = slice(r - owner * half, r - owner * half + CHUNK)
-
-            @pl.when(core == owner)
-            def _():
-                mine[index, to] = total
-
-            @pl.when(core != owner)
-            def _():
-                theirs[index, to] = total
+            if r == 0 or r + CHUNK == rows:
+                scale = along_z / counts(row + r, rows)
+            else:
+                scale = inner
+            weighted[index, r : r + CHUNK] = (zm + zp + 2.0 * along) * scale
+    for owner, (kept, sent) in enumerate(((0, half), (half, 0))):
+
+        @pl.when(core == owner)
+        def _():
+            for p in range(2):
+                mine[p] = weighted[p, kept : kept + half]
+                theirs[p] = weighted[p, sent : sent + half]
 
     for copy in copies:
         copy.wait()
@@ -341,19 +344,20 @@
     halo_first = swap(first, 1)
     halo_far = swap(far, 0)
     halo_second = swap(second, 1)
-    part, factor, scaled = call(first_local, [SM] + [VM] * 6, [half_state, field, field])(
+    part, factor, scaled = call(first_local, [SM] + [VM] * 6, [half_state, field, field], flops=1000000)(
         reynolds, first, second, far, fwd_velocity, porosity, flags
     )
-    (first,) = call(near_first, [VM] * 4, [pair])(part, factor, scaled, halo_first)
+    (first,) = call(near_first, [VM] * 4, [pair], flops=4000000000)(part, factor, scaled, halo_first)
     halo_first = swap(first, 1)
-    (far,) = call(far_all, [VM] * 5, [plane])(part, factor, scaled, halo_far, first)
+    (far,) = call(far_all, [VM] * 5, [plane], flops=4000000000)(part, factor, scaled, halo_far, first)
     halo_far = swap(far, 0)
-    (second,) = call(near_second, [VM] * 4, [pair])(part, factor, halo_second, far)
+    (second,) = call(near_second, [VM] * 4, [pair], flops=4000000000)(part, factor, halo_second, far)
     halo_second = swap(second, 1)
     part, pull = call(
         second_local,
         [SM, SM] + [VM] * 7,
         [half_state, shape(3, planes, rows, depth)],
+        flops=4000000000,
     )(reynolds, weights, first, second, far, fwd_velocity, porosity, flags, scaled)
     half = shape(planes, rows // cores, depth)
     state, mine, theirs = call(
@@ -363,6 +367,7 @@
         specs=[HB, VM, VM],
         scratch=[
             pltpu.VMEM((planes, 4, rows, depth), F32),
+            pltpu.VMEM((planes, rows, depth), F32),
             pltpu.VMEM((planes, rows, depth), F32),
             pltpu.SemaphoreType.DMA((2,)),
         ],

time: 122 us -> 117 us (0.959)
  blocking collectives: 76.3 us -> 68.6 us
  waiting for transfers between devices: 10.9 us -> 15.1 us
    all_to_all x1, blocking collectives: 47.7 us -> 40.1 us  [shards(): lax.all_to_all(blocks.reshape(group, 1, depth), SPACE + ('zhi',), 0, 0, t...]
    ppermute x6, waiting for transfers between devices: 8.75 us -> 13 us  [swap(): return lax.ppermute(value, SPACE, pairs(start))]
    ppermute x1, starting transfers between devices: 9.45 us -> 5.71 us  [shards(): other = lax.ppermute(theirs, 'core', [(0, 1), (1, 0)])]
    ppermute x6, starting transfers between devices: 10.9 us -> 13.5 us  [swap(): return lax.ppermute(value, SPACE, pairs(start))]
where the time goes in v4:
time: 117 us
  blocking collectives  68.6 us (59%)
  starting transfers between devices  25.3 us (22%)
  waiting for transfers between devices  15.1 us (13%)
  Pallas kernels  5.17 us (4%)
  between operations  1.47 us (1%)
  local copies, waits for them, and re-layouts  1.24 us (1%)
    all_to_all x1, blocking collectives, shards(): lax.all_to_all(blocks.reshape(group, 1, depth), SPACE + ('zhi',), 0, 0, t...  40.1 us
    all_to_all x1, blocking collectives, shards(): lax.all_to_all(copies.reshape(group, 2, depth), SPACE + ('zhi',), 0, 0, t...  28.5 us
    ppermute x6, starting transfers between devices, swap(): return lax.ppermute(value, SPACE, pairs(start))  13.5 us
    ppermute x6, waiting for transfers between devices, swap(): return lax.ppermute(value, SPACE, pairs(start))  13 us
    ppermute x1, starting transfers between devices, shards(): other = lax.ppermute(own, 'core', [(0, 1), (1, 0)])  6.09 us
    ppermute x1, starting transfers between devices, shards(): other = lax.ppermute(theirs, 'core', [(0, 1), (1, 0)])  5.71 us
  transfers between devices with their start and end apart: 8, of which 4 were waited for; matrix products, arithmetic and copies ran while one was open for 0% of the time, Pallas kernels for 2%

profile of v4, /device:TPU:1, one launch (start us, length us, event | category | flops | bytes accessed | tf_op | source)
XLA Modules:
  0.0 116.9 jit_solution(7464316651147225206)
XLA Ops:
  0.6 1.2 %copy-done = f32[1,4,2,256,128]{4,3,2,1,0:T(8,128)S(1)} copy-done((f32[1,4,2,256,128]{4,3,2,1,0:T(8,128)S(1)}, f32[1,4,2,256,128]{4,3,2,1,0:T(8,128)}, u32[]{:S(2)}) %copy-start) | copy-done | bytes 1048600
  1.9 0.1 shard_map.77
  1.9 0.8 collective-permute-start
  2.8 6.6 %collective-permute-start.2 = (f32[4,256,128]{2,1,0:T(8,128)S(1)}, f32[4,256,128]{2,1,0:T(8,128)S(1)}, u32[]{:S(2)}, u32[]{:S(2)}) collective-permute-start(f32[4,256,128]{2,1,0:T(8,128)S(1)} %get-tuple-element.15.far), channel_id=1, source_target_pairs={{0,1},{2,3},{4,5},{6,7},{8,9},{10,11},{12,13},{14,15},{16,17},{18,... | collective-permute-start | bytes 1572872 | tf_op jit(solution)/shard_map/ppermute | solution.py:333
  9.3 0.7 collective-permute-start.1
  10.7 1.0 shard_map.78
  11.7 0.1 shard_map.79.after.first
  11.7 0.7 collective-permute-start.3
  12.4 6.1 %collective-permute-done.2.halo = f32[4,256,128]{2,1,0:T(8,128)S(1)} collective-permute-done((f32[4,256,128]{2,1,0:T(8,128)S(1)}, f32[4,256,128]{2,1,0:T(8,128)S(1)}, u32[]{:S(2)}, u32[]{:S(2)}) %collective-permute-start.2) | collective-permute-done | bytes 524320 | tf_op jit(solution)/shard_map/ppermute | solution.py:333
  18.6 0.1 shard_map.80.after.far
  18.6 4.1 %collective-permute-start.5 = (f32[4,256,128]{2,1,0:T(8,128)S(1)}, f32[4,256,128]{2,1,0:T(8,128)S(1)}, u32[]{:S(2)}, u32[]{:S(2)}) collective-permute-start(f32[4,256,128]{2,1,0:T(8,128)S(1)} %shard_map.80.after.far), channel_id=1, source_target_pairs={{0,1},{2,3},{4,5},{6,7},{8,9},{10,11},{12,13},{14,15},{16,17},{18,... | collective-permute-start | bytes 1572872 | tf_op jit(solution)/shard_map/ppermute | solution.py:333
  22.8 0.7 collective-permute-start.4
  23.5 1.5 %shard_map.82 = (f32[4,2,256,128]{3,2,1,0:T(8,128)S(1)}, f32[3,2,256,128]{3,2,1,0:T(8,128)S(1)}) custom-call(f32[1]{0:T(128)S(6)} %copy.9.reynolds, s32[8]{0:T(128)S(1)} %copy-done.4, f32[2,256,128]{2,1,0:T(8,128)S(1)} %shard_map.79.after.first, f32[2,256,128]{2,1,0:T(8,128)S(1)} %shard_map.81.second, f32[4,256,128]{2,1,0:T(8,128)S(1)} %shard_map.80.after.far, ...), custom_call_target="tpu_custom_call" | custom-call | flops 4000000000 | bytes 4000000 | tf_op jit(solution)/shard_map/pallas_call | solution.py:356
  25.0 6.8 %collective-permute-done.5.far = f32[4,256,128]{2,1,0:T(8,128)S(1)} collective-permute-done((f32[4,256,128]{2,1,0:T(8,128)S(1)}, f32[4,256,128]{2,1,0:T(8,128)S(1)}, u32[]{:S(2)}, u32[]{:S(2)}) %collective-permute-start.5) | collective-permute-done | bytes 524320 | tf_op jit(solution)/shard_map/ppermute | solution.py:333
  31.8 1.3 %shard_map.83 = (f32[1,4,2,256,128]{4,3,2,1,0:T(8,128)}, f32[2,128,128]{2,1,0:T(8,128)S(1)}, f32[2,128,128]{2,1,0:T(8,128)S(1)}) custom-call(f32[4,2,256,128]{3,2,1,0:T(8,128)S(1)} %get-tuple-element.19.part, f32[2,256,128]{2,1,0:T(8,128)S(1)} %get-tuple-element.17.factor, f32[2,256,128]{2,1,0:T(8,128)S(1)} %get-tuple-element.18.scaled, ...), custom_call_target="tpu_custom_call" | custom-call | flops 1000000 | bytes 4000000 | tf_op jit(solution)/shard_map/pallas_call | solution.py:363
  33.1 5.7 %collective-permute-start.6 = (f32[2,128,128]{2,1,0:T(8,128)S(1)}, f32[2,128,128]{2,1,0:T(8,128)S(1)}, u32[]{:S(2)}, u32[]{:S(2)}) collective-permute-start(f32[2,128,128]{2,1,0:T(8,128)S(1)} %get-tuple-element.23), channel_id=1, source_target_pairs={{0,64},{64,0},{1,65},{65,1},{2,66},{66,2},{3,67},{67,3},{4,68},{68... | collective-permute-start | bytes 393224 | tf_op jit(solution)/shard_map/ppermute | solution.py:375
  38.8 1.0 collective-permute-done.6.other
  39.8 0.1 shard_map.84
  39.9 40.1 %all_to_all.10 = f32[256,1,128]{2,1,0:T(1,128)S(1)} all-to-all(f32[256,1,128]{2,1,0:T(1,128)S(1)} %bitcast.9), channel_id=1, replica_groups=mesh['zhi'=4,'core'=2,'zlo'=4,'x'=4,'y'=4] {'zlo','x','y','zhi'}, dimensions={0} | all-to-all | bytes 262144 | tf_op jit(solution)/shard_map/all_to_all | solution.py:378
  80.0 0.2 shard_map.85
  80.2 28.5 %all_to_all.11 = f32[256,2,128]{2,1,0:T(2,128)S(1)} all-to-all(f32[256,2,128]{2,1,0:T(2,128)S(1)} %bitcast.6), channel_id=1, replica_groups=mesh['zhi'=4,'core'=2,'zlo'=4,'x'=4,'y'=4] {'zlo','x','y','zhi'}, dimensions={0} | all-to-all | bytes 524288 | tf_op jit(solution)/shard_map/all_to_all | solution.py:382
  108.8 6.1 %collective-permute-start.7 = (f32[512,128]{1,0:T(8,128)S(1)}, f32[512,128]{1,0:T(8,128)S(1)}, u32[]{:S(2)}, u32[]{:S(2)}) collective-permute-start(f32[512,128]{1,0:T(8,128)S(1)} %bitcast.7), channel_id=1, source_target_pairs={{0,64},{64,0},{1,65},{65,1},{2,66},{66,2},{3,67},{67,3},{4,68},{68... | collective-permute-start | bytes 786440 | tf_op jit(solution)/shard_map/ppermute | solution.py:384
  114.9 1.1 collective-permute-done.7.other
  116.0 0.9 shard_map.86
  (14 shorter events, 0.1 us)
Async XLA Ops:
  0.6 1.2 %copy-start = (f32[1,4,2,256,128]{4,3,2,1,0:T(8,128)S(1)}, f32[1,4,2,256,128]{4,3,2,1,0:T(8,128)}, u32[]{:S(2)}) copy-start(f32[1,4,2,256,128]{4,3,2,1,0:T(8,128)} %adjoint.1) | copy-start | bytes 3145732
  1.9 8.8 %copy-start.1 = (f32[2,256,128]{2,1,0:T(8,128)S(1)}, f32[2,256,128]{2,1,0:T(8,128)}, u32[]{:S(2)}) copy-start(f32[2,256,128]{2,1,0:T(8,128)} %porosity.5) | copy-start | bytes 786436
  1.9 8.8 %copy-start.2 = (bf16[1,3,2,256,128]{4,3,2,1,0:T(8,128)(2,1)S(1)}, bf16[1,3,2,256,128]{4,3,2,1,0:T(8,128)(2,1)}, u32[]{:S(2)}) copy-start(bf16[1,3,2,256,128]{4,3,2,1,0:T(8,128)(2,1)} %vel.3) | copy-start | bytes 1179652
  1.9 8.8 %copy-start.3 = (s32[2,256,128]{2,1,0:T(8,128)S(1)}, s32[2,256,128]{2,1,0:T(8,128)}, u32[]{:S(2)}) copy-start(s32[2,256,128]{2,1,0:T(8,128)} %flags.3) | copy-start | bytes 786436
  1.9 9.7 %collective-permute-start = (f32[2,256,128]{2,1,0:T(8,128)S(1)}, f32[2,256,128]{2,1,0:T(8,128)S(1)}, u32[]{:S(2)}, u32[]{:S(2)}) collective-permute-start(f32[2,256,128]{2,1,0:T(8,128)S(1)} %get-tuple-element.13.first), channel_id=1, source_target_pairs={{1,2},{3,4},{5,6},{7,8},{9,10},{11,12},{13,14},{15,16},{17,18},{19... | collective-permute-start | bytes 786440 | tf_op jit(solution)/shard_map/ppermute | solution.py:333
  2.8 15.8 %collective-permute-start.2 = (f32[4,256,128]{2,1,0:T(8,128)S(1)}, f32[4,256,128]{2,1,0:T(8,128)S(1)}, u32[]{:S(2)}, u32[]{:S(2)}) collective-permute-start(f32[4,256,128]{2,1,0:T(8,128)S(1)} %get-tuple-element.15.far), channel_id=1, source_target_pairs={{0,1},{2,3},{4,5},{6,7},{8,9},{10,11},{12,13},{14,15},{16,17},{18,... | collective-permute-start | bytes 1572872 | tf_op jit(solution)/shard_map/ppermute | solution.py:333
  9.3 13.4 %collective-permute-start.1 = (f32[2,256,128]{2,1,0:T(8,128)S(1)}, f32[2,256,128]{2,1,0:T(8,128)S(1)}, u32[]{:S(2)}, u32[]{:S(2)}) collective-permute-start(f32[2,256,128]{2,1,0:T(8,128)S(1)} %get-tuple-element.14.second), channel_id=1, source_target_pairs={{1,2},{3,4},{5,6},{7,8},{9,10},{11,12},{13,14},{15,16},{17,18},{19... | collective-permute-start | bytes 786440 | tf_op jit(solution)/shard_map/ppermute | solution.py:333
  11.7 13.2 %collective-permute-start.3 = (f32[2,256,128]{2,1,0:T(8,128)S(1)}, f32[2,256,128]{2,1,0:T(8,128)S(1)}, u32[]{:S(2)}, u32[]{:S(2)}) collective-permute-start(f32[2,256,128]{2,1,0:T(8,128)S(1)} %shard_map.79.after.first), channel_id=1, source_target_pairs={{1,2},{3,4},{5,6},{7,8},{9,10},{11,12},{13,14},{15,16},{17,18},{19... | collective-permute-start | bytes 786440 | tf_op jit(solution)/shard_map/ppermute | solution.py:333
  18.6 4.9 %copy-start.4 = (s32[8]{0:T(128)S(1)}, s32[8]{0:T(128)}, u32[]{:S(2)}) copy-start(s32[8]{0:T(128)} %weights.1) | copy-start | bytes 100
  18.6 13.2 %collective-permute-start.5 = (f32[4,256,128]{2,1,0:T(8,128)S(1)}, f32[4,256,128]{2,1,0:T(8,128)S(1)}, u32[]{:S(2)}, u32[]{:S(2)}) collective-permute-start(f32[4,256,128]{2,1,0:T(8,128)S(1)} %shard_map.80.after.far), channel_id=1, source_target_pairs={{0,1},{2,3},{4,5},{6,7},{8,9},{10,11},{12,13},{14,15},{16,17},{18,... | collective-permute-start | bytes 1572872 | tf_op jit(solution)/shard_map/ppermute | solution.py:333
  22.8 2.2 %collective-permute-start.4 = (f32[2,256,128]{2,1,0:T(8,128)S(1)}, f32[2,256,128]{2,1,0:T(8,128)S(1)}, u32[]{:S(2)}, u32[]{:S(2)}) collective-permute-start(f32[2,256,128]{2,1,0:T(8,128)S(1)} %shard_map.81.second), channel_id=1, source_target_pairs={{1,2},{3,4},{5,6},{7,8},{9,10},{11,12},{13,14},{15,16},{17,18},{19... | collective-permute-start | bytes 786440 | tf_op jit(solution)/shard_map/ppermute | solution.py:333
  33.1 6.7 %collective-permute-start.6 = (f32[2,128,128]{2,1,0:T(8,128)S(1)}, f32[2,128,128]{2,1,0:T(8,128)S(1)}, u32[]{:S(2)}, u32[]{:S(2)}) collective-permute-start(f32[2,128,128]{2,1,0:T(8,128)S(1)} %get-tuple-element.23), channel_id=1, source_target_pairs={{0,64},{64,0},{1,65},{65,1},{2,66},{66,2},{3,67},{67,3},{4,68},{68... | collective-permute-start | bytes 393224 | tf_op jit(solution)/shard_map/ppermute | solution.py:375
  108.8 7.2 %collective-permute-start.7 = (f32[512,128]{1,0:T(8,128)S(1)}, f32[512,128]{1,0:T(8,128)S(1)}, u32[]{:S(2)}, u32[]{:S(2)}) collective-permute-start(f32[512,128]{1,0:T(8,128)S(1)} %bitcast.7), channel_id=1, source_target_pairs={{0,64},{64,0},{1,65},{65,1},{2,66},{66,2},{3,67},{67,3},{4,68},{68... | collective-permute-start | bytes 786440 | tf_op jit(solution)/shard_map/ppermute | solution.py:384

commit v5 on v4

--- a/solution.py
+++ b/solution.py
@@ -213,13 +213,12 @@
 
 
 def second_join(
-    part, factor, scaled, pull, first, second, far, state, mine, theirs, held, sens, weighted, sems
+    part, factor, scaled, pull, first, second, far, held, mine, theirs, sens, weighted
 ):
     rows = far.shape[1]
     read = reader(first, second, far)
-    copies = []
     for p in range(2):
-        index, sign = side(p)
+        _, sign = side(p)
         for r in range(0, rows, CHUNK):
             now = slice(r, r + CHUNK)
             halo = [read(c, p, r, CHUNK) for c in range(4)]
@@ -230,9 +229,6 @@
             held[p, 2, now] = lam2
             held[p, 3, now] = mu
             sens[p, now] = pull[0, p, now] * lam0 + pull[1, p, now] * lam1 + pull[2, p, now] * lam2
-        copy = pltpu.make_async_copy(held.at[p], state.at[0, :, index], sems.at[p])
-        copy.start()
-        copies.append(copy)
     half = rows // 2
     core = lax.axis_index("core")
     lane = lax.broadcasted_iota(jnp.int32, (1, 128), 1)
@@ -259,6 +255,13 @@
                 mine[p] = weighted[p, kept : kept + half]
                 theirs[p] = weighted[p, sent : sent + half]
 
+
+def write_state(held, state, sems):
+    copies = [
+        pltpu.make_async_copy(held.at[p], state.at[0, :, side(p)[0]], sems.at[p]) for p in range(2)
+    ]
+    for copy in copies:
+        copy.start()
     for copy in copies:
         copy.wait()
 
@@ -360,19 +363,20 @@
         flops=4000000000,
     )(reynolds, weights, first, second, far, fwd_velocity, porosity, flags, scaled)
     half = shape(planes, rows // cores, depth)
-    state, mine, theirs = call(
+    held, mine, theirs = call(
         second_join,
         [VM] * 7,
-        [shape(1, 4, planes, rows, depth), half, half],
-        specs=[HB, VM, VM],
-        scratch=[
-            pltpu.VMEM((planes, 4, rows, depth), F32),
-            pltpu.VMEM((planes, rows, depth), F32),
-            pltpu.VMEM((planes, rows, depth), F32),
-            pltpu.SemaphoreType.DMA((2,)),
-        ],
+        [shape(planes, 4, rows, depth), half, half],
+        scratch=[pltpu.VMEM((planes, rows, depth), F32)] * 2,
     )(part, factor, scaled, pull, halo_first, halo_second, halo_far)
     other = lax.ppermute(theirs, "core", [(0, 1), (1, 0)])
+    (state,) = call(
+        write_state,
+        [VM],
+        [shape(1, 4, planes, rows, depth)],
+        specs=[HB],
+        scratch=[pltpu.SemaphoreType.DMA((2,))],
+    )(held)
     group = points * spaces
     (blocks,) = call(add_cores, [VM, VM], [shape(group, depth)])(mine, other)
     blocks = lax.all_to_all(blocks.reshape(group, 1, depth), SPACE + ("zhi",), 0, 0, tiled=True)

time: 117 us -> 116 us (level)
  transfers between devices with their start and end apart: 8 -> 8, of which waited for: 4 -> 4; matrix products, arithmetic and copies ran while one was open for 0% -> 0% of each run, Pallas kernels for 2% -> 3%
where the time goes in v5:
time: 116 us
  blocking collectives  68.6 us (59%)
  starting transfers between devices  25.3 us (22%)
  waiting for transfers between devices  14.2 us (12%)
  Pallas kernels  5.1 us (4%)
  between operations  1.49 us (1%)
  local copies, waits for them, and re-layouts  1.24 us (1%)
    all_to_all x1, blocking collectives, shards(): lax.all_to_all(blocks.reshape(group, 1, depth), SPACE + ('zhi',), 0, 0, t...  40.1 us
    all_to_all x1, blocking collectives, shards(): lax.all_to_all(copies.reshape(group, 2, depth), SPACE + ('zhi',), 0, 0, t...  28.5 us
    ppermute x6, starting transfers between devices, swap(): return lax.ppermute(value, SPACE, pairs(start))  13.5 us
    ppermute x6, waiting for transfers between devices, swap(): return lax.ppermute(value, SPACE, pairs(start))  13.1 us
    ppermute x1, starting transfers between devices, shards(): other = lax.ppermute(own, 'core', [(0, 1), (1, 0)])  6.09 us
    ppermute x1, starting transfers between devices, shards(): other = lax.ppermute(theirs, 'core', [(0, 1), (1, 0)])  5.71 us
  transfers between devices with their start and end apart: 8, of which 4 were waited for; matrix products, arithmetic and copies ran while one was open for 0% of the time, Pallas kernels for 3%

profile of v5, /device:TPU:1, one launch (start us, length us, event | category | flops | bytes accessed | tf_op | source)
XLA Modules:
  0.0 116.0 jit_solution(2625540729130164198)
XLA Ops:
  0.6 1.2 %copy-done = f32[1,4,2,256,128]{4,3,2,1,0:T(8,128)S(1)} copy-done((f32[1,4,2,256,128]{4,3,2,1,0:T(8,128)S(1)}, f32[1,4,2,256,128]{4,3,2,1,0:T(8,128)}, u32[]{:S(2)}) %copy-start) | copy-done | bytes 1048600
  1.9 0.1 shard_map.77
  1.9 0.8 collective-permute-start
  2.8 6.6 %collective-permute-start.2 = (f32[4,256,128]{2,1,0:T(8,128)S(1)}, f32[4,256,128]{2,1,0:T(8,128)S(1)}, u32[]{:S(2)}, u32[]{:S(2)}) collective-permute-start(f32[4,256,128]{2,1,0:T(8,128)S(1)} %get-tuple-element.15.far), channel_id=1, source_target_pairs={{0,1},{2,3},{4,5},{6,7},{8,9},{10,11},{12,13},{14,15},{16,17},{18,... | collective-permute-start | bytes 1572872 | tf_op jit(solution)/shard_map/ppermute | solution.py:336
  9.3 0.7 collective-permute-start.1
  10.7 0.9 shard_map.78
  11.7 0.7 collective-permute-start.3
  12.3 6.2 %collective-permute-done.2.halo = f32[4,256,128]{2,1,0:T(8,128)S(1)} collective-permute-done((f32[4,256,128]{2,1,0:T(8,128)S(1)}, f32[4,256,128]{2,1,0:T(8,128)S(1)}, u32[]{:S(2)}, u32[]{:S(2)}) %collective-permute-start.2) | collective-permute-done | bytes 524320 | tf_op jit(solution)/shard_map/ppermute | solution.py:336
  18.6 0.1 shard_map.80.after.far
  18.6 4.1 %collective-permute-start.5 = (f32[4,256,128]{2,1,0:T(8,128)S(1)}, f32[4,256,128]{2,1,0:T(8,128)S(1)}, u32[]{:S(2)}, u32[]{:S(2)}) collective-permute-start(f32[4,256,128]{2,1,0:T(8,128)S(1)} %shard_map.80.after.far), channel_id=1, source_target_pairs={{0,1},{2,3},{4,5},{6,7},{8,9},{10,11},{12,13},{14,15},{16,17},{18,... | collective-permute-start | bytes 1572872 | tf_op jit(solution)/shard_map/ppermute | solution.py:336
  22.8 0.7 collective-permute-start.4
  23.5 1.4 %shard_map.82 = (f32[4,2,256,128]{3,2,1,0:T(8,128)S(1)}, f32[3,2,256,128]{3,2,1,0:T(8,128)S(1)}) custom-call(f32[1]{0:T(128)S(6)} %copy.9.reynolds, s32[8]{0:T(128)S(1)} %copy-done.4, f32[2,256,128]{2,1,0:T(8,128)S(1)} %shard_map.79.after.first, f32[2,256,128]{2,1,0:T(8,128)S(1)} %shard_map.81.second, f32[4,256,128]{2,1,0:T(8,128)S(1)} %shard_map.80.after.far, ...), custom_call_target="tpu_custom_call" | custom-call | flops 4000000000 | bytes 4000000 | tf_op jit(solution)/shard_map/pallas_call | solution.py:359
  24.9 6.9 %collective-permute-done.5.far = f32[4,256,128]{2,1,0:T(8,128)S(1)} collective-permute-done((f32[4,256,128]{2,1,0:T(8,128)S(1)}, f32[4,256,128]{2,1,0:T(8,128)S(1)}, u32[]{:S(2)}, u32[]{:S(2)}) %collective-permute-start.5) | collective-permute-done | bytes 524320 | tf_op jit(solution)/shard_map/ppermute | solution.py:336
  31.8 0.4 shard_map.83
  32.2 5.7 %collective-permute-start.6 = (f32[2,128,128]{2,1,0:T(8,128)S(1)}, f32[2,128,128]{2,1,0:T(8,128)S(1)}, u32[]{:S(2)}, u32[]{:S(2)}) collective-permute-start(f32[2,128,128]{2,1,0:T(8,128)S(1)} %get-tuple-element.23), channel_id=1, source_target_pairs={{0,64},{64,0},{1,65},{65,1},{2,66},{66,2},{3,67},{67,3},{4,68},{68... | collective-permute-start | bytes 393224 | tf_op jit(solution)/shard_map/ppermute | solution.py:372
  37.9 1.0 collective-permute-done.6.other
  38.9 0.1 shard_map.85
  39.0 40.1 %all_to_all.10 = f32[256,1,128]{2,1,0:T(1,128)S(1)} all-to-all(f32[256,1,128]{2,1,0:T(1,128)S(1)} %bitcast.9), channel_id=1, replica_groups=mesh['zhi'=4,'core'=2,'zlo'=4,'x'=4,'y'=4] {'zlo','x','y','zhi'}, dimensions={0} | all-to-all | bytes 262144 | tf_op jit(solution)/shard_map/all_to_all | solution.py:382
  79.1 0.2 shard_map.86
  79.3 28.5 %all_to_all.11 = f32[256,2,128]{2,1,0:T(2,128)S(1)} all-to-all(f32[256,2,128]{2,1,0:T(2,128)S(1)} %bitcast.6), channel_id=1, replica_groups=mesh['zhi'=4,'core'=2,'zlo'=4,'x'=4,'y'=4] {'zlo','x','y','zhi'}, dimensions={0} | all-to-all | bytes 524288 | tf_op jit(solution)/shard_map/all_to_all | solution.py:386
  107.8 6.1 %collective-permute-start.7 = (f32[512,128]{1,0:T(8,128)S(1)}, f32[512,128]{1,0:T(8,128)S(1)}, u32[]{:S(2)}, u32[]{:S(2)}) collective-permute-start(f32[512,128]{1,0:T(8,128)S(1)} %bitcast.7), channel_id=1, source_target_pairs={{0,64},{64,0},{1,65},{65,1},{2,66},{66,2},{3,67},{67,3},{4,68},{68... | collective-permute-start | bytes 786440 | tf_op jit(solution)/shard_map/ppermute | solution.py:388
  113.9 1.0 shard_map.84
  114.9 0.1 collective-permute-done.7.other
  115.1 0.9 shard_map.87
  (15 shorter events, 0.1 us)
Async XLA Ops:
  0.6 1.2 %copy-start = (f32[1,4,2,256,128]{4,3,2,1,0:T(8,128)S(1)}, f32[1,4,2,256,128]{4,3,2,1,0:T(8,128)}, u32[]{:S(2)}) copy-start(f32[1,4,2,256,128]{4,3,2,1,0:T(8,128)} %adjoint.1) | copy-start | bytes 3145732
  1.9 8.8 %copy-start.1 = (f32[2,256,128]{2,1,0:T(8,128)S(1)}, f32[2,256,128]{2,1,0:T(8,128)}, u32[]{:S(2)}) copy-start(f32[2,256,128]{2,1,0:T(8,128)} %porosity.5) | copy-start | bytes 786436
  1.9 8.8 %copy-start.2 = (bf16[1,3,2,256,128]{4,3,2,1,0:T(8,128)(2,1)S(1)}, bf16[1,3,2,256,128]{4,3,2,1,0:T(8,128)(2,1)}, u32[]{:S(2)}) copy-start(bf16[1,3,2,256,128]{4,3,2,1,0:T(8,128)(2,1)} %vel.3) | copy-start | bytes 1179652
  1.9 8.8 %copy-start.3 = (s32[2,256,128]{2,1,0:T(8,128)S(1)}, s32[2,256,128]{2,1,0:T(8,128)}, u32[]{:S(2)}) copy-start(s32[2,256,128]{2,1,0:T(8,128)} %flags.3) | copy-start | bytes 786436
  1.9 9.7 %collective-permute-start = (f32[2,256,128]{2,1,0:T(8,128)S(1)}, f32[2,256,128]{2,1,0:T(8,128)S(1)}, u32[]{:S(2)}, u32[]{:S(2)}) collective-permute-start(f32[2,256,128]{2,1,0:T(8,128)S(1)} %get-tuple-element.13.first), channel_id=1, source_target_pairs={{1,2},{3,4},{5,6},{7,8},{9,10},{11,12},{13,14},{15,16},{17,18},{19... | collective-permute-start | bytes 786440 | tf_op jit(solution)/shard_map/ppermute | solution.py:336
  2.8 15.8 %collective-permute-start.2 = (f32[4,256,128]{2,1,0:T(8,128)S(1)}, f32[4,256,128]{2,1,0:T(8,128)S(1)}, u32[]{:S(2)}, u32[]{:S(2)}) collective-permute-start(f32[4,256,128]{2,1,0:T(8,128)S(1)} %get-tuple-element.15.far), channel_id=1, source_target_pairs={{0,1},{2,3},{4,5},{6,7},{8,9},{10,11},{12,13},{14,15},{16,17},{18,... | collective-permute-start | bytes 1572872 | tf_op jit(solution)/shard_map/ppermute | solution.py:336
  9.3 13.4 %collective-permute-start.1 = (f32[2,256,128]{2,1,0:T(8,128)S(1)}, f32[2,256,128]{2,1,0:T(8,128)S(1)}, u32[]{:S(2)}, u32[]{:S(2)}) collective-permute-start(f32[2,256,128]{2,1,0:T(8,128)S(1)} %get-tuple-element.14.second), channel_id=1, source_target_pairs={{1,2},{3,4},{5,6},{7,8},{9,10},{11,12},{13,14},{15,16},{17,18},{19... | collective-permute-start | bytes 786440 | tf_op jit(solution)/shard_map/ppermute | solution.py:336
  11.7 13.3 %collective-permute-start.3 = (f32[2,256,128]{2,1,0:T(8,128)S(1)}, f32[2,256,128]{2,1,0:T(8,128)S(1)}, u32[]{:S(2)}, u32[]{:S(2)}) collective-permute-start(f32[2,256,128]{2,1,0:T(8,128)S(1)} %shard_map.79.after.first), channel_id=1, source_target_pairs={{1,2},{3,4},{5,6},{7,8},{9,10},{11,12},{13,14},{15,16},{17,18},{19... | collective-permute-start | bytes 786440 | tf_op jit(solution)/shard_map/ppermute | solution.py:336
  18.6 4.9 %copy-start.4 = (s32[8]{0:T(128)S(1)}, s32[8]{0:T(128)}, u32[]{:S(2)}) copy-start(s32[8]{0:T(128)} %weights.1) | copy-start | bytes 100
  18.6 13.2 %collective-permute-start.5 = (f32[4,256,128]{2,1,0:T(8,128)S(1)}, f32[4,256,128]{2,1,0:T(8,128)S(1)}, u32[]{:S(2)}, u32[]{:S(2)}) collective-permute-start(f32[4,256,128]{2,1,0:T(8,128)S(1)} %shard_map.80.after.far), channel_id=1, source_target_pairs={{0,1},{2,3},{4,5},{6,7},{8,9},{10,11},{12,13},{14,15},{16,17},{18,... | collective-permute-start | bytes 1572872 | tf_op jit(solution)/shard_map/ppermute | solution.py:336
  22.8 2.1 %collective-permute-start.4 = (f32[2,256,128]{2,1,0:T(8,128)S(1)}, f32[2,256,128]{2,1,0:T(8,128)S(1)}, u32[]{:S(2)}, u32[]{:S(2)}) collective-permute-start(f32[2,256,128]{2,1,0:T(8,128)S(1)} %shard_map.81.second), channel_id=1, source_target_pairs={{1,2},{3,4},{5,6},{7,8},{9,10},{11,12},{13,14},{15,16},{17,18},{19... | collective-permute-start | bytes 786440 | tf_op jit(solution)/shard_map/ppermute | solution.py:336
  32.2 6.7 %collective-permute-start.6 = (f32[2,128,128]{2,1,0:T(8,128)S(1)}, f32[2,128,128]{2,1,0:T(8,128)S(1)}, u32[]{:S(2)}, u32[]{:S(2)}) collective-permute-start(f32[2,128,128]{2,1,0:T(8,128)S(1)} %get-tuple-element.23), channel_id=1, source_target_pairs={{0,64},{64,0},{1,65},{65,1},{2,66},{66,2},{3,67},{67,3},{4,68},{68... | collective-permute-start | bytes 393224 | tf_op jit(solution)/shard_map/ppermute | solution.py:372
  107.8 7.2 %collective-permute-start.7 = (f32[512,128]{1,0:T(8,128)S(1)}, f32[512,128]{1,0:T(8,128)S(1)}, u32[]{:S(2)}, u32[]{:S(2)}) collective-permute-start(f32[512,128]{1,0:T(8,128)S(1)} %bitcast.7), channel_id=1, source_target_pairs={{0,64},{64,0},{1,65},{65,1},{2,66},{66,2},{3,67},{67,3},{4,68},{68... | collective-permute-start | bytes 786440 | tf_op jit(solution)/shard_map/ppermute | solution.py:388

commit v6 on v5

--- a/solution.py
+++ b/solution.py
@@ -300,7 +300,7 @@
     above = jnp.where(at == slabs - 1, 0.0, pltpu.roll(swapped, slabs - 1, 0))
     plane = 2 * at + jnp.where(left, 0, 1)
     filtered = (2.0 * total + swapped + jnp.where(left, below, above)) / counts(plane, 2 * slabs)
-    largest = jnp.full(total.shape, jnp.max(jnp.abs(filtered)), F32)
+    largest = jnp.broadcast_to(jnp.max(jnp.abs(filtered), axis=0, keepdims=True), total.shape)
     for q in range(points):
         out[pl.ds(2 * q, slabs, stride=2 * points)] = filtered
         out[pl.ds(2 * q + 1, slabs, stride=2 * points)] = largest
@@ -310,8 +310,8 @@
     n = own.shape[0] // 2
     half = n // 2
     ends = [ref[pl.ds(1, n, stride=2)] for ref in (own, other)]
-    largest = jnp.max(jnp.maximum(ends[0], ends[1]))
-    factor = STEP / jnp.full((1, 128), largest + EPS, F32)
+    largest = jnp.max(jnp.maximum(ends[0], ends[1]), axis=0, keepdims=True)
+    factor = STEP / (jnp.max(largest, axis=1, keepdims=True) + EPS)
     core = lax.axis_index("core")
     for held, base in ((own, core * half), (other, half - core * half)):
         for r in range(0, half, CHUNK):

time: 116 us -> 116 us (level)
  no operation moved by 1% of the time
where the time goes in v6:
time: 116 us
  blocking collectives  68.6 us (59%)
  starting transfers between devices  25.3 us (22%)
  waiting for transfers between devices  14.2 us (12%)
  Pallas kernels  4.98 us (4%)
  between operations  1.49 us (1%)
  local copies, waits for them, and re-layouts  1.24 us (1%)
    all_to_all x1, blocking collectives, shards(): lax.all_to_all(blocks.reshape(group, 1, depth), SPACE + ('zhi',), 0, 0, t...  40.1 us
    all_to_all x1, blocking collectives, shards(): lax.all_to_all(copies.reshape(group, 2, depth), SPACE + ('zhi',), 0, 0, t...  28.5 us
    ppermute x6, starting transfers between devices, swap(): return lax.ppermute(value, SPACE, pairs(start))  13.5 us
    ppermute x6, waiting for transfers between devices, swap(): return lax.ppermute(value, SPACE, pairs(start))  13.1 us
    ppermute x1, starting transfers between devices, shards(): other = lax.ppermute(own, 'core', [(0, 1), (1, 0)])  6.09 us
    ppermute x1, starting transfers between devices, shards(): other = lax.ppermute(theirs, 'core', [(0, 1), (1, 0)])  5.71 us
  transfers between devices with their start and end apart: 8, of which 4 were waited for; matrix products, arithmetic and copies ran while one was open for 0% of the time, Pallas kernels for 3%

profile of v6, /device:TPU:1, one launch (start us, length us, event | category | flops | bytes accessed | tf_op | source)
XLA Modules:
  0.0 115.8 jit_solution(2482431051903608944)
XLA Ops:
  0.6 1.2 %copy-done = f32[1,4,2,256,128]{4,3,2,1,0:T(8,128)S(1)} copy-done((f32[1,4,2,256,128]{4,3,2,1,0:T(8,128)S(1)}, f32[1,4,2,256,128]{4,3,2,1,0:T(8,128)}, u32[]{:S(2)}) %copy-start) | copy-done | bytes 1048600
  1.9 0.1 shard_map.77
  1.9 0.8 collective-permute-start
  2.8 6.6 %collective-permute-start.2 = (f32[4,256,128]{2,1,0:T(8,128)S(1)}, f32[4,256,128]{2,1,0:T(8,128)S(1)}, u32[]{:S(2)}, u32[]{:S(2)}) collective-permute-start(f32[4,256,128]{2,1,0:T(8,128)S(1)} %get-tuple-element.15.far), channel_id=1, source_target_pairs={{0,1},{2,3},{4,5},{6,7},{8,9},{10,11},{12,13},{14,15},{16,17},{18,... | collective-permute-start | bytes 1572872 | tf_op jit(solution)/shard_map/ppermute | solution.py:336
  9.3 0.7 collective-permute-start.1
  10.7 0.9 shard_map.78
  11.7 0.7 collective-permute-start.3
  12.3 6.2 %collective-permute-done.2.halo = f32[4,256,128]{2,1,0:T(8,128)S(1)} collective-permute-done((f32[4,256,128]{2,1,0:T(8,128)S(1)}, f32[4,256,128]{2,1,0:T(8,128)S(1)}, u32[]{:S(2)}, u32[]{:S(2)}) %collective-permute-start.2) | collective-permute-done | bytes 524320 | tf_op jit(solution)/shard_map/ppermute | solution.py:336
  18.6 0.1 shard_map.80.after.far
  18.6 4.1 %collective-permute-start.5 = (f32[4,256,128]{2,1,0:T(8,128)S(1)}, f32[4,256,128]{2,1,0:T(8,128)S(1)}, u32[]{:S(2)}, u32[]{:S(2)}) collective-permute-start(f32[4,256,128]{2,1,0:T(8,128)S(1)} %shard_map.80.after.far), channel_id=1, source_target_pairs={{0,1},{2,3},{4,5},{6,7},{8,9},{10,11},{12,13},{14,15},{16,17},{18,... | collective-permute-start | bytes 1572872 | tf_op jit(solution)/shard_map/ppermute | solution.py:336
  22.8 0.7 collective-permute-start.4
  23.5 1.4 %shard_map.82 = (f32[4,2,256,128]{3,2,1,0:T(8,128)S(1)}, f32[3,2,256,128]{3,2,1,0:T(8,128)S(1)}) custom-call(f32[1]{0:T(128)S(6)} %copy.9.reynolds, s32[8]{0:T(128)S(1)} %copy-done.4, f32[2,256,128]{2,1,0:T(8,128)S(1)} %shard_map.79.after.first, f32[2,256,128]{2,1,0:T(8,128)S(1)} %shard_map.81.second, f32[4,256,128]{2,1,0:T(8,128)S(1)} %shard_map.80.after.far, ...), custom_call_target="tpu_custom_call" | custom-call | flops 4000000000 | bytes 4000000 | tf_op jit(solution)/shard_map/pallas_call | solution.py:359
  24.9 6.9 %collective-permute-done.5.far = f32[4,256,128]{2,1,0:T(8,128)S(1)} collective-permute-done((f32[4,256,128]{2,1,0:T(8,128)S(1)}, f32[4,256,128]{2,1,0:T(8,128)S(1)}, u32[]{:S(2)}, u32[]{:S(2)}) %collective-permute-start.5) | collective-permute-done | bytes 524320 | tf_op jit(solution)/shard_map/ppermute | solution.py:336
  31.8 0.4 shard_map.83
  32.2 5.7 %collective-permute-start.6 = (f32[2,128,128]{2,1,0:T(8,128)S(1)}, f32[2,128,128]{2,1,0:T(8,128)S(1)}, u32[]{:S(2)}, u32[]{:S(2)}) collective-permute-start(f32[2,128,128]{2,1,0:T(8,128)S(1)} %get-tuple-element.23), channel_id=1, source_target_pairs={{0,64},{64,0},{1,65},{65,1},{2,66},{66,2},{3,67},{67,3},{4,68},{68... | collective-permute-start | bytes 393224 | tf_op jit(solution)/shard_map/ppermute | solution.py:372
  37.9 1.0 collective-permute-done.6.other
  38.9 0.1 shard_map.85
  39.0 40.1 %all_to_all.10 = f32[256,1,128]{2,1,0:T(1,128)S(1)} all-to-all(f32[256,1,128]{2,1,0:T(1,128)S(1)} %bitcast.9), channel_id=1, replica_groups=mesh['zhi'=4,'core'=2,'zlo'=4,'x'=4,'y'=4] {'zlo','x','y','zhi'}, dimensions={0} | all-to-all | bytes 262144 | tf_op jit(solution)/shard_map/all_to_all | solution.py:382
  79.1 0.1 shard_map.86
  79.2 28.5 %all_to_all.11 = f32[256,2,128]{2,1,0:T(2,128)S(1)} all-to-all(f32[256,2,128]{2,1,0:T(2,128)S(1)} %bitcast.6), channel_id=1, replica_groups=mesh['zhi'=4,'core'=2,'zlo'=4,'x'=4,'y'=4] {'zlo','x','y','zhi'}, dimensions={0} | all-to-all | bytes 524288 | tf_op jit(solution)/shard_map/all_to_all | solution.py:386
  107.7 6.1 %collective-permute-start.7 = (f32[512,128]{1,0:T(8,128)S(1)}, f32[512,128]{1,0:T(8,128)S(1)}, u32[]{:S(2)}, u32[]{:S(2)}) collective-permute-start(f32[512,128]{1,0:T(8,128)S(1)} %bitcast.7), channel_id=1, source_target_pairs={{0,64},{64,0},{1,65},{65,1},{2,66},{66,2},{3,67},{67,3},{4,68},{68... | collective-permute-start | bytes 786440 | tf_op jit(solution)/shard_map/ppermute | solution.py:388
  113.8 1.0 shard_map.84
  114.8 0.1 collective-permute-done.7.other
  115.0 0.9 shard_map.87
  (15 shorter events, 0.1 us)
Async XLA Ops:
  0.6 1.2 %copy-start = (f32[1,4,2,256,128]{4,3,2,1,0:T(8,128)S(1)}, f32[1,4,2,256,128]{4,3,2,1,0:T(8,128)}, u32[]{:S(2)}) copy-start(f32[1,4,2,256,128]{4,3,2,1,0:T(8,128)} %adjoint.1) | copy-start | bytes 3145732
  1.9 8.8 %copy-start.1 = (f32[2,256,128]{2,1,0:T(8,128)S(1)}, f32[2,256,128]{2,1,0:T(8,128)}, u32[]{:S(2)}) copy-start(f32[2,256,128]{2,1,0:T(8,128)} %porosity.5) | copy-start | bytes 786436
  1.9 8.8 %copy-start.2 = (bf16[1,3,2,256,128]{4,3,2,1,0:T(8,128)(2,1)S(1)}, bf16[1,3,2,256,128]{4,3,2,1,0:T(8,128)(2,1)}, u32[]{:S(2)}) copy-start(bf16[1,3,2,256,128]{4,3,2,1,0:T(8,128)(2,1)} %vel.3) | copy-start | bytes 1179652
  1.9 8.8 %copy-start.3 = (s32[2,256,128]{2,1,0:T(8,128)S(1)}, s32[2,256,128]{2,1,0:T(8,128)}, u32[]{:S(2)}) copy-start(s32[2,256,128]{2,1,0:T(8,128)} %flags.3) | copy-start | bytes 786436
  1.9 9.7 %collective-permute-start = (f32[2,256,128]{2,1,0:T(8,128)S(1)}, f32[2,256,128]{2,1,0:T(8,128)S(1)}, u32[]{:S(2)}, u32[]{:S(2)}) collective-permute-start(f32[2,256,128]{2,1,0:T(8,128)S(1)} %get-tuple-element.13.first), channel_id=1, source_target_pairs={{1,2},{3,4},{5,6},{7,8},{9,10},{11,12},{13,14},{15,16},{17,18},{19... | collective-permute-start | bytes 786440 | tf_op jit(solution)/shard_map/ppermute | solution.py:336
  2.8 15.8 %collective-permute-start.2 = (f32[4,256,128]{2,1,0:T(8,128)S(1)}, f32[4,256,128]{2,1,0:T(8,128)S(1)}, u32[]{:S(2)}, u32[]{:S(2)}) collective-permute-start(f32[4,256,128]{2,1,0:T(8,128)S(1)} %get-tuple-element.15.far), channel_id=1, source_target_pairs={{0,1},{2,3},{4,5},{6,7},{8,9},{10,11},{12,13},{14,15},{16,17},{18,... | collective-permute-start | bytes 1572872 | tf_op jit(solution)/shard_map/ppermute | solution.py:336
  9.3 13.4 %collective-permute-start.1 = (f32[2,256,128]{2,1,0:T(8,128)S(1)}, f32[2,256,128]{2,1,0:T(8,128)S(1)}, u32[]{:S(2)}, u32[]{:S(2)}) collective-permute-start(f32[2,256,128]{2,1,0:T(8,128)S(1)} %get-tuple-element.14.second), channel_id=1, source_target_pairs={{1,2},{3,4},{5,6},{7,8},{9,10},{11,12},{13,14},{15,16},{17,18},{19... | collective-permute-start | bytes 786440 | tf_op jit(solution)/shard_map/ppermute | solution.py:336
  11.7 13.3 %collective-permute-start.3 = (f32[2,256,128]{2,1,0:T(8,128)S(1)}, f32[2,256,128]{2,1,0:T(8,128)S(1)}, u32[]{:S(2)}, u32[]{:S(2)}) collective-permute-start(f32[2,256,128]{2,1,0:T(8,128)S(1)} %shard_map.79.after.first), channel_id=1, source_target_pairs={{1,2},{3,4},{5,6},{7,8},{9,10},{11,12},{13,14},{15,16},{17,18},{19... | collective-permute-start | bytes 786440 | tf_op jit(solution)/shard_map/ppermute | solution.py:336
  18.6 4.9 %copy-start.4 = (s32[8]{0:T(128)S(1)}, s32[8]{0:T(128)}, u32[]{:S(2)}) copy-start(s32[8]{0:T(128)} %weights.1) | copy-start | bytes 100
  18.6 13.2 %collective-permute-start.5 = (f32[4,256,128]{2,1,0:T(8,128)S(1)}, f32[4,256,128]{2,1,0:T(8,128)S(1)}, u32[]{:S(2)}, u32[]{:S(2)}) collective-permute-start(f32[4,256,128]{2,1,0:T(8,128)S(1)} %shard_map.80.after.far), channel_id=1, source_target_pairs={{0,1},{2,3},{4,5},{6,7},{8,9},{10,11},{12,13},{14,15},{16,17},{18,... | collective-permute-start | bytes 1572872 | tf_op jit(solution)/shard_map/ppermute | solution.py:336
  22.8 2.1 %collective-permute-start.4 = (f32[2,256,128]{2,1,0:T(8,128)S(1)}, f32[2,256,128]{2,1,0:T(8,128)S(1)}, u32[]{:S(2)}, u32[]{:S(2)}) collective-permute-start(f32[2,256,128]{2,1,0:T(8,128)S(1)} %shard_map.81.second), channel_id=1, source_target_pairs={{1,2},{3,4},{5,6},{7,8},{9,10},{11,12},{13,14},{15,16},{17,18},{19... | collective-permute-start | bytes 786440 | tf_op jit(solution)/shard_map/ppermute | solution.py:336
  32.2 6.7 %collective-permute-start.6 = (f32[2,128,128]{2,1,0:T(8,128)S(1)}, f32[2,128,128]{2,1,0:T(8,128)S(1)}, u32[]{:S(2)}, u32[]{:S(2)}) collective-permute-start(f32[2,128,128]{2,1,0:T(8,128)S(1)} %get-tuple-element.23), channel_id=1, source_target_pairs={{0,64},{64,0},{1,65},{65,1},{2,66},{66,2},{3,67},{67,3},{4,68},{68... | collective-permute-start | bytes 393224 | tf_op jit(solution)/shard_map/ppermute | solution.py:372
  107.7 7.2 %collective-permute-start.7 = (f32[512,128]{1,0:T(8,128)S(1)}, f32[512,128]{1,0:T(8,128)S(1)}, u32[]{:S(2)}, u32[]{:S(2)}) collective-permute-start(f32[512,128]{1,0:T(8,128)S(1)} %bitcast.7), channel_id=1, source_target_pairs={{0,64},{64,0},{1,65},{65,1},{2,66},{66,2},{3,67},{67,3},{4,68},{68... | collective-permute-start | bytes 786440 | tf_op jit(solution)/shard_map/ppermute | solution.py:388

commit v7 on v6

--- a/solution.py
+++ b/solution.py
@@ -76,18 +76,6 @@
         return first[min(c, 1), r : r + n]
 
     return read
-
-
-def take_planes(adjoint, first, second, far):
-    index, _ = side(0)
-    for r in range(0, far.shape[1], CHUNK):
-        now = slice(r, r + CHUNK)
-        first[0, now] = adjoint[0, 0, index, now]
-        first[1, now] = adjoint[0, 3, index, now]
-        for c in range(2):
-            second[c, now] = adjoint[0, c + 1, index, now]
-        for c in range(4):
-            far[c, now] = adjoint[0, c, 1 - index, now]
 
 
 def local_chunk(read, p, sign, r, size, rows, u, nu, scale, drive):
@@ -339,11 +327,11 @@
     field = shape(planes, rows, depth)
     plane = shape(4, rows, depth)
     pair = shape(2, rows, depth)
-    first, second, far = call(
-        take_planes,
-        [VM],
-        [pair, pair, plane],
-    )(adjoint)
+    place = (lax.axis_index("zlo") * lax.axis_size("x") + lax.axis_index("x")) * lax.axis_size("y")
+    odd = lax.rem(place + lax.axis_index("y"), 2)
+    near = lax.dynamic_index_in_dim(adjoint[0], odd, 1, keepdims=False)
+    first, second = near[0::3], near[1:3]
+    far = lax.dynamic_index_in_dim(adjoint[0], 1 - odd, 1, keepdims=False)
     halo_first = swap(first, 1)
     halo_far = swap(far, 0)
     halo_second = swap(second, 1)

time: 116 us -> 116 us (level)
    squeeze x0 -> x1, local copies, waits for them, and re-layouts: none -> 1.36 us  [shards(): far = lax.dynamic_index_in_dim(adjoint[0], 1 - odd, 1, keepdims=False)]
    unnamed x10 -> x8, local copies, waits for them, and re-layouts: 1.24 us -> 0.03 us
where the time goes in v7:
time: 116 us
  blocking collectives  68.5 us (59%)
  starting transfers between devices  25.4 us (22%)
  waiting for transfers between devices  14 us (12%)
  Pallas kernels  4.96 us (4%)
  between operations  1.54 us (1%)
  local copies, waits for them, and re-layouts  1.42 us (1%)
    all_to_all x1, blocking collectives, shards(): lax.all_to_all(blocks.reshape(group, 1, depth), SPACE + ('zhi',), 0, 0, t...  40 us
    all_to_all x1, blocking collectives, shards(): lax.all_to_all(copies.reshape(group, 2, depth), SPACE + ('zhi',), 0, 0, t...  28.5 us
    ppermute x6, starting transfers between devices, swap(): return lax.ppermute(value, SPACE, pairs(start))  13.6 us
    ppermute x6, waiting for transfers between devices, swap(): return lax.ppermute(value, SPACE, pairs(start))  12.9 us
    ppermute x1, starting transfers between devices, shards(): other = lax.ppermute(own, 'core', [(0, 1), (1, 0)])  6.09 us
    ppermute x1, starting transfers between devices, shards(): other = lax.ppermute(theirs, 'core', [(0, 1), (1, 0)])  5.71 us
  transfers between devices with their start and end apart: 8, of which 4 were waited for; matrix products, arithmetic and copies ran while one was open for 0% of the time, Pallas kernels for 3%

profile of v7, /device:TPU:1, one launch (start us, length us, event | category | flops | bytes accessed | tf_op | source)
XLA Modules:
  0.0 115.8 jit_solution(4474626280243042777)
XLA Ops:
  0.6 1.4 %dynamic-slice_bitcast_fusion = (f32[4,256,128]{2,1,0:T(8,128)S(1)}, f32[4,256,128]{2,1,0:T(8,128)S(1)}, f32[1,4,1,256,128]{4,3,1,2,0:T(8,128)S(1)}) fusion(f32[1,4,2,256,128]{4,3,2,1,0:T(8,128)} %param.6, s32[]{:T(128)S(6)} %select_n.8, s32[]{:T(128)S(6)} %select_n.7), kind=kLoop, calls=%fused_computation | loop fusion | bytes 2621448 | tf_op jit(solution)/shard_map/jit(dynamic_index_in_dim)/squeeze | solution.py:334
  2.0 0.0 copy-start.1
  2.0 0.8 collective-permute-start
  2.9 6.6 %collective-permute-start.2 = (f32[4,256,128]{2,1,0:T(8,128)S(1)}, f32[4,256,128]{2,1,0:T(8,128)S(1)}, u32[]{:S(2)}, u32[]{:S(2)}) collective-permute-start(f32[4,256,128]{2,1,0:T(8,128)S(1)} %get-tuple-element.18.far), channel_id=1, source_target_pairs={{0,1},{2,3},{4,5},{6,7},{8,9},{10,11},{12,13},{14,15},{16,17},{18,... | collective-permute-start | bytes 1572872 | tf_op jit(solution)/shard_map/ppermute | solution.py:324
  9.5 0.8 collective-permute-start.1
  11.0 0.9 shard_map.77
  12.0 0.7 collective-permute-start.3
  12.6 6.0 %collective-permute-done.2.halo = f32[4,256,128]{2,1,0:T(8,128)S(1)} collective-permute-done((f32[4,256,128]{2,1,0:T(8,128)S(1)}, f32[4,256,128]{2,1,0:T(8,128)S(1)}, u32[]{:S(2)}, u32[]{:S(2)}) %collective-permute-start.2) | collective-permute-done | bytes 524320 | tf_op jit(solution)/shard_map/ppermute | solution.py:324
  18.7 0.1 shard_map.79.after.far
  18.7 4.1 %collective-permute-start.5 = (f32[4,256,128]{2,1,0:T(8,128)S(1)}, f32[4,256,128]{2,1,0:T(8,128)S(1)}, u32[]{:S(2)}, u32[]{:S(2)}) collective-permute-start(f32[4,256,128]{2,1,0:T(8,128)S(1)} %shard_map.79.after.far), channel_id=1, source_target_pairs={{0,1},{2,3},{4,5},{6,7},{8,9},{10,11},{12,13},{14,15},{16,17},{18,... | collective-permute-start | bytes 1572872 | tf_op jit(solution)/shard_map/ppermute | solution.py:324
  22.9 0.7 collective-permute-start.4
  23.6 1.5 %shard_map.81 = (f32[4,2,256,128]{3,2,1,0:T(8,128)S(1)}, f32[3,2,256,128]{3,2,1,0:T(8,128)S(1)}) custom-call(f32[1]{0:T(128)S(6)} %copy.12.reynolds, s32[8]{0:T(128)S(1)} %copy-done.3, f32[2,256,128]{2,1,0:T(8,128)S(1)} %shard_map.78.after.first, f32[2,256,128]{2,1,0:T(8,128)S(1)} %shard_map.80.second, f32[4,256,128]{2,1,0:T(8,128)S(1)} %shard_map.79.after.far, ...), custom_call_target="tpu_custom_call" | custom-call | flops 4000000000 | bytes 4000000 | tf_op jit(solution)/shard_map/pallas_call | solution.py:347
  25.1 6.8 %collective-permute-done.5.far = f32[4,256,128]{2,1,0:T(8,128)S(1)} collective-permute-done((f32[4,256,128]{2,1,0:T(8,128)S(1)}, f32[4,256,128]{2,1,0:T(8,128)S(1)}, u32[]{:S(2)}, u32[]{:S(2)}) %collective-permute-start.5) | collective-permute-done | bytes 524320 | tf_op jit(solution)/shard_map/ppermute | solution.py:324
  31.9 0.4 shard_map.82
  32.3 5.7 %collective-permute-start.6 = (f32[2,128,128]{2,1,0:T(8,128)S(1)}, f32[2,128,128]{2,1,0:T(8,128)S(1)}, u32[]{:S(2)}, u32[]{:S(2)}) collective-permute-start(f32[2,128,128]{2,1,0:T(8,128)S(1)} %get-tuple-element.17), channel_id=1, source_target_pairs={{0,64},{64,0},{1,65},{65,1},{2,66},{66,2},{3,67},{67,3},{4,68},{68... | collective-permute-start | bytes 393224 | tf_op jit(solution)/shard_map/ppermute | solution.py:360
  38.0 1.0 collective-permute-done.6.other
  39.0 0.1 shard_map.84
  39.1 40.0 %all_to_all.10 = f32[256,1,128]{2,1,0:T(1,128)S(1)} all-to-all(f32[256,1,128]{2,1,0:T(1,128)S(1)} %bitcast.18), channel_id=1, replica_groups=mesh['zhi'=4,'core'=2,'zlo'=4,'x'=4,'y'=4] {'zlo','x','y','zhi'}, dimensions={0} | all-to-all | bytes 262144 | tf_op jit(solution)/shard_map/all_to_all | solution.py:370
  79.1 0.1 shard_map.85
  79.2 28.5 %all_to_all.11 = f32[256,2,128]{2,1,0:T(2,128)S(1)} all-to-all(f32[256,2,128]{2,1,0:T(2,128)S(1)} %bitcast.15), channel_id=1, replica_groups=mesh['zhi'=4,'core'=2,'zlo'=4,'x'=4,'y'=4] {'zlo','x','y','zhi'}, dimensions={0} | all-to-all | bytes 524288 | tf_op jit(solution)/shard_map/all_to_all | solution.py:374
  107.7 6.1 %collective-permute-start.7 = (f32[512,128]{1,0:T(8,128)S(1)}, f32[512,128]{1,0:T(8,128)S(1)}, u32[]{:S(2)}, u32[]{:S(2)}) collective-permute-start(f32[512,128]{1,0:T(8,128)S(1)} %bitcast.16), channel_id=1, source_target_pairs={{0,64},{64,0},{1,65},{65,1},{2,66},{66,2},{3,67},{67,3},{4,68},{68... | collective-permute-start | bytes 786440 | tf_op jit(solution)/shard_map/ppermute | solution.py:376
  113.8 1.0 shard_map.83
  114.8 0.1 collective-permute-done.7.other
  115.0 0.9 shard_map.86
  (15 shorter events, 0.2 us)
Async XLA Ops:
  2.0 8.9 %copy-start.1 = (bf16[1,3,2,256,128]{4,3,2,1,0:T(8,128)(2,1)S(1)}, bf16[1,3,2,256,128]{4,3,2,1,0:T(8,128)(2,1)}, u32[]{:S(2)}) copy-start(bf16[1,3,2,256,128]{4,3,2,1,0:T(8,128)(2,1)} %vel.3) | copy-start | bytes 1179652
  2.0 9.8 %collective-permute-start = (f32[2,256,128]{2,1,0:T(8,128)S(1)}, f32[2,256,128]{2,1,0:T(8,128)S(1)}, u32[]{:S(2)}, u32[]{:S(2)}) collective-permute-start(f32[2,256,128]{2,1,0:T(8,128)S(1)} %slice.9.first), channel_id=1, source_target_pairs={{1,2},{3,4},{5,6},{7,8},{9,10},{11,12},{13,14},{15,16},{17,18},{19... | collective-permute-start | bytes 786440 | tf_op jit(solution)/shard_map/ppermute | solution.py:324
  2.9 15.8 %collective-permute-start.2 = (f32[4,256,128]{2,1,0:T(8,128)S(1)}, f32[4,256,128]{2,1,0:T(8,128)S(1)}, u32[]{:S(2)}, u32[]{:S(2)}) collective-permute-start(f32[4,256,128]{2,1,0:T(8,128)S(1)} %get-tuple-element.18.far), channel_id=1, source_target_pairs={{0,1},{2,3},{4,5},{6,7},{8,9},{10,11},{12,13},{14,15},{16,17},{18,... | collective-permute-start | bytes 1572872 | tf_op jit(solution)/shard_map/ppermute | solution.py:324
  9.4 1.5 %copy-start = (f32[2,256,128]{2,1,0:T(8,128)S(1)}, f32[2,256,128]{2,1,0:T(8,128)}, u32[]{:S(2)}) copy-start(f32[2,256,128]{2,1,0:T(8,128)} %porosity.5) | copy-start | bytes 786436
  9.4 1.5 %copy-start.2 = (s32[2,256,128]{2,1,0:T(8,128)S(1)}, s32[2,256,128]{2,1,0:T(8,128)}, u32[]{:S(2)}) copy-start(s32[2,256,128]{2,1,0:T(8,128)} %flags.3) | copy-start | bytes 786436
  9.5 13.4 %collective-permute-start.1 = (f32[2,256,128]{2,1,0:T(8,128)S(1)}, f32[2,256,128]{2,1,0:T(8,128)S(1)}, u32[]{:S(2)}, u32[]{:S(2)}) collective-permute-start(f32[2,256,128]{2,1,0:T(8,128)S(1)} %slice_bitcast_fusion.second), channel_id=1, source_target_pairs={{1,2},{3,4},{5,6},{7,8},{9,10},{11,12},{13,14},{15,16},{17,18},{19... | collective-permute-start | bytes 786440 | tf_op jit(solution)/shard_map/ppermute | solution.py:324
  12.0 13.1 %collective-permute-start.3 = (f32[2,256,128]{2,1,0:T(8,128)S(1)}, f32[2,256,128]{2,1,0:T(8,128)S(1)}, u32[]{:S(2)}, u32[]{:S(2)}) collective-permute-start(f32[2,256,128]{2,1,0:T(8,128)S(1)} %shard_map.78.after.first), channel_id=1, source_target_pairs={{1,2},{3,4},{5,6},{7,8},{9,10},{11,12},{13,14},{15,16},{17,18},{19... | collective-permute-start | bytes 786440 | tf_op jit(solution)/shard_map/ppermute | solution.py:324
  18.7 4.9 %copy-start.3 = (s32[8]{0:T(128)S(1)}, s32[8]{0:T(128)}, u32[]{:S(2)}) copy-start(s32[8]{0:T(128)} %weights.1) | copy-start | bytes 100
  18.7 13.2 %collective-permute-start.5 = (f32[4,256,128]{2,1,0:T(8,128)S(1)}, f32[4,256,128]{2,1,0:T(8,128)S(1)}, u32[]{:S(2)}, u32[]{:S(2)}) collective-permute-start(f32[4,256,128]{2,1,0:T(8,128)S(1)} %shard_map.79.after.far), channel_id=1, source_target_pairs={{0,1},{2,3},{4,5},{6,7},{8,9},{10,11},{12,13},{14,15},{16,17},{18,... | collective-permute-start | bytes 1572872 | tf_op jit(solution)/shard_map/ppermute | solution.py:324
  22.9 2.2 %collective-permute-start.4 = (f32[2,256,128]{2,1,0:T(8,128)S(1)}, f32[2,256,128]{2,1,0:T(8,128)S(1)}, u32[]{:S(2)}, u32[]{:S(2)}) collective-permute-start(f32[2,256,128]{2,1,0:T(8,128)S(1)} %shard_map.80.second), channel_id=1, source_target_pairs={{1,2},{3,4},{5,6},{7,8},{9,10},{11,12},{13,14},{15,16},{17,18},{19... | collective-permute-start | bytes 786440 | tf_op jit(solution)/shard_map/ppermute | solution.py:324
  32.3 6.7 %collective-permute-start.6 = (f32[2,128,128]{2,1,0:T(8,128)S(1)}, f32[2,128,128]{2,1,0:T(8,128)S(1)}, u32[]{:S(2)}, u32[]{:S(2)}) collective-permute-start(f32[2,128,128]{2,1,0:T(8,128)S(1)} %get-tuple-element.17), channel_id=1, source_target_pairs={{0,64},{64,0},{1,65},{65,1},{2,66},{66,2},{3,67},{67,3},{4,68},{68... | collective-permute-start | bytes 393224 | tf_op jit(solution)/shard_map/ppermute | solution.py:360
  107.7 7.2 %collective-permute-start.7 = (f32[512,128]{1,0:T(8,128)S(1)}, f32[512,128]{1,0:T(8,128)S(1)}, u32[]{:S(2)}, u32[]{:S(2)}) collective-permute-start(f32[512,128]{1,0:T(8,128)S(1)} %bitcast.16), channel_id=1, source_target_pairs={{0,64},{64,0},{1,65},{65,1},{2,66},{66,2},{3,67},{67,3},{4,68},{68... | collective-permute-start | bytes 786440 | tf_op jit(solution)/shard_map/ppermute | solution.py:376

commit v8 on v6

--- a/solution.py
+++ b/solution.py
@@ -251,9 +251,12 @@
 
         @pl.when(core == owner)
         def _():
-            for p in range(2):
-                mine[p] = weighted[p, kept : kept + half]
-                theirs[p] = weighted[p, sent : sent + half]
+            for out, base in ((mine, kept), (theirs, sent)):
+                for r in range(0, half, CHUNK):
+                    now = slice(base + r, base + r + CHUNK)
+                    out[r : r + CHUNK], out[half + r : half + r + CHUNK] = interleave(
+                        weighted[0, now], weighted[1, now]
+                    )
 
 
 def write_state(held, state, sems):
@@ -280,12 +283,9 @@
 
 
 def add_cores(mine, other, blocks):
-    half = mine.shape[1]
-    for r in range(0, half, CHUNK):
+    for r in range(0, blocks.shape[0], CHUNK):
         now = slice(r, r + CHUNK)
-        first, second = interleave(mine[0, now] + other[0, now], mine[1, now] + other[1, now])
-        blocks[now] = first
-        blocks[half + r : half + r + CHUNK] = second
+        blocks[now] = mine[now] + other[now]
 
 
 def filter_planes(points, blocks, out):
@@ -362,7 +362,7 @@
         [half_state, shape(3, planes, rows, depth)],
         flops=4000000000,
     )(reynolds, weights, first, second, far, fwd_velocity, porosity, flags, scaled)
-    half = shape(planes, rows // cores, depth)
+    half = shape(planes * rows // cores, depth)
     held, mine, theirs = call(
         second_join,
         [VM] * 7,

time: 116 us -> 116 us (level)
  no operation moved by 1% of the time
where the time goes in v8:
time: 116 us
  blocking collectives  68.6 us (59%)
  starting transfers between devices  25.3 us (22%)
  waiting for transfers between devices  14.2 us (12%)
  Pallas kernels  5.01 us (4%)
  between operations  1.49 us (1%)
  local copies, waits for them, and re-layouts  1.24 us (1%)
    all_to_all x1, blocking collectives, shards(): lax.all_to_all(blocks.reshape(group, 1, depth), SPACE + ('zhi',), 0, 0, t...  40.1 us
    all_to_all x1, blocking collectives, shards(): lax.all_to_all(copies.reshape(group, 2, depth), SPACE + ('zhi',), 0, 0, t...  28.5 us
    ppermute x6, starting transfers between devices, swap(): return lax.ppermute(value, SPACE, pairs(start))  13.5 us
    ppermute x6, waiting for transfers between devices, swap(): return lax.ppermute(value, SPACE, pairs(start))  13.1 us
    ppermute x1, starting transfers between devices, shards(): other = lax.ppermute(own, 'core', [(0, 1), (1, 0)])  6.09 us
    ppermute x1, starting transfers between devices, shards(): other = lax.ppermute(theirs, 'core', [(0, 1), (1, 0)])  5.71 us
  transfers between devices with their start and end apart: 8, of which 4 were waited for; matrix products, arithmetic and copies ran while one was open for 0% of the time, Pallas kernels for 3%

profile of v8, /device:TPU:1, one launch (start us, length us, event | category | flops | bytes accessed | tf_op | source)
XLA Modules:
  0.0 115.9 jit_solution(13634493980306692654)
XLA Ops:
  0.6 1.2 %copy-done = f32[1,4,2,256,128]{4,3,2,1,0:T(8,128)S(1)} copy-done((f32[1,4,2,256,128]{4,3,2,1,0:T(8,128)S(1)}, f32[1,4,2,256,128]{4,3,2,1,0:T(8,128)}, u32[]{:S(2)}) %copy-start) | copy-done | bytes 1048600
  1.9 0.1 shard_map.77
  1.9 0.8 collective-permute-start
  2.8 6.6 %collective-permute-start.2 = (f32[4,256,128]{2,1,0:T(8,128)S(1)}, f32[4,256,128]{2,1,0:T(8,128)S(1)}, u32[]{:S(2)}, u32[]{:S(2)}) collective-permute-start(f32[4,256,128]{2,1,0:T(8,128)S(1)} %get-tuple-element.15.far), channel_id=1, source_target_pairs={{0,1},{2,3},{4,5},{6,7},{8,9},{10,11},{12,13},{14,15},{16,17},{18,... | collective-permute-start | bytes 1572872 | tf_op jit(solution)/shard_map/ppermute | solution.py:336
  9.3 0.7 collective-permute-start.1
  10.7 0.9 shard_map.78
  11.7 0.7 collective-permute-start.3
  12.3 6.2 %collective-permute-done.2.halo = f32[4,256,128]{2,1,0:T(8,128)S(1)} collective-permute-done((f32[4,256,128]{2,1,0:T(8,128)S(1)}, f32[4,256,128]{2,1,0:T(8,128)S(1)}, u32[]{:S(2)}, u32[]{:S(2)}) %collective-permute-start.2) | collective-permute-done | bytes 524320 | tf_op jit(solution)/shard_map/ppermute | solution.py:336
  18.6 0.1 shard_map.80.after.far
  18.6 0.0 copy-start.4
  18.6 4.1 %collective-permute-start.5 = (f32[4,256,128]{2,1,0:T(8,128)S(1)}, f32[4,256,128]{2,1,0:T(8,128)S(1)}, u32[]{:S(2)}, u32[]{:S(2)}) collective-permute-start(f32[4,256,128]{2,1,0:T(8,128)S(1)} %shard_map.80.after.far), channel_id=1, source_target_pairs={{0,1},{2,3},{4,5},{6,7},{8,9},{10,11},{12,13},{14,15},{16,17},{18,... | collective-permute-start | bytes 1572872 | tf_op jit(solution)/shard_map/ppermute | solution.py:336
  22.8 0.7 collective-permute-start.4
  23.5 1.4 %shard_map.82 = (f32[4,2,256,128]{3,2,1,0:T(8,128)S(1)}, f32[3,2,256,128]{3,2,1,0:T(8,128)S(1)}) custom-call(f32[1]{0:T(128)S(6)} %copy.9.reynolds, s32[8]{0:T(128)S(1)} %copy-done.4, f32[2,256,128]{2,1,0:T(8,128)S(1)} %shard_map.79.after.first, f32[2,256,128]{2,1,0:T(8,128)S(1)} %shard_map.81.second, f32[4,256,128]{2,1,0:T(8,128)S(1)} %shard_map.80.after.far, ...), custom_call_target="tpu_custom_call" | custom-call | flops 4000000000 | bytes 4000000 | tf_op jit(solution)/shard_map/pallas_call | solution.py:359
  24.9 6.9 %collective-permute-done.5.far = f32[4,256,128]{2,1,0:T(8,128)S(1)} collective-permute-done((f32[4,256,128]{2,1,0:T(8,128)S(1)}, f32[4,256,128]{2,1,0:T(8,128)S(1)}, u32[]{:S(2)}, u32[]{:S(2)}) %collective-permute-start.5) | collective-permute-done | bytes 524320 | tf_op jit(solution)/shard_map/ppermute | solution.py:336
  31.8 0.5 shard_map.83
  32.3 5.7 %collective-permute-start.6 = (f32[256,128]{1,0:T(8,128)S(1)}, f32[256,128]{1,0:T(8,128)S(1)}, u32[]{:S(2)}, u32[]{:S(2)}) collective-permute-start(f32[256,128]{1,0:T(8,128)S(1)} %get-tuple-element.23), channel_id=1, source_target_pairs={{0,64},{64,0},{1,65},{65,1},{2,66},{66,2},{3,67},{67,3},{4,68},{68... | collective-permute-start | bytes 393224 | tf_op jit(solution)/shard_map/ppermute | solution.py:372
  38.0 1.0 collective-permute-done.6.other
  39.0 40.1 %all_to_all.10 = f32[256,1,128]{2,1,0:T(1,128)S(1)} all-to-all(f32[256,1,128]{2,1,0:T(1,128)S(1)} %bitcast.9), channel_id=1, replica_groups=mesh['zhi'=4,'core'=2,'zlo'=4,'x'=4,'y'=4] {'zlo','x','y','zhi'}, dimensions={0} | all-to-all | bytes 262144 | tf_op jit(solution)/shard_map/all_to_all | solution.py:382
  79.1 0.1 shard_map.86
  79.2 28.5 %all_to_all.11 = f32[256,2,128]{2,1,0:T(2,128)S(1)} all-to-all(f32[256,2,128]{2,1,0:T(2,128)S(1)} %bitcast.6), channel_id=1, replica_groups=mesh['zhi'=4,'core'=2,'zlo'=4,'x'=4,'y'=4] {'zlo','x','y','zhi'}, dimensions={0} | all-to-all | bytes 524288 | tf_op jit(solution)/shard_map/all_to_all | solution.py:386
  107.8 6.1 %collective-permute-start.7 = (f32[512,128]{1,0:T(8,128)S(1)}, f32[512,128]{1,0:T(8,128)S(1)}, u32[]{:S(2)}, u32[]{:S(2)}) collective-permute-start(f32[512,128]{1,0:T(8,128)S(1)} %bitcast.7), channel_id=1, source_target_pairs={{0,64},{64,0},{1,65},{65,1},{2,66},{66,2},{3,67},{67,3},{4,68},{68... | collective-permute-start | bytes 786440 | tf_op jit(solution)/shard_map/ppermute | solution.py:388
  113.9 1.0 shard_map.84
  114.9 0.1 collective-permute-done.7.other
  115.0 0.9 shard_map.87
  (15 shorter events, 0.1 us)
Async XLA Ops:
  0.6 1.2 %copy-start = (f32[1,4,2,256,128]{4,3,2,1,0:T(8,128)S(1)}, f32[1,4,2,256,128]{4,3,2,1,0:T(8,128)}, u32[]{:S(2)}) copy-start(f32[1,4,2,256,128]{4,3,2,1,0:T(8,128)} %adjoint.1) | copy-start | bytes 3145732
  1.9 8.8 %copy-start.1 = (f32[2,256,128]{2,1,0:T(8,128)S(1)}, f32[2,256,128]{2,1,0:T(8,128)}, u32[]{:S(2)}) copy-start(f32[2,256,128]{2,1,0:T(8,128)} %porosity.5) | copy-start | bytes 786436
  1.9 8.8 %copy-start.2 = (bf16[1,3,2,256,128]{4,3,2,1,0:T(8,128)(2,1)S(1)}, bf16[1,3,2,256,128]{4,3,2,1,0:T(8,128)(2,1)}, u32[]{:S(2)}) copy-start(bf16[1,3,2,256,128]{4,3,2,1,0:T(8,128)(2,1)} %vel.3) | copy-start | bytes 1179652
  1.9 8.8 %copy-start.3 = (s32[2,256,128]{2,1,0:T(8,128)S(1)}, s32[2,256,128]{2,1,0:T(8,128)}, u32[]{:S(2)}) copy-start(s32[2,256,128]{2,1,0:T(8,128)} %flags.3) | copy-start | bytes 786436
  1.9 9.7 %collective-permute-start = (f32[2,256,128]{2,1,0:T(8,128)S(1)}, f32[2,256,128]{2,1,0:T(8,128)S(1)}, u32[]{:S(2)}, u32[]{:S(2)}) collective-permute-start(f32[2,256,128]{2,1,0:T(8,128)S(1)} %get-tuple-element.13.first), channel_id=1, source_target_pairs={{1,2},{3,4},{5,6},{7,8},{9,10},{11,12},{13,14},{15,16},{17,18},{19... | collective-permute-start | bytes 786440 | tf_op jit(solution)/shard_map/ppermute | solution.py:336
  2.8 15.8 %collective-permute-start.2 = (f32[4,256,128]{2,1,0:T(8,128)S(1)}, f32[4,256,128]{2,1,0:T(8,128)S(1)}, u32[]{:S(2)}, u32[]{:S(2)}) collective-permute-start(f32[4,256,128]{2,1,0:T(8,128)S(1)} %get-tuple-element.15.far), channel_id=1, source_target_pairs={{0,1},{2,3},{4,5},{6,7},{8,9},{10,11},{12,13},{14,15},{16,17},{18,... | collective-permute-start | bytes 1572872 | tf_op jit(solution)/shard_map/ppermute | solution.py:336
  9.3 13.4 %collective-permute-start.1 = (f32[2,256,128]{2,1,0:T(8,128)S(1)}, f32[2,256,128]{2,1,0:T(8,128)S(1)}, u32[]{:S(2)}, u32[]{:S(2)}) collective-permute-start(f32[2,256,128]{2,1,0:T(8,128)S(1)} %get-tuple-element.14.second), channel_id=1, source_target_pairs={{1,2},{3,4},{5,6},{7,8},{9,10},{11,12},{13,14},{15,16},{17,18},{19... | collective-permute-start | bytes 786440 | tf_op jit(solution)/shard_map/ppermute | solution.py:336
  11.7 13.3 %collective-permute-start.3 = (f32[2,256,128]{2,1,0:T(8,128)S(1)}, f32[2,256,128]{2,1,0:T(8,128)S(1)}, u32[]{:S(2)}, u32[]{:S(2)}) collective-permute-start(f32[2,256,128]{2,1,0:T(8,128)S(1)} %shard_map.79.after.first), channel_id=1, source_target_pairs={{1,2},{3,4},{5,6},{7,8},{9,10},{11,12},{13,14},{15,16},{17,18},{19... | collective-permute-start | bytes 786440 | tf_op jit(solution)/shard_map/ppermute | solution.py:336
  18.6 4.9 %copy-start.4 = (s32[8]{0:T(128)S(1)}, s32[8]{0:T(128)}, u32[]{:S(2)}) copy-start(s32[8]{0:T(128)} %weights.1) | copy-start | bytes 100
  18.6 13.2 %collective-permute-start.5 = (f32[4,256,128]{2,1,0:T(8,128)S(1)}, f32[4,256,128]{2,1,0:T(8,128)S(1)}, u32[]{:S(2)}, u32[]{:S(2)}) collective-permute-start(f32[4,256,128]{2,1,0:T(8,128)S(1)} %shard_map.80.after.far), channel_id=1, source_target_pairs={{0,1},{2,3},{4,5},{6,7},{8,9},{10,11},{12,13},{14,15},{16,17},{18,... | collective-permute-start | bytes 1572872 | tf_op jit(solution)/shard_map/ppermute | solution.py:336
  22.8 2.1 %collective-permute-start.4 = (f32[2,256,128]{2,1,0:T(8,128)S(1)}, f32[2,256,128]{2,1,0:T(8,128)S(1)}, u32[]{:S(2)}, u32[]{:S(2)}) collective-permute-start(f32[2,256,128]{2,1,0:T(8,128)S(1)} %shard_map.81.second), channel_id=1, source_target_pairs={{1,2},{3,4},{5,6},{7,8},{9,10},{11,12},{13,14},{15,16},{17,18},{19... | collective-permute-start | bytes 786440 | tf_op jit(solution)/shard_map/ppermute | solution.py:336
  32.3 6.7 %collective-permute-start.6 = (f32[256,128]{1,0:T(8,128)S(1)}, f32[256,128]{1,0:T(8,128)S(1)}, u32[]{:S(2)}, u32[]{:S(2)}) collective-permute-start(f32[256,128]{1,0:T(8,128)S(1)} %get-tuple-element.23), channel_id=1, source_target_pairs={{0,64},{64,0},{1,65},{65,1},{2,66},{66,2},{3,67},{67,3},{4,68},{68... | collective-permute-start | bytes 393224 | tf_op jit(solution)/shard_map/ppermute | solution.py:372
  107.8 7.2 %collective-permute-start.7 = (f32[512,128]{1,0:T(8,128)S(1)}, f32[512,128]{1,0:T(8,128)S(1)}, u32[]{:S(2)}, u32[]{:S(2)}) collective-permute-start(f32[512,128]{1,0:T(8,128)S(1)} %bitcast.7), channel_id=1, source_target_pairs={{0,64},{64,0},{1,65},{65,1},{2,66},{66,2},{3,67},{67,3},{4,68},{68... | collective-permute-start | bytes 786440 | tf_op jit(solution)/shard_map/ppermute | solution.py:388
